TPU v7x, 32 devices: a whole 2x2x4 slice. The times are simulated.
32 devices in a mesh: dp: 8 (over z, x), tensor: 4 (over y, core).
Axes of the slice: x: 2, y: 2, z: 4, core: 2. Of those that a mesh axis runs over, the one named last changes fastest.
Arguments:
- tokens_in: bfloat16 [16384, 1024], P(('dp', 'tensor')), may hold values from -6 to 6
- doc_ids: int32 [16384], P('dp'), may hold values from 0 to 15, as said below
- gain_mixer: bfloat16 [1024], replicated, may hold values from 0.25 to 1.75
- in_weight: bfloat16 [1024, 3, 1024], P('dp', None, 'tensor'), may hold values from -0.1875 to 0.1875
- conv_weight: bfloat16 [3, 1024], P(None, 'tensor'), may hold values from -3.5 to 3.5
- out_weight: bfloat16 [1024, 1024], P('tensor', 'dp'), may hold values from -0.1875 to 0.1875
- gain_ffn: bfloat16 [1024], replicated, may hold values from 0.25 to 1.75
- gate_up_weight: bfloat16 [1024, 2, 4608], P('dp', None, 'tensor'), may hold values from -0.1875 to 0.1875
- down_weight: bfloat16 [4608, 1024], P('tensor', 'dp'), may hold values from -0.09375 to 0.09375
- cotangent: bfloat16 [16384, 1024], P(('dp', 'tensor')), may hold values from -6 to 6
Outputs:
- block_out: bfloat16 [16384, 1024], P(('dp', 'tensor'))
- grad_input: float32 [16384, 1024], P(('dp', 'tensor'))
- grad_gain_mixer: float32 [1024], replicated
- grad_in_weight: float32 [1024, 3, 1024], P('dp', None, 'tensor')
- grad_conv_weight: float32 [3, 1024], P(None, 'tensor')
- grad_out_weight: float32 [1024, 1024], P('tensor', 'dp')
- grad_gain_ffn: float32 [1024], replicated
- grad_gate_up: float32 [1024, 2, 4608], P('dp', None, 'tensor')
- grad_down: float32 [4608, 1024], P('tensor', 'dp')
Inputs may be any that keep to these rules, and one draw needn't show every extreme that they name: `doc_ids`: document numbers start at 0 at the first token and never fall; each aligned stretch of 1024 tokens after the first holds exactly one document start, never at its first two tokens, and the first stretch holds none.
All inputs are finite; a program needn't handle non-finite values.
Results may differ from a plain program's by a relative error of at most 0.0099.
Values may be sent and summed in bfloat16 or wider, within the bound.
No kernel may reach another device: no remote copies, remote signals or barrier semaphores. Data moves between devices by JAX's collectives and lax.ppermute only.
A program may use at most 192 MiB of HBM per device.

v0:
```python
import jax
import jax.numpy as jnp
from jax import lax
from jax.experimental import pallas as pl
from jax.experimental.pallas import tpu as pltpu
from jax.sharding import PartitionSpec as P

epsilon = 1e-05
HALO = 16
LONG = 8
BF = jnp.bfloat16
F32 = jnp.float32


def swap(value, axis, bit):
    peers = lax.axis_size(axis)
    return lax.ppermute(value, axis, [(i, i ^ bit) for i in range(peers)])


def ring(value, axis, by):
    peers = lax.axis_size(axis)
    return lax.ppermute(value, axis, [(i, (i + by) % peers) for i in range(peers)])


def shift(value, by):
    peers = lax.axis_size("dp") * lax.axis_size("tensor")
    pairs = [(i, i + by) for i in range(peers) if 0 <= i + by < peers]
    return lax.ppermute(value, ("dp", "tensor"), pairs)


def nn(left, right):
    return jnp.dot(left, right, preferred_element_type=F32)


def tn(left, right):
    return lax.dot_general(left, right, (((0,), (0,)), ((), ())), preferred_element_type=F32)


def nt(left, right):
    return lax.dot_general(left, right, (((1,), (1,)), ((), ())), preferred_element_type=F32)


def normalize(values):
    scale_vec = lax.rsqrt(jnp.mean(values * values, axis=-1, keepdims=True) + epsilon)
    return (values * scale_vec, scale_vec)


def norm_back(d_normed, normed, scale_vec):
    return scale_vec * (d_normed - normed * jnp.mean(d_normed * normed, axis=-1, keepdims=True))


def after(value, *others):
    return lax.optimization_barrier((value,) + others)[0]


def reorder(values, perm):
    return nn(values, perm).astype(BF)


def reorder_f32(values, perm):
    high = lax.optimization_barrier(values.astype(BF))
    low = (values - high.astype(F32)).astype(BF)
    return nn(high, perm) + nn(low, perm)


def blocks_order():
    steps, me = lax.axis_size("dp") // 2, lax.axis_index("dp")
    index = jnp.arange(2 * steps, dtype=jnp.int32)
    order = ((me // 2 - index % steps) % steps) * 2 + ((me % 2) ^ (index // steps))
    inverse = ((index % 2) ^ (me % 2)) * steps + (me // 2 - index // 2) % steps
    return order, inverse


def long_gather(shard):
    whole = lax.all_gather(shard, "dp", axis=0)[blocks_order()[0]]
    return whole.reshape(-1, shard.shape[1])


def long_scatter(near, far):
    total = jnp.concatenate([near, far], axis=0)
    peers = lax.axis_size("dp")
    total = total.reshape(peers, total.shape[0] // peers, -1)[blocks_order()[1]].reshape(total.shape)
    return lax.psum_scatter(total, "dp", scatter_dimension=0, tiled=True).astype(F32)


def chain(shard):
    here = [shard]
    for _ in range(lax.axis_size("dp") // 2 - 1):
        here.append(ring(here[-1], "dp", 2))
    return here


def others(here):
    return [swap(piece, "dp", 1) for piece in here]


def ffn(hidden, cot, weights, order, before, kept, part, tile):
    rows, width = hidden.shape
    size = weights[0].shape[1] // 3
    count = order.shape[0]
    block = width // count
    skip = part * (rows // tile)

    def kernel(order_ref, h_ref, g_ref, *refs):
        w_any, refs = refs[: len(weights)], refs[len(weights) :]
        w_ref, sems = refs[-2:]
        d_ref, o_ref, d_gu_ref, act_ref = refs[-6:-2]

        @pl.when(pl.program_id(0) == 0)
        def _():
            if len(weights) > 1:
                pieces = w_any
            else:
                starts = [pl.multiple_of(order_ref[i] * block, block) for i in range(count)]
                pieces = [w_any[0].at[pl.ds(start, block)] for start in starts]
            copies = [
                pltpu.make_async_copy(piece, w_ref.at[pl.ds(i * block, block)], sems.at[i])
                for i, piece in enumerate(pieces)
            ]
            for copy in copies:
                copy.start()
            for copy in copies:
                copy.wait()

        gate_up = nn(h_ref[...], w_ref[:, : 2 * size])
        d_act = nn(g_ref[...], w_ref[:, 2 * size :])
        gate, up = gate_up[:, :size], gate_up[:, size:]
        sigma = 1.0 / (1.0 + jnp.exp(-gate))
        silu = gate * sigma
        act = (silu * up).astype(BF)
        act_ref[...] = act
        d_gu_ref[:, :size] = (d_act * up * (sigma * (1.0 + gate * (1.0 - sigma)))).astype(BF)
        d_gu_ref[:, size:] = (d_act * silu).astype(BF)
        d_sum = nt(d_gu_ref[...], w_ref[:, : 2 * size])
        o_sum = nt(act, w_ref[:, 2 * size :])
        if before:
            d_sum = d_sum + refs[0][...]
            o_sum = o_sum + refs[1][...]
        d_ref[...] = d_sum.astype(d_ref.dtype)
        o_ref[...] = o_sum.astype(o_ref.dtype)

    tokens = pl.BlockSpec((tile, width), lambda i, _: (i, 0))
    whole = pl.BlockSpec(memory_space=pl.ANY)
    kind = BF if before else F32
    aliased = 3 + len(weights) + len(before)
    return pl.pallas_call(
        kernel,
        grid_spec=pltpu.PrefetchScalarGridSpec(
            num_scalar_prefetch=1,
            grid=(rows // tile,),
            in_specs=[tokens] * 2 + [whole] * len(weights) + [tokens] * len(before) + [whole] * len(kept),
            out_specs=[
                tokens,
                tokens,
                pl.BlockSpec((tile, 2 * size), lambda i, _: (i + skip, 0)),
                pl.BlockSpec((tile, size), lambda i, _: (i + skip, 0)),
            ],
            scratch_shapes=[
                pltpu.VMEM((width, 3 * size), BF),
                pltpu.SemaphoreType.DMA((count,)),
            ],
        ),
        out_shape=[
            jax.ShapeDtypeStruct((rows, width), kind),
            jax.ShapeDtypeStruct((rows, width), kind),
            jax.ShapeDtypeStruct((2 * rows, 2 * size), BF),
            jax.ShapeDtypeStruct((2 * rows, size), BF),
        ],
        input_output_aliases={aliased: 2, aliased + 1: 3} if kept else {},
        compiler_params=pltpu.CompilerParams(vmem_limit_bytes=48 << 20),
        cost_estimate=pl.CostEstimate(
            flops=12 * rows * width * size,
            bytes_accessed=rows * width * 12 + width * size * 6,
            transcendentals=rows * size,
        ),
    )(order, hidden, cot, *weights, *before, *kept)


def by_xor(groups, me):
    one = [jnp.where((me & 1) == 1, groups[i ^ 1], groups[i]) for i in range(4)]
    return [jnp.where((me & 2) == 2, one[i ^ 2], one[i]) for i in range(4)]


def sum_all(value):
    return jnp.sum(lax.all_gather(value, ("dp", "tensor"), axis=0), axis=0)


def body(
    tokens_in,
    doc_ids,
    gain_mixer,
    in_weight,
    conv_weight,
    out_weight,
    gain_ffn,
    gate_up_weight,
    down_weight,
    cotangent,
):
    rows, width = tokens_in.shape
    dp_count = lax.axis_size("dp")
    block = width // dp_count
    channels = in_weight.shape[2]
    units = gate_up_weight.shape[2]
    me_t = lax.axis_index("tensor")
    deep = dp_count // 2
    half = width // 2
    long = deep > LONG

    tail = tokens_in[rows - HALO :]
    linked = (doc_ids[(me_t + 1) * rows - 2] == doc_ids[(me_t + 1) * rows - 1]).astype(BF)
    tail = tail * jnp.ones((HALO, 1), BF).at[HALO - 2, 0].set(linked)
    halo = shift(tail, 1)

    packed = jnp.concatenate(
        [in_weight[:, 0], in_weight[:, 2], in_weight[:, 1], out_weight.T], axis=1
    )
    taps_rows = jnp.zeros((HALO, 4 * channels), BF).at[:3, :channels].set(conv_weight)
    cut = units // 2 // 128 * 128
    bounds = [(0, cut), (cut, units)]

    shards = [
        jnp.concatenate(
            [gate_up_weight[:, 0, lo:hi], gate_up_weight[:, 1, lo:hi], down_weight[lo:hi].T], axis=1
        )
        for lo, hi in bounds
    ]
    block_two = [lax.all_gather(shards[1], "dp", axis=0, tiled=True)]

    if long:
        whole = jnp.concatenate([long_gather(packed), taps_rows], axis=0)
        whole_y = swap(whole, "tensor", 2)
        here = [packed] * 3
        block_one = [lax.all_gather(shards[0], "dp", axis=0, tiled=True)]
        here_one = across_one = block_one * 3
    else:
        here = chain(packed)
        across = others(here)
        pairs = [jnp.concatenate(pair, axis=0) for pair in zip(here, across)]
        pairs[-1] = jnp.concatenate([here[-1], across[-1], taps_rows], axis=0)
        pairs_y = [swap(pair, "tensor", 2) for pair in pairs]
        whole = jnp.concatenate(here + across + [taps_rows], axis=0)
        whole_y = jnp.concatenate(
            [pair[:block] for pair in pairs_y]
            + [pair[block : 2 * block] for pair in pairs_y]
            + [pairs_y[-1][2 * block :]],
            axis=0,
        )
        here_one = chain(after(shards[0], here[-1]))
        across_one = others(here_one)
        block_one = here_one + across_one
    mix = [whole, swap(whole, "tensor", 1), whole_y, swap(whole_y, "tensor", 1)]

    lane = jnp.arange(width, dtype=jnp.int32)
    order = blocks_order()[0]
    source = jnp.repeat(order, block) * block + lane % block
    perm = (lane[:, None] == source[None, :]).astype(BF)
    perm_back = (source[:, None] == lane[None, :]).astype(BF)
    doc_ids = after(doc_ids, here[2])
    last = doc_ids.shape[0]
    ids = jnp.concatenate([doc_ids[:1], doc_ids[:1], doc_ids, doc_ids[last - 1 :], doc_ids[last - 1 :]])
    ids = lax.dynamic_slice(ids, (me_t * rows,), (rows + 4,))
    one_all = (ids[1:] == ids[:-1]).astype(F32)[:, None]
    two_all = (ids[2:] == ids[:-2]).astype(F32)[:, None]
    keep_one, keep_two = one_all[1 : rows + 1], two_all[:rows]
    next_one, next_two = one_all[2 : rows + 2], two_all[2 : rows + 2]
    cot = reorder(after(cotangent, here[1]), perm)
    gains = reorder(jnp.stack([gain_mixer, gain_ffn]), perm).astype(F32)
    gain_one, gain_two = gains[:1], gains[1:]
    cot_y = swap(after(cot, whole_y), "tensor", 2)
    extended = after(jnp.concatenate([halo, tokens_in], axis=0), here[1])
    extended = reorder(extended, perm)

    normed_ext, scale_ext = normalize(extended.astype(F32))
    hidden_ext = (normed_ext * gain_one).astype(BF)
    normed_one, scale_one = normed_ext[HALO:], scale_ext[HALO:]
    hidden_one = hidden_ext[HALO:]
    tokens_f = extended[HALO:].astype(F32)

    saved = []
    mixed = tokens_f
    earlier = [(), (), (here_one[1],), (here_one[2], across_one[0])]
    for group, arrived in zip(mix, earlier):
        taps = group[width : width + 3, :channels].astype(F32)
        projected = nn(after(hidden_ext, *arrived), group[:width, : 3 * channels])
        b_part = projected[:, :channels]
        v_part = projected[:, channels : 2 * channels]
        c_part = projected[HALO:, 2 * channels :]
        bx = b_part * v_part
        bx0, bx1, bx2 = bx[HALO:], keep_one * bx[HALO - 1 : -1], keep_two * bx[HALO - 2 : -2]
        conv_out = taps[0] * bx0 + taps[1] * bx1 + taps[2] * bx2
        gated = (c_part * conv_out).astype(BF)
        mixed = mixed + nt(gated, group[:width, 3 * channels :])
        saved.append((b_part[HALO:], c_part, v_part[HALO:], bx0, bx1, bx2, conv_out, gated, taps))
    resid = mixed
    normed_two, scale_two = normalize(resid)
    hidden_two = (normed_two * gain_two).astype(BF)
    hid_y = swap(hidden_two, "tensor", 2)
    tile = min(rows, 256)

    def weight_grads(d_gu, act, earlier):
        parts = []
        for part, first in zip((slice(half, width), slice(0, half)), earlier):
            tokens, grads = lax.optimization_barrier((hid_all, cot_all) + first)[:2]
            grads = [tn(tokens[:, part], d_gu).astype(BF), tn(grads[:, part], act).astype(BF)]
            parts.append(jnp.concatenate(grads, axis=1))
        return parts

    def over_x(parts):
        if long:
            return parts
        total = parts[1].astype(F32) + swap(parts[0], "dp", 1).astype(F32)
        return total.reshape(deep, block, -1)

    hid = [jnp.concatenate([hidden_two, swap(hidden_two, "tensor", 1)], axis=0)]
    cots = [jnp.concatenate([cot, swap(cot, "tensor", 1)], axis=0)]
    near = ffn(after(hid[0], *block_two), cots[0], block_one, order, (), (), 0, tile)
    hid_y, cot_y = lax.optimization_barrier((hid_y, cot_y, near[0]))[:2]
    hid.append(jnp.concatenate([hid_y, swap(hid_y, "tensor", 1)], axis=0))
    cots.append(jnp.concatenate([cot_y, swap(cot_y, "tensor", 1)], axis=0))
    hid_all, cot_all = jnp.concatenate(hid, axis=0), jnp.concatenate(cots, axis=0)
    far = ffn(hid[1], cots[1], block_one, order, (), tuple(near[2:]), 1, tile)
    parts_one = weight_grads(*far[2:], ((), ()))
    sums_one = over_x(parts_one)
    far_two = ffn(after(hid[1], *parts_one), cots[1], block_two, order, tuple(far[:2]), (), 1, tile)
    d_far = far_two[0][:rows].astype(F32) + swap(far_two[0][rows:], "tensor", 1).astype(F32)
    d_far = d_far.astype(BF)
    d_y = [swap(part, "tensor", 2) for part in (d_far[: rows // 2], d_far[rows // 2 :])]
    near_two = ffn(
        after(hid[0], d_far), cots[0], block_two, order, tuple(near[:2]), tuple(far_two[2:]), 0, tile
    )
    parts_two = weight_grads(*near_two[2:], ((d_y[0],), ()))
    sums_two = over_x(parts_two)

    d_hidden_two = near_two[0][:rows].astype(F32) + swap(near_two[0][rows:], "tensor", 1).astype(F32)
    d_hidden_two = d_hidden_two + jnp.concatenate(d_y, axis=0).astype(F32)
    d_hidden_two = after(d_hidden_two, parts_two[1])
    out_far = far_two[1][:rows].astype(F32) + swap(far_two[1][rows:], "tensor", 1).astype(F32)
    out_y = swap(after(out_far.astype(BF), *d_y), "tensor", 2)
    out_own = near_two[1][:rows].astype(F32) + swap(near_two[1][rows:], "tensor", 1).astype(F32)
    out_own = out_own + out_y.astype(F32)
    block_out = reorder((resid + out_own).astype(BF), perm_back)

    d_resid = cot.astype(F32) + norm_back(d_hidden_two * gain_two, normed_two, scale_two)
    d_mix = d_resid.astype(BF)

    d_gated = [nn(d_mix, group[:width, 3 * channels :]) for group in mix]
    d_conv = [back * keep[1] for back, keep in zip(d_gated, saved)]
    first = jnp.stack(by_xor([value[:2] for value in d_conv], me_t))
    following = shift(first, -1)
    following = by_xor([following[i] for i in range(4)], me_t)

    def over_z(sums):
        sums = sums.reshape(deep, block, -1)
        low = sums.astype(BF)
        total = sums[0]
        for k in range(1, deep):
            total = total + ring(low[k], "dp", -2 * k).astype(F32)
        return total

    d_cs = [(d_gated[r] * saved[r][6]).astype(BF) for r in range(4)]
    right = [
        jnp.concatenate(
            [tn(hidden_one, d_cs[r]).astype(BF), tn(d_mix, saved[r][7]).astype(BF)], axis=1
        )
        for r in range(4)
    ]
    right_near = right[0].astype(F32) + swap(right[1], "tensor", 1).astype(F32)
    right_far = right[2].astype(F32) + swap(right[3], "tensor", 1).astype(F32)

    d_bvs = []
    for r in range(4):
        b_part, c_part, v_part, bx0, bx1, bx2, conv_out, gated, taps = saved[r]
        ahead = jnp.concatenate([d_conv[r], following[r]], axis=0)
        d_bx = (
            taps[0] * d_conv[r]
            + taps[1] * next_one * ahead[1 : rows + 1]
            + taps[2] * next_two * ahead[2:]
        )
        d_bvs.append(jnp.concatenate([d_bx * v_part, d_bx * b_part], axis=1).astype(BF))
    hidden_late = after(hidden_one, right[1], right[3], sums_one[0], out_y)
    left = [tn(hidden_late, d_bvs[r]).astype(BF) for r in range(4)]
    left_near = left[0].astype(F32) + swap(left[1], "tensor", 1).astype(F32)
    left_far = left[2].astype(F32) + swap(left[3], "tensor", 1).astype(F32)

    left_y = swap(left_far.astype(BF), "tensor", 2)
    left_sum = left_near + left_y.astype(F32)
    if long:
        right_sum = right_near + swap(right_far.astype(BF), "tensor", 2).astype(F32)
        total = jnp.concatenate([left_sum, right_sum], axis=1).astype(BF)
        mix_sum = long_scatter(total[:half], total[half:])
        ffn_grads = [long_scatter(parts[1], parts[0]) for parts in (sums_one, sums_two)]
        d_late = d_cs
    else:
        right_x = swap(jnp.concatenate([right_near[half:], right_far[half:]], axis=0).astype(BF), "dp", 1)
        right_near = right_near[:half] + right_x[:half].astype(F32)
        right_far = right_far[:half] + right_x[half:].astype(F32)
        right_sum = right_near + swap(right_far.astype(BF), "tensor", 2).astype(F32)
        left_sum = left_sum[:half] + swap(left_sum[half:].astype(BF), "dp", 1).astype(F32)

        mix_sum = jnp.concatenate([over_z(left_sum), over_z(right_sum)], axis=1)
        ffn_grads = [over_z(sums_one), over_z(sums_two)]
        d_late = lax.optimization_barrier((d_cs, left[0], left[2], left[1], left[3]))[0]

    d_hidden_one = 0.0
    for r, group in enumerate(mix):
        d_proj = jnp.concatenate([d_bvs[r], d_late[r]], axis=1)
        d_hidden_one = d_hidden_one + nt(d_proj, group[:width, : 3 * channels])
    part_gain_one = jnp.sum(d_hidden_one * normed_one, axis=0)
    part_gain_two = jnp.sum(d_hidden_two * normed_two, axis=0)
    grad_input = d_resid + norm_back(d_hidden_one * gain_one, normed_one, scale_one)
    grad_input = reorder_f32(grad_input, perm_back)

    conv_parts = [
        jnp.stack([jnp.sum(value * d_conv[r], axis=0) for value in saved[r][3:6]]) for r in range(4)
    ]
    conv_all = jnp.stack(by_xor(conv_parts, me_t), axis=1)
    gain_parts = reorder_f32(jnp.stack([part_gain_one, part_gain_two]), perm_back)
    small = sum_all(jnp.concatenate([gain_parts, conv_all.reshape(-1, width)], axis=0))
    grad_conv = lax.dynamic_slice(small, (2, me_t * channels), (small.shape[0] - 2, channels))

    grad_in = jnp.stack([mix_sum[:, i * channels : (i + 1) * channels] for i in (0, 2, 1)], axis=1)
    grad_out = mix_sum[:, 3 * channels :].T
    grad_gu, grad_down = [], []
    for part, (lo, hi) in zip(ffn_grads, bounds):
        size = hi - lo
        grad_gu.append(part[:, : 2 * size].reshape(block, 2, size))
        grad_down.append(part[:, 2 * size :].T)
    return (
        block_out,
        grad_input,
        small[0],
        grad_in,
        grad_conv,
        grad_out,
        small[1],
        jnp.concatenate(grad_gu, axis=2),
        jnp.concatenate(grad_down, axis=0),
    )


def solution(mesh):
    return jax.shard_map(
        body,
        mesh=mesh,
        in_specs=(
            P(("dp", "tensor"), None),
            P("dp"),
            P(),
            P("dp", None, "tensor"),
            P(None, "tensor"),
            P("tensor", "dp"),
            P(),
            P("dp", None, "tensor"),
            P("tensor", "dp"),
            P(("dp", "tensor"), None),
        ),
        out_specs=(
            P(("dp", "tensor"), None),
            P(("dp", "tensor"), None),
            P(),
            P("dp", None, "tensor"),
            P(None, "tensor"),
            P("tensor", "dp"),
            P(),
            P("dp", None, "tensor"),
            P("tensor", "dp"),
        ),
        check_vma=False,
    )
```

profile of v0, /device:TPU:0, one launch (start us, length us, event | category | flops | bytes accessed | tf_op | source)
XLA Modules:
  0.0 521.9 jit_solution(10926272952724985908)
XLA Ops:
  10.3 3.0 collective-permute-start.1
  33.8 2.3 fusion.33
  36.2 2.5 collective-permute-start.5
  39.5 8.8 %collective-permute-done.2 = bf16[128,1024]{1,0:T(8,128)(2,1)S(1)} collective-permute-done((bf16[128,1024]{1,0:T(8,128)(2,1)S(1)}, bf16[128,1024]{1,0:T(8,128)(2,1)S(1)}, u32[]{:S(2)}, u32[]{:S(2)}) %collective-permute-start.2) | collective-permute-done | bytes 262176 | tf_op jit(solution)/shard_map/ppermute | solution.py:22
  49.0 2.6 concatenate.237
  52.2 2.4 collective-permute-start.3
  57.9 6.2 %collective-permute-done.6 = bf16[128,1024]{1,0:T(8,128)(2,1)S(1)} collective-permute-done((bf16[128,1024]{1,0:T(8,128)(2,1)}, bf16[128,1024]{1,0:T(8,128)(2,1)S(1)}, u32[]{:S(2)}, u32[]{:S(2)}) %collective-permute-start.6) | collective-permute-done | bytes 262176 | tf_op jit(solution)/shard_map/ppermute | solution.py:17
  66.7 2.4 collective-permute-start.7
  72.5 5.5 %collective-permute-start.9 = (bf16[128,1536]{1,0:T(8,128)(2,1)S(1)}, bf16[128,1536]{1,0:T(8,128)(2,1)S(1)}, u32[]{:S(2)}, u32[]{:S(2)}) collective-permute-start(bf16[128,1536]{1,0:T(8,128)(2,1)S(1)} %pad_maximum_fusion.23.refs_0_), channel_id=1, source_target_pairs={{0,8},{4,12},{8,16},{12,20},{16,24},{20,28},{24,0},{28,4},{1,9},{5... | collective-permute-start | bytes 1179656 | tf_op jit(solution)/shard_map/ppermute | solution.py:22
  83.0 2.4 fusion.54
  87.2 6.1 %collective-permute-done.9.refs_1_ = bf16[128,1536]{1,0:T(8,128)(2,1)S(1)} collective-permute-done((bf16[128,1536]{1,0:T(8,128)(2,1)S(1)}, bf16[128,1536]{1,0:T(8,128)(2,1)S(1)}, u32[]{:S(2)}, u32[]{:S(2)}) %collective-permute-start.9) | collective-permute-done | bytes 393248 | tf_op jit(solution)/shard_map/ppermute | solution.py:22
  94.2 4.5 collective-permute-done.15.refs_4_
  98.8 15.0 %collective-permute-done.14.refs_2_ = bf16[128,1536]{1,0:T(8,128)(2,1)S(1)} collective-permute-done((bf16[128,1536]{1,0:T(8,128)(2,1)S(1)}, bf16[128,1536]{1,0:T(8,128)(2,1)S(1)}, u32[]{:S(2)}, u32[]{:S(2)}) %collective-permute-start.14) | collective-permute-done | bytes 393248 | tf_op jit(solution)/shard_map/ppermute | solution.py:22
  132.5 8.8 %collective-permute-done.21.refs_3_ = bf16[128,1536]{1,0:T(8,128)(2,1)S(1)} collective-permute-done((bf16[128,1536]{1,0:T(8,128)(2,1)S(1)}, bf16[128,1536]{1,0:T(8,128)(2,1)S(1)}, u32[]{:S(2)}, u32[]{:S(2)}) %collective-permute-start.21) | collective-permute-done | bytes 393248 | tf_op jit(solution)/shard_map/ppermute | solution.py:22
  143.4 3.1 pad_maximum_fusion.3.g_ref
  146.4 2.8 pad_maximum_fusion.2.h_ref
  149.2 4.1 collective-permute-done.23.refs_6_
  153.3 7.0 %collective-permute-done.24.refs_7_ = bf16[128,1536]{1,0:T(8,128)(2,1)} collective-permute-done((bf16[128,1536]{1,0:T(8,128)(2,1)S(1)}, bf16[128,1536]{1,0:T(8,128)(2,1)}, u32[]{:S(2)}, u32[]{:S(2)}) %collective-permute-start.24) | collective-permute-done | bytes 393248 | tf_op jit(solution)/shard_map/ppermute | solution.py:17
  160.3 13.2 %shard_map.169 = (f32[1024,1024]{1,0:T(8,128)}, f32[1024,1024]{1,0:T(8,128)}, bf16[2048,1024]{1,0:T(8,128)(2,1)}, bf16[2048,512]{1,0:T(8,128)(2,1)S(1)}) custom-call(s32[8]{0:T(128)S(1)} %get-tuple-element.181.order_ref, bf16[1024,1024]{1,0:T(8,128)(2,1)} %pad_maximum_fusion.2.h_ref, bf16[1024,1024]{1,0:T(8,128)(2,1)} %pad_maximum_fusion.3.g_ref, ...), custom_call_target="tpu_custom_call" | custom-call | flops 6442450944 | bytes 15728640 | tf_op jit(solution)/shard_map/pallas_call | solution.py:146
  177.3 2.3 slice.793
  182.9 2.6 pad_maximum_fusion.1
  193.5 13.2 %shard_map.170 = (f32[1024,1024]{1,0:T(8,128)}, f32[1024,1024]{1,0:T(8,128)}, bf16[2048,1024]{1,0:T(8,128)(2,1)}, bf16[2048,512]{1,0:T(8,128)(2,1)S(1)}) custom-call(s32[8]{0:T(128)S(1)} %get-tuple-element.181.order_ref, bf16[1024,1024]{1,0:T(8,128)(2,1)} %copy-done.65, ...), custom_call_target="tpu_custom_call", output_to_operand_aliasing={{2}: (11, {}), {3}: (12, {})} | custom-call | flops 6442450944 | bytes 15728640 | tf_op jit(solution)/shard_map/pallas_call | solution.py:146
  206.7 4.5 fusion.38
  213.9 15.0 %shard_map.171 = (bf16[1024,1024]{1,0:T(8,128)(2,1)S(1)}, bf16[1024,1024]{1,0:T(8,128)(2,1)S(1)}, bf16[2048,1280]{1,0:T(8,128)(2,1)}, bf16[2048,640]{1,0:T(8,128)(2,1)}) custom-call(s32[8]{0:T(128)S(1)} %get-tuple-element.181.order_ref, bf16[1024,1024]{1,0:T(8,128)(2,1)} %copy-done.65, bf16[1024,1024]{1,0:T(8,128)(2,1)} %copy-done.66, ...), custom_call_target="tpu_custom_call" | custom-call | flops 8053063680 | bytes 16515072 | tf_op jit(solution)/shard_map/pallas_call | solution.py:146
  232.9 3.3 fusion.35
  239.0 14.5 %shard_map.172 = (bf16[1024,1024]{1,0:T(8,128)(2,1)S(1)}, bf16[1024,1024]{1,0:T(8,128)(2,1)S(1)}, bf16[2048,1280]{1,0:T(8,128)(2,1)}, bf16[2048,640]{1,0:T(8,128)(2,1)}) custom-call(s32[8]{0:T(128)S(1)} %get-tuple-element.181.order_ref, bf16[1024,1024]{1,0:T(8,128)(2,1)} %pad_maximum_fusion.2.h_ref, ...), custom_call_target="tpu_custom_call", output_to_operand_aliasing={{2}: (6, {}), {3}: (7, {})} | custom-call | flops 8053063680 | bytes 16515072 | tf_op jit(solution)/shard_map/pallas_call | solution.py:146
  258.6 2.7 fusion.56
  261.2 6.6 %convolution_convert_fusion.1 = bf16[512,1280]{1,0:T(8,128)(2,1)} fusion(bf16[2048,1280]{1,0:T(8,128)(2,1)} %get-tuple-element.101, bf16[2048,1024]{1,0:T(8,128)(2,1)S(1)} %copy-done.36), kind=kOutput, calls=%fused_computation.15 | convolution fusion | flops 2685009920 | bytes 8650752 | tf_op jit(solution)/shard_map/dot_general | solution.py:36
  270.0 2.8 collective-permute-start.50
  275.1 3.0 convolution_convert_fusion
  283.5 25.0 %collective-permute-done.51 = bf16[128,1536]{1,0:T(8,128)(2,1)S(1)} collective-permute-done((bf16[128,1536]{1,0:T(8,128)(2,1)S(1)}, bf16[128,1536]{1,0:T(8,128)(2,1)S(1)}, u32[]{:S(2)}, u32[]{:S(2)}) %collective-permute-start.51) | collective-permute-done | bytes 393248 | tf_op jit(solution)/shard_map/ppermute | solution.py:22
  337.1 2.4 collective-permute-start.44
  352.5 2.8 multiply_reduce_fusion.1
  357.1 3.0 fusion.190
  360.1 41.0 %all-gather.1 = f32[32,5,1024]{2,1,0:T(8,128)S(1)} all-gather(f32[1,5,1024]{2,1,0:T(8,128)S(1)} %maximum_bitcast_fusion), channel_id=2, replica_groups=mesh['dp'=8,'tensor'=4] {'dp','tensor'}, dimensions={0}, use_global_device_ids=true | all-gather | bytes 675840 | tf_op jit(solution)/shard_map/all_gather | solution.py:185
  401.3 2.8 fusion.2
  405.4 2.8 fusion.32
  408.5 4.3 fusion.34
  422.5 2.6 add_convert_fusion
  425.2 5.1 collective-permute-done.54
  431.8 25.1 %collective-permute-done.55 = bf16[128,1920]{1,0:T(8,128)(2,1)S(1)} collective-permute-done((bf16[128,1920]{1,0:T(8,128)(2,1)S(1)}, bf16[128,1920]{1,0:T(8,128)(2,1)S(1)}, u32[]{:S(2)}, u32[]{:S(2)}) %collective-permute-start.55) | collective-permute-done | bytes 491552 | tf_op jit(solution)/shard_map/ppermute | solution.py:22
  460.2 2.9 pad_maximum_fusion.8
  467.8 9.9 %collective-permute-done.46 = bf16[512,512]{0,1:T(8,128)(2,1)S(1)} collective-permute-done((bf16[512,512]{0,1:T(8,128)(2,1)S(1)}, bf16[512,512]{0,1:T(8,128)(2,1)S(1)}, u32[]{:S(2)}, u32[]{:S(2)}) %collective-permute-start.46) | collective-permute-done | bytes 524320 | tf_op jit(solution)/shard_map/ppermute | solution.py:17
  477.7 2.3 fusion.187
  480.8 6.8 %collective-permute-start.48 = (bf16[128,512]{0,1:T(8,128)(2,1)}, bf16[128,512]{0,1:T(8,128)(2,1)S(1)}, u32[]{:S(2)}, u32[]{:S(2)}) collective-permute-start(bf16[128,512]{0,1:T(8,128)(2,1)} %get-tuple-element.206), channel_id=1, source_target_pairs={{0,16},{4,20},{8,24},{12,28},{16,0},{20,4},{24,8},{28,12},{1,17},{... | collective-permute-start | bytes 393224 | tf_op jit(solution)/shard_map/ppermute | solution.py:22
  490.8 8.5 %collective-permute-done.48 = bf16[128,512]{0,1:T(8,128)(2,1)S(1)} collective-permute-done((bf16[128,512]{0,1:T(8,128)(2,1)}, bf16[128,512]{0,1:T(8,128)(2,1)S(1)}, u32[]{:S(2)}, u32[]{:S(2)}) %collective-permute-start.48) | collective-permute-done | bytes 131104 | tf_op jit(solution)/shard_map/ppermute | solution.py:22
  504.4 2.8 collective-permute-done.40
  507.1 6.4 %collective-permute-done.41 = bf16[128,512]{0,1:T(8,128)(2,1)S(1)} collective-permute-done((bf16[128,512]{0,1:T(8,128)(2,1)S(1)}, bf16[128,512]{0,1:T(8,128)(2,1)S(1)}, u32[]{:S(2)}, u32[]{:S(2)}) %collective-permute-start.41) | collective-permute-done | bytes 131104 | tf_op jit(solution)/shard_map/ppermute | solution.py:22
  (469 shorter events, 174.5 us)
Async XLA Ops:
  7.2 142.0 %all-gather.4.cloned.1.call-start = ((), (), s32[]{:S(2)}) async-start(), calls=%async_computation | async-start | bytes 4423680 | tf_op jit(solution)/shard_map/all_gather | solution.py:228
  10.3 15.6 %collective-permute-start.1 = (bf16[128,1024]{1,0:T(8,128)(2,1)}, bf16[128,1024]{1,0:T(8,128)(2,1)S(1)}, u32[]{:S(2)}, u32[]{:S(2)}) collective-permute-start(bf16[128,1024]{1,0:T(8,128)(2,1)} %get-tuple-element.234), channel_id=1, source_target_pairs={{0,8},{4,12},{8,16},{12,20},{16,24},{20,28},{24,0},{28,4},{1,9},{5... | collective-permute-start | bytes 786440 | tf_op jit(solution)/shard_map/ppermute | solution.py:22
  13.3 15.8 %collective-permute-start.4 = (bf16[128,1024]{1,0:T(8,128)(2,1)}, bf16[128,1024]{1,0:T(8,128)(2,1)S(1)}, u32[]{:S(2)}, u32[]{:S(2)}) collective-permute-start(bf16[128,1024]{1,0:T(8,128)(2,1)} %get-tuple-element.234), channel_id=1, source_target_pairs={{0,4},{4,0},{8,12},{12,8},{16,20},{20,16},{24,28},{28,24},{1,5},{5... | collective-permute-start | bytes 786440 | tf_op jit(solution)/shard_map/ppermute | solution.py:17
  30.1 42.4 %collective-permute-start.10 = (bf16[256,1024]{1,0:T(8,128)(2,1)}, bf16[256,1024]{1,0:T(8,128)(2,1)}, u32[]{:S(2)}, u32[]{:S(2)}) collective-permute-start(bf16[256,1024]{1,0:T(8,128)(2,1)} %pad_maximum_fusion.19), channel_id=1, source_target_pairs={{0,2},{1,3},{2,0},{3,1},{4,6},{5,7},{6,4},{7,5},{8,10},{9,11},{10,... | collective-permute-start | bytes 1572872 | tf_op jit(solution)/shard_map/ppermute | solution.py:17
  32.2 16.1 %collective-permute-start.2 = (bf16[128,1024]{1,0:T(8,128)(2,1)S(1)}, bf16[128,1024]{1,0:T(8,128)(2,1)S(1)}, u32[]{:S(2)}, u32[]{:S(2)}) collective-permute-start(bf16[128,1024]{1,0:T(8,128)(2,1)S(1)} %collective-permute-done.1), channel_id=1, source_target_pairs={{0,8},{4,12},{8,16},{12,20},{16,24},{20,28},{24,0},{28,4},{1,9},{5... | collective-permute-start | bytes 786440 | tf_op jit(solution)/shard_map/ppermute | solution.py:22
  36.1 95.1 %collective-permute-start.20 = (bf16[512,1024]{1,0:T(8,128)(2,1)}, bf16[512,1024]{1,0:T(8,128)(2,1)}, u32[]{:S(2)}, u32[]{:S(2)}) collective-permute-start(bf16[512,1024]{1,0:T(8,128)(2,1)} %fusion.33), channel_id=1, source_target_pairs={{0,1},{1,0},{2,3},{3,2},{4,5},{5,4},{6,7},{7,6},{8,9},{9,8},{10,11... | collective-permute-start | bytes 3145736 | tf_op jit(solution)/shard_map/ppermute | solution.py:17
  36.2 15.6 %collective-permute-start.5 = (bf16[128,1024]{1,0:T(8,128)(2,1)S(1)}, bf16[128,1024]{1,0:T(8,128)(2,1)S(1)}, u32[]{:S(2)}, u32[]{:S(2)}) collective-permute-start(bf16[128,1024]{1,0:T(8,128)(2,1)S(1)} %collective-permute-done.1), channel_id=1, source_target_pairs={{0,4},{4,0},{8,12},{12,8},{16,20},{20,16},{24,28},{28,24},{1,5},{5... | collective-permute-start | bytes 786440 | tf_op jit(solution)/shard_map/ppermute | solution.py:17
  51.9 33.6 %collective-permute-start.11 = (bf16[256,1024]{1,0:T(8,128)(2,1)S(1)}, bf16[256,1024]{1,0:T(8,128)(2,1)S(1)}, u32[]{:S(2)}, u32[]{:S(2)}) collective-permute-start(bf16[256,1024]{1,0:T(8,128)(2,1)S(1)} %pad_maximum_fusion.20), channel_id=1, source_target_pairs={{0,2},{1,3},{2,0},{3,1},{4,6},{5,7},{6,4},{7,5},{8,10},{9,11},{10,... | collective-permute-start | bytes 1572872 | tf_op jit(solution)/shard_map/ppermute | solution.py:17
  52.2 14.5 %collective-permute-start.3 = (bf16[128,1024]{1,0:T(8,128)(2,1)}, bf16[128,1024]{1,0:T(8,128)(2,1)S(1)}, u32[]{:S(2)}, u32[]{:S(2)}) collective-permute-start(bf16[128,1024]{1,0:T(8,128)(2,1)} %copy-done.55), channel_id=1, source_target_pairs={{0,8},{4,12},{8,16},{12,20},{16,24},{20,28},{24,0},{28,4},{1,9},{5... | collective-permute-start | bytes 786440 | tf_op jit(solution)/shard_map/ppermute | solution.py:22
  65.1 29.0 %collective-permute-start.12 = (bf16[256,1024]{1,0:T(8,128)(2,1)S(1)}, bf16[256,1024]{1,0:T(8,128)(2,1)S(1)}, u32[]{:S(2)}, u32[]{:S(2)}) collective-permute-start(bf16[256,1024]{1,0:T(8,128)(2,1)S(1)} %pad_maximum_fusion.21), channel_id=1, source_target_pairs={{0,2},{1,3},{2,0},{3,1},{4,6},{5,7},{6,4},{7,5},{8,10},{9,11},{10,... | collective-permute-start | bytes 1572872 | tf_op jit(solution)/shard_map/ppermute | solution.py:17
  66.7 14.0 %collective-permute-start.7 = (bf16[128,1024]{1,0:T(8,128)(2,1)S(1)}, bf16[128,1024]{1,0:T(8,128)(2,1)S(1)}, u32[]{:S(2)}, u32[]{:S(2)}) collective-permute-start(bf16[128,1024]{1,0:T(8,128)(2,1)S(1)} %collective-permute-done.3), channel_id=1, source_target_pairs={{0,4},{4,0},{8,12},{12,8},{16,20},{20,16},{24,28},{28,24},{1,5},{5... | collective-permute-start | bytes 786440 | tf_op jit(solution)/shard_map/ppermute | solution.py:17
  72.5 20.8 %collective-permute-start.9 = (bf16[128,1536]{1,0:T(8,128)(2,1)S(1)}, bf16[128,1536]{1,0:T(8,128)(2,1)S(1)}, u32[]{:S(2)}, u32[]{:S(2)}) collective-permute-start(bf16[128,1536]{1,0:T(8,128)(2,1)S(1)} %pad_maximum_fusion.23.refs_0_), channel_id=1, source_target_pairs={{0,8},{4,12},{8,16},{12,20},{16,24},{20,28},{24,0},{28,4},{1,9},{5... | collective-permute-start | bytes 1179656 | tf_op jit(solution)/shard_map/ppermute | solution.py:22
  82.2 31.5 %collective-permute-start.13 = (bf16[272,1024]{1,0:T(8,128)(2,1)S(1)}, bf16[272,1024]{1,0:T(8,128)(2,1)S(1)}, u32[]{:S(2)}, u32[]{:S(2)}) collective-permute-start(bf16[272,1024]{1,0:T(8,128)(2,1)S(1)} %pad_maximum_fusion.14), channel_id=1, source_target_pairs={{0,2},{1,3},{2,0},{3,1},{4,6},{5,7},{6,4},{7,5},{8,10},{9,11},{10,... | collective-permute-start | bytes 1671176 | tf_op jit(solution)/shard_map/ppermute | solution.py:17
  85.5 13.2 %collective-permute-start.15 = (bf16[128,1536]{1,0:T(8,128)(2,1)S(1)}, bf16[128,1536]{1,0:T(8,128)(2,1)S(1)}, u32[]{:S(2)}, u32[]{:S(2)}) collective-permute-start(bf16[128,1536]{1,0:T(8,128)(2,1)S(1)} %pad_maximum_fusion.23.refs_0_), channel_id=1, source_target_pairs={{0,4},{4,0},{8,12},{12,8},{16,20},{20,16},{24,28},{28,24},{1,5},{5... | collective-permute-start | bytes 1179656 | tf_op jit(solution)/shard_map/ppermute | solution.py:17
  93.4 20.4 %collective-permute-start.14 = (bf16[128,1536]{1,0:T(8,128)(2,1)S(1)}, bf16[128,1536]{1,0:T(8,128)(2,1)S(1)}, u32[]{:S(2)}, u32[]{:S(2)}) collective-permute-start(bf16[128,1536]{1,0:T(8,128)(2,1)S(1)} %collective-permute-done.9.refs_1_), channel_id=1, source_target_pairs={{0,8},{4,12},{8,16},{12,20},{16,24},{20,28},{24,0},{28,4},{1,9},{5... | collective-permute-start | bytes 1179656 | tf_op jit(solution)/shard_map/ppermute | solution.py:22
  94.1 22.0 %collective-permute-start.8 = (bf16[1040,1024]{1,0:T(8,128)(2,1)S(1)}, bf16[1040,1024]{1,0:T(8,128)(2,1)S(1)}, u32[]{:S(2)}, u32[]{:S(2)}) collective-permute-start(bf16[1040,1024]{1,0:T(8,128)(2,1)S(1)} %copy-done.80), channel_id=1, source_target_pairs={{0,1},{1,0},{2,3},{3,2},{4,5},{5,4},{6,7},{7,6},{8,9},{9,8},{10,11... | collective-permute-start | bytes 6389768 | tf_op jit(solution)/shard_map/ppermute | solution.py:17
  127.3 14.8 %collective-permute-start.17 = (bf16[512,1024]{1,0:T(8,128)(2,1)}, bf16[512,1024]{1,0:T(8,128)(2,1)S(1)}, u32[]{:S(2)}, u32[]{:S(2)}) collective-permute-start(bf16[512,1024]{1,0:T(8,128)(2,1)} %multiply_convert_fusion.1), channel_id=1, source_target_pairs={{0,1},{1,0},{2,3},{3,2},{4,5},{5,4},{6,7},{7,6},{8,9},{9,8},{10,11... | collective-permute-start | bytes 3145736 | tf_op jit(solution)/shard_map/ppermute | solution.py:17
  127.9 13.4 %collective-permute-start.21 = (bf16[128,1536]{1,0:T(8,128)(2,1)S(1)}, bf16[128,1536]{1,0:T(8,128)(2,1)S(1)}, u32[]{:S(2)}, u32[]{:S(2)}) collective-permute-start(bf16[128,1536]{1,0:T(8,128)(2,1)S(1)} %collective-permute-done.14.refs_2_), channel_id=1, source_target_pairs={{0,8},{4,12},{8,16},{12,20},{16,24},{20,28},{24,0},{28,4},{1,9},{5... | collective-permute-start | bytes 1179656 | tf_op jit(solution)/shard_map/ppermute | solution.py:22
  129.2 45.6 %collective-permute-start.19 = (bf16[512,1024]{1,0:T(8,128)(2,1)}, bf16[512,1024]{1,0:T(8,128)(2,1)}, u32[]{:S(2)}, u32[]{:S(2)}) collective-permute-start(bf16[512,1024]{1,0:T(8,128)(2,1)} %fusion.33), channel_id=1, source_target_pairs={{0,2},{1,3},{2,0},{3,1},{4,6},{5,7},{6,4},{7,5},{8,10},{9,11},{10,... | collective-permute-start | bytes 3145736 | tf_op jit(solution)/shard_map/ppermute | solution.py:17
  129.2 47.6 %collective-permute-start.18 = (bf16[512,1024]{1,0:T(8,128)(2,1)}, bf16[512,1024]{1,0:T(8,128)(2,1)}, u32[]{:S(2)}, u32[]{:S(2)}) collective-permute-start(bf16[512,1024]{1,0:T(8,128)(2,1)} %multiply_convert_fusion.1), channel_id=1, source_target_pairs={{0,2},{1,3},{2,0},{3,1},{4,6},{5,7},{6,4},{7,5},{8,10},{9,11},{10,... | collective-permute-start | bytes 3145736 | tf_op jit(solution)/shard_map/ppermute | solution.py:17
  131.2 18.0 %collective-permute-start.22 = (bf16[128,1536]{1,0:T(8,128)(2,1)S(1)}, bf16[128,1536]{1,0:T(8,128)(2,1)S(1)}, u32[]{:S(2)}, u32[]{:S(2)}) collective-permute-start(bf16[128,1536]{1,0:T(8,128)(2,1)S(1)} %collective-permute-done.9.refs_1_), channel_id=1, source_target_pairs={{0,4},{4,0},{8,12},{12,8},{16,20},{20,16},{24,28},{28,24},{1,5},{5... | collective-permute-start | bytes 1179656 | tf_op jit(solution)/shard_map/ppermute | solution.py:17
  141.3 12.1 %collective-permute-start.23 = (bf16[128,1536]{1,0:T(8,128)(2,1)S(1)}, bf16[128,1536]{1,0:T(8,128)(2,1)S(1)}, u32[]{:S(2)}, u32[]{:S(2)}) collective-permute-start(bf16[128,1536]{1,0:T(8,128)(2,1)S(1)} %collective-permute-done.14.refs_2_), channel_id=1, source_target_pairs={{0,4},{4,0},{8,12},{12,8},{16,20},{20,16},{24,28},{28,24},{1,5},{5... | collective-permute-start | bytes 1179656 | tf_op jit(solution)/shard_map/ppermute | solution.py:17
  142.1 18.1 %collective-permute-start.24 = (bf16[128,1536]{1,0:T(8,128)(2,1)S(1)}, bf16[128,1536]{1,0:T(8,128)(2,1)}, u32[]{:S(2)}, u32[]{:S(2)}) collective-permute-start(bf16[128,1536]{1,0:T(8,128)(2,1)S(1)} %collective-permute-done.21.refs_3_), channel_id=1, source_target_pairs={{0,4},{4,0},{8,12},{12,8},{16,20},{20,16},{24,28},{28,24},{1,5},{5... | collective-permute-start | bytes 1179656 | tf_op jit(solution)/shard_map/ppermute | solution.py:17
  212.6 55.3 %collective-permute-start.35 = (bf16[512,1536]{1,0:T(8,128)(2,1)S(1)}, bf16[512,1536]{1,0:T(8,128)(2,1)}, u32[]{:S(2)}, u32[]{:S(2)}) collective-permute-start(bf16[512,1536]{1,0:T(8,128)(2,1)S(1)} %pad_maximum_fusion.6), channel_id=1, source_target_pairs={{0,4},{4,0},{8,12},{12,8},{16,20},{20,16},{24,28},{28,24},{1,5},{5... | collective-permute-start | bytes 4718600 | tf_op jit(solution)/shard_map/ppermute | solution.py:17
  230.1 26.4 %collective-permute-start.29 = (bf16[512,1024]{1,0:T(8,128)(2,1)}, bf16[512,1024]{1,0:T(8,128)(2,1)S(1)}, u32[]{:S(2)}, u32[]{:S(2)}) collective-permute-start(bf16[512,1024]{1,0:T(8,128)(2,1)} %slice.651), channel_id=1, source_target_pairs={{0,1},{1,0},{2,3},{3,2},{4,5},{5,4},{6,7},{7,6},{8,9},{9,8},{10,11... | collective-permute-start | bytes 3145736 | tf_op jit(solution)/shard_map/ppermute | solution.py:17
  237.7 36.3 %collective-permute-start.30 = (bf16[256,1024]{1,0:T(8,128)(2,1)}, bf16[256,1024]{1,0:T(8,128)(2,1)}, u32[]{:S(2)}, u32[]{:S(2)}) collective-permute-start(bf16[256,1024]{1,0:T(8,128)(2,1)} %get-tuple-element.199), channel_id=1, source_target_pairs={{0,2},{1,3},{2,0},{3,1},{4,6},{5,7},{6,4},{7,5},{8,10},{9,11},{10,... | collective-permute-start | bytes 1572872 | tf_op jit(solution)/shard_map/ppermute | solution.py:17
  254.6 59.2 %collective-permute-start.33 = (bf16[512,1024]{1,0:T(8,128)(2,1)}, bf16[512,1024]{1,0:T(8,128)(2,1)}, u32[]{:S(2)}, u32[]{:S(2)}) collective-permute-start(bf16[512,1024]{1,0:T(8,128)(2,1)} %slice.655), channel_id=1, source_target_pairs={{0,1},{1,0},{2,3},{3,2},{4,5},{5,4},{6,7},{7,6},{8,9},{9,8},{10,11... | collective-permute-start | bytes 3145736 | tf_op jit(solution)/shard_map/ppermute | solution.py:17
  254.6 25.3 %collective-permute-start.31 = (bf16[256,1024]{1,0:T(8,128)(2,1)}, bf16[256,1024]{1,0:T(8,128)(2,1)S(1)}, u32[]{:S(2)}, u32[]{:S(2)}) collective-permute-start(bf16[256,1024]{1,0:T(8,128)(2,1)} %get-tuple-element.198), channel_id=1, source_target_pairs={{0,2},{1,3},{2,0},{3,1},{4,6},{5,7},{6,4},{7,5},{8,10},{9,11},{10,... | collective-permute-start | bytes 1572872 | tf_op jit(solution)/shard_map/ppermute | solution.py:17
  270.0 12.4 %collective-permute-start.50 = (bf16[128,1536]{1,0:T(8,128)(2,1)S(1)}, bf16[128,1536]{1,0:T(8,128)(2,1)S(1)}, u32[]{:S(2)}, u32[]{:S(2)}) collective-permute-start(bf16[128,1536]{1,0:T(8,128)(2,1)S(1)} %get-tuple-element.193), channel_id=1, source_target_pairs={{0,24},{4,28},{8,0},{12,4},{16,8},{20,12},{24,16},{28,20},{1,25},{... | collective-permute-start | bytes 1179656 | tf_op jit(solution)/shard_map/ppermute | solution.py:22
  272.8 35.7 %collective-permute-start.51 = (bf16[128,1536]{1,0:T(8,128)(2,1)S(1)}, bf16[128,1536]{1,0:T(8,128)(2,1)S(1)}, u32[]{:S(2)}, u32[]{:S(2)}) collective-permute-start(bf16[128,1536]{1,0:T(8,128)(2,1)S(1)} %get-tuple-element.195), channel_id=1, source_target_pairs={{0,16},{4,20},{8,24},{12,28},{16,0},{20,4},{24,8},{28,12},{1,17},{... | collective-permute-start | bytes 1179656 | tf_op jit(solution)/shard_map/ppermute | solution.py:22
  274.0 35.8 %collective-permute-start.52 = (bf16[128,1536]{1,0:T(8,128)(2,1)S(1)}, bf16[128,1536]{1,0:T(8,128)(2,1)S(1)}, u32[]{:S(2)}, u32[]{:S(2)}) collective-permute-start(bf16[128,1536]{1,0:T(8,128)(2,1)S(1)} %get-tuple-element.194), channel_id=1, source_target_pairs={{0,8},{4,12},{8,16},{12,20},{16,24},{20,28},{24,0},{28,4},{1,9},{5... | collective-permute-start | bytes 1179656 | tf_op jit(solution)/shard_map/ppermute | solution.py:22
  280.0 128.2 %collective-permute-start.28 = (bf16[512,1024]{1,0:T(8,128)(2,1)}, bf16[512,1024]{1,0:T(8,128)(2,1)}, u32[]{:S(2)}, u32[]{:S(2)}) collective-permute-start(bf16[512,1024]{1,0:T(8,128)(2,1)} %slice.649), channel_id=1, source_target_pairs={{0,1},{1,0},{2,3},{3,2},{4,5},{5,4},{6,7},{7,6},{8,9},{9,8},{10,11... | collective-permute-start | bytes 3145736 | tf_op jit(solution)/shard_map/ppermute | solution.py:17
  282.3 132.3 %collective-permute-start.53 = (bf16[512,1920]{1,0:T(8,128)(2,1)}, bf16[512,1920]{1,0:T(8,128)(2,1)}, u32[]{:S(2)}, u32[]{:S(2)}) collective-permute-start(bf16[512,1920]{1,0:T(8,128)(2,1)} %pad_maximum_fusion.5), channel_id=1, source_target_pairs={{0,4},{4,0},{8,12},{12,8},{16,20},{20,16},{24,28},{28,24},{1,5},{5... | collective-permute-start | bytes 5898248 | tf_op jit(solution)/shard_map/ppermute | solution.py:17
  308.5 32.5 %collective-permute-start.32 = (bf16[512,1024]{1,0:T(8,128)(2,1)}, bf16[512,1024]{1,0:T(8,128)(2,1)}, u32[]{:S(2)}, u32[]{:S(2)}) collective-permute-start(bf16[512,1024]{1,0:T(8,128)(2,1)} %add_convert_fusion.2), channel_id=1, source_target_pairs={{0,2},{1,3},{2,0},{3,1},{4,6},{5,7},{6,4},{7,5},{8,10},{9,11},{10,... | collective-permute-start | bytes 3145736 | tf_op jit(solution)/shard_map/ppermute | solution.py:17
  332.1 80.6 %collective-permute-start.43 = (bf16[1024,512]{0,1:T(8,128)(2,1)}, bf16[1024,512]{0,1:T(8,128)(2,1)}, u32[]{:S(2)}, u32[]{:S(2)}) collective-permute-start(bf16[1024,512]{0,1:T(8,128)(2,1)} %pad_maximum_fusion.10), channel_id=1, source_target_pairs={{0,1},{1,0},{2,3},{3,2},{4,5},{5,4},{6,7},{7,6},{8,9},{9,8},{10,11... | collective-permute-start | bytes 3145736 | tf_op jit(solution)/shard_map/ppermute | solution.py:17
  337.1 79.9 %collective-permute-start.44 = (bf16[1024,512]{0,1:T(8,128)(2,1)}, bf16[1024,512]{0,1:T(8,128)(2,1)}, u32[]{:S(2)}, u32[]{:S(2)}) collective-permute-start(bf16[1024,512]{0,1:T(8,128)(2,1)} %pad_maximum_fusion.11), channel_id=1, source_target_pairs={{0,1},{1,0},{2,3},{3,2},{4,5},{5,4},{6,7},{7,6},{8,9},{9,8},{10,11... | collective-permute-start | bytes 3145736 | tf_op jit(solution)/shard_map/ppermute | solution.py:17
  343.5 78.7 %collective-permute-start.37 = (bf16[1024,512]{0,1:T(8,128)(2,1)}, bf16[1024,512]{0,1:T(8,128)(2,1)}, u32[]{:S(2)}, u32[]{:S(2)}) collective-permute-start(bf16[1024,512]{0,1:T(8,128)(2,1)} %convolution_convert_fusion.2), channel_id=1, source_target_pairs={{0,1},{1,0},{2,3},{3,2},{4,5},{5,4},{6,7},{7,6},{8,9},{9,8},{10,11... | collective-permute-start | bytes 3145736 | tf_op jit(solution)/shard_map/ppermute | solution.py:17
  408.2 56.4 %collective-permute-start.36 = (bf16[1024,512]{0,1:T(8,128)(2,1)}, bf16[1024,512]{0,1:T(8,128)(2,1)}, u32[]{:S(2)}, u32[]{:S(2)}) collective-permute-start(bf16[1024,512]{0,1:T(8,128)(2,1)} %convolution_convert_fusion.3), channel_id=1, source_target_pairs={{0,1},{1,0},{2,3},{3,2},{4,5},{5,4},{6,7},{7,6},{8,9},{9,8},{10,11... | collective-permute-start | bytes 3145736 | tf_op jit(solution)/shard_map/ppermute | solution.py:17
  416.8 13.5 %collective-permute-start.54 = (bf16[128,1920]{1,0:T(8,128)(2,1)S(1)}, bf16[128,1920]{1,0:T(8,128)(2,1)S(1)}, u32[]{:S(2)}, u32[]{:S(2)}) collective-permute-start(bf16[128,1920]{1,0:T(8,128)(2,1)S(1)} %get-tuple-element.190), channel_id=1, source_target_pairs={{0,24},{4,28},{8,0},{12,4},{16,8},{20,12},{24,16},{28,20},{1,25},{... | collective-permute-start | bytes 1474568 | tf_op jit(solution)/shard_map/ppermute | solution.py:22
  416.9 39.9 %collective-permute-start.55 = (bf16[128,1920]{1,0:T(8,128)(2,1)S(1)}, bf16[128,1920]{1,0:T(8,128)(2,1)S(1)}, u32[]{:S(2)}, u32[]{:S(2)}) collective-permute-start(bf16[128,1920]{1,0:T(8,128)(2,1)S(1)} %get-tuple-element.192), channel_id=1, source_target_pairs={{0,16},{4,20},{8,24},{12,28},{16,0},{20,4},{24,8},{28,12},{1,17},{... | collective-permute-start | bytes 1474568 | tf_op jit(solution)/shard_map/ppermute | solution.py:22
  417.0 39.9 %collective-permute-start.56 = (bf16[128,1920]{1,0:T(8,128)(2,1)S(1)}, bf16[128,1920]{1,0:T(8,128)(2,1)S(1)}, u32[]{:S(2)}, u32[]{:S(2)}) collective-permute-start(bf16[128,1920]{1,0:T(8,128)(2,1)S(1)} %get-tuple-element.191), channel_id=1, source_target_pairs={{0,8},{4,12},{8,16},{12,20},{16,24},{20,28},{24,0},{28,4},{1,9},{5... | collective-permute-start | bytes 1474568 | tf_op jit(solution)/shard_map/ppermute | solution.py:22
  422.2 40.9 %collective-permute-start.45 = (bf16[1024,512]{0,1:T(8,128)(2,1)}, bf16[1024,512]{0,1:T(8,128)(2,1)}, u32[]{:S(2)}, u32[]{:S(2)}) collective-permute-start(bf16[1024,512]{0,1:T(8,128)(2,1)} %pad_maximum_fusion.12), channel_id=1, source_target_pairs={{0,4},{4,0},{8,12},{12,8},{16,20},{20,16},{24,28},{28,24},{1,5},{5... | collective-permute-start | bytes 3145736 | tf_op jit(solution)/shard_map/ppermute | solution.py:17
  430.3 34.3 %collective-permute-start.38 = (bf16[1024,512]{0,1:T(8,128)(2,1)}, bf16[1024,512]{0,1:T(8,128)(2,1)}, u32[]{:S(2)}, u32[]{:S(2)}) collective-permute-start(bf16[1024,512]{0,1:T(8,128)(2,1)} %add_convert_fusion), channel_id=1, source_target_pairs={{0,2},{1,3},{2,0},{3,1},{4,6},{5,7},{6,4},{7,5},{8,10},{9,11},{10,... | collective-permute-start | bytes 3145736 | tf_op jit(solution)/shard_map/ppermute | solution.py:17
  464.4 13.3 %collective-permute-start.46 = (bf16[512,512]{0,1:T(8,128)(2,1)S(1)}, bf16[512,512]{0,1:T(8,128)(2,1)S(1)}, u32[]{:S(2)}, u32[]{:S(2)}) collective-permute-start(bf16[512,512]{0,1:T(8,128)(2,1)S(1)} %fusion.71), channel_id=1, source_target_pairs={{0,2},{1,3},{2,0},{3,1},{4,6},{5,7},{6,4},{7,5},{8,10},{9,11},{10,... | collective-permute-start | bytes 1572872 | tf_op jit(solution)/shard_map/ppermute | solution.py:17
  467.8 32.5 %collective-permute-start.39 = (bf16[512,512]{0,1:T(8,128)(2,1)}, bf16[512,512]{0,1:T(8,128)(2,1)}, u32[]{:S(2)}, u32[]{:S(2)}) collective-permute-start(bf16[512,512]{0,1:T(8,128)(2,1)} %slice.1199), channel_id=1, source_target_pairs={{0,4},{4,0},{8,12},{12,8},{16,20},{20,16},{24,28},{28,24},{1,5},{5... | collective-permute-start | bytes 1572872 | tf_op jit(solution)/shard_map/ppermute | solution.py:17
  480.8 18.4 %collective-permute-start.48 = (bf16[128,512]{0,1:T(8,128)(2,1)}, bf16[128,512]{0,1:T(8,128)(2,1)S(1)}, u32[]{:S(2)}, u32[]{:S(2)}) collective-permute-start(bf16[128,512]{0,1:T(8,128)(2,1)} %get-tuple-element.206), channel_id=1, source_target_pairs={{0,16},{4,20},{8,24},{12,28},{16,0},{20,4},{24,8},{28,12},{1,17},{... | collective-permute-start | bytes 393224 | tf_op jit(solution)/shard_map/ppermute | solution.py:22
  487.6 11.6 %collective-permute-start.49 = (bf16[128,512]{0,1:T(8,128)(2,1)S(1)}, bf16[128,512]{0,1:T(8,128)(2,1)S(1)}, u32[]{:S(2)}, u32[]{:S(2)}) collective-permute-start(bf16[128,512]{0,1:T(8,128)(2,1)S(1)} %get-tuple-element.205), channel_id=1, source_target_pairs={{0,8},{4,12},{8,16},{12,20},{16,24},{20,28},{24,0},{28,4},{1,9},{5... | collective-permute-start | bytes 393224 | tf_op jit(solution)/shard_map/ppermute | solution.py:22
  501.7 11.9 %collective-permute-start.41 = (bf16[128,512]{0,1:T(8,128)(2,1)S(1)}, bf16[128,512]{0,1:T(8,128)(2,1)S(1)}, u32[]{:S(2)}, u32[]{:S(2)}) collective-permute-start(bf16[128,512]{0,1:T(8,128)(2,1)S(1)} %get-tuple-element.209), channel_id=1, source_target_pairs={{0,16},{4,20},{8,24},{12,28},{16,0},{20,4},{24,8},{28,12},{1,17},{... | collective-permute-start | bytes 393224 | tf_op jit(solution)/shard_map/ppermute | solution.py:22
  (112 other events, 709.8 us)
Sparse Core Ops, SparseCore 0:
  22.0 94.3 all-gather.3
where the time goes:
time: 530 us; the launch traced here: 522 us
  waiting for transfers between devices  148 us (28%)
  matrix products  74.4 us (14%)
  starting transfers between devices  67.2 us (13%)
  other arithmetic  60.2 us (11%)
  local copies, waits for them, and re-layouts  57.1 us (11%)
  Pallas kernels  55.9 us (11%)
  blocking collectives  41 us (8%)
  between operations  17.7 us (3%)
    ppermute x18, waiting for transfers between devices, ring(): lax.ppermute(value, axis, [(i, (i + by) % peers) for i in range(peers)])  112 us
    pallas_call x4, Pallas kernels, ffn(): pl.pallas_call(kernel, grid_spec=pltpu.PrefetchScalarGridSpec(num_scalar_...  55.9 us
    all_gather x1, blocking collectives, sum_all(): return jnp.sum(lax.all_gather(value, ('dp', 'tensor'), axis=0), axis=0)  41 us
    dot_general x20, matrix products, tn(): lax.dot_general(left, right, (((0,), (0,)), ((), ())), preferred_element_...  39.7 us
    ppermute x37, waiting for transfers between devices, swap(): return lax.ppermute(value, axis, [(i, i ^ bit) for i in range(peers)])  35.4 us
    ppermute x18, starting transfers between devices, ring(): lax.ppermute(value, axis, [(i, (i + by) % peers) for i in range(peers)])  32.8 us
    ppermute x37, starting transfers between devices, swap(): return lax.ppermute(value, axis, [(i, i ^ bit) for i in range(peers)])  31.8 us
    dot_general x16, matrix products, nn(): return jnp.dot(left, right, preferred_element_type=F32)  25.4 us
  transfers between devices with their start and end apart: 58, of which 19 were waited for; matrix products, arithmetic and copies ran while one was open for 31% of the time, Pallas kernels for 8%

commit v1 on v0

--- a/solution.py
+++ b/solution.py
@@ -28,6 +28,12 @@
     return lax.ppermute(value, ("dp", "tensor"), pairs)
 
 
+def cross(value):
+    inner = lax.axis_size("tensor")
+    peers = lax.axis_size("dp") * inner
+    return lax.ppermute(value, ("dp", "tensor"), [(i, i ^ (inner + 2)) for i in range(peers)])
+
+
 def nn(left, right):
     return jnp.dot(left, right, preferred_element_type=F32)
 
@@ -95,16 +101,17 @@
 
 
 def ffn(hidden, cot, weights, order, before, kept, part, tile):
-    rows, width = hidden.shape
+    rows, width = 2 * hidden[0].shape[0], hidden[0].shape[1]
     size = weights[0].shape[1] // 3
     count = order.shape[0]
     block = width // count
-    skip = part * (rows // tile)
-
-    def kernel(order_ref, h_ref, g_ref, *refs):
-        w_any, refs = refs[: len(weights)], refs[len(weights) :]
-        w_ref, sems = refs[-2:]
-        d_ref, o_ref, d_gu_ref, act_ref = refs[-6:-2]
+    steps = rows // tile
+    skip = part * steps
+
+    def kernel(order_ref, *refs):
+        slots, w_any, refs = refs[:4], refs[4 : 4 + len(weights)], refs[4 + len(weights) :]
+        w_ref, sems, h_ref, g_ref = refs[-4:]
+        sum_ref, d_gu_ref, act_ref = refs[-7:-4]
 
         @pl.when(pl.program_id(0) == 0)
         def _():
@@ -122,6 +129,13 @@
             for copy in copies:
                 copy.wait()
 
+        for slot in (0, 1):
+
+            @pl.when(pl.program_id(0) // (steps // 2) == slot)
+            def _(slot=slot):
+                h_ref[...] = slots[slot][...]
+                g_ref[...] = slots[2 + slot][...]
+
         gate_up = nn(h_ref[...], w_ref[:, : 2 * size])
         d_act = nn(g_ref[...], w_ref[:, 2 * size :])
         gate, up = gate_up[:, :size], gate_up[:, size:]
@@ -134,23 +148,24 @@
         d_sum = nt(d_gu_ref[...], w_ref[:, : 2 * size])
         o_sum = nt(act, w_ref[:, 2 * size :])
         if before:
-            d_sum = d_sum + refs[0][...]
-            o_sum = o_sum + refs[1][...]
-        d_ref[...] = d_sum.astype(d_ref.dtype)
-        o_ref[...] = o_sum.astype(o_ref.dtype)
-
-    tokens = pl.BlockSpec((tile, width), lambda i, _: (i, 0))
+            d_sum = d_sum + refs[0][:, :width]
+            o_sum = o_sum + refs[0][:, width:]
+        sum_ref[:, :width] = d_sum.astype(sum_ref.dtype)
+        sum_ref[:, width:] = o_sum.astype(sum_ref.dtype)
+
+    tokens = pl.BlockSpec((tile, 2 * width), lambda i, _: (i, 0))
     whole = pl.BlockSpec(memory_space=pl.ANY)
+    near = pl.BlockSpec((tile, width), lambda i, _: (jnp.minimum(i, steps // 2 - 1), 0))
+    far = pl.BlockSpec((tile, width), lambda i, _: (jnp.maximum(i - steps // 2, 0), 0))
     kind = BF if before else F32
-    aliased = 3 + len(weights) + len(before)
+    aliased = 5 + len(weights) + len(before)
     return pl.pallas_call(
         kernel,
         grid_spec=pltpu.PrefetchScalarGridSpec(
             num_scalar_prefetch=1,
             grid=(rows // tile,),
-            in_specs=[tokens] * 2 + [whole] * len(weights) + [tokens] * len(before) + [whole] * len(kept),
+            in_specs=[near, far] * 2 + [whole] * len(weights) + [tokens] * len(before) + [whole] * len(kept),
             out_specs=[
-                tokens,
                 tokens,
                 pl.BlockSpec((tile, 2 * size), lambda i, _: (i + skip, 0)),
                 pl.BlockSpec((tile, size), lambda i, _: (i + skip, 0)),
@@ -158,31 +173,28 @@
             scratch_shapes=[
                 pltpu.VMEM((width, 3 * size), BF),
                 pltpu.SemaphoreType.DMA((count,)),
+                pltpu.VMEM((tile, width), BF),
+                pltpu.VMEM((tile, width), BF),
             ],
         ),
         out_shape=[
-            jax.ShapeDtypeStruct((rows, width), kind),
-            jax.ShapeDtypeStruct((rows, width), kind),
+            jax.ShapeDtypeStruct((rows, 2 * width), kind),
             jax.ShapeDtypeStruct((2 * rows, 2 * size), BF),
             jax.ShapeDtypeStruct((2 * rows, size), BF),
         ],
-        input_output_aliases={aliased: 2, aliased + 1: 3} if kept else {},
+        input_output_aliases={aliased: 1, aliased + 1: 2} if kept else {},
         compiler_params=pltpu.CompilerParams(vmem_limit_bytes=48 << 20),
         cost_estimate=pl.CostEstimate(
             flops=12 * rows * width * size,
             bytes_accessed=rows * width * 12 + width * size * 6,
             transcendentals=rows * size,
         ),
-    )(order, hidden, cot, *weights, *before, *kept)
+    )(order, *hidden, *cot, *weights, *before, *kept)
 
 
 def by_xor(groups, me):
     one = [jnp.where((me & 1) == 1, groups[i ^ 1], groups[i]) for i in range(4)]
     return [jnp.where((me & 2) == 2, one[i ^ 2], one[i]) for i in range(4)]
-
-
-def sum_all(value):
-    return jnp.sum(lax.all_gather(value, ("dp", "tensor"), axis=0), axis=0)
 
 
 def body(
@@ -225,7 +237,6 @@
         )
         for lo, hi in bounds
     ]
-    block_two = [lax.all_gather(shards[1], "dp", axis=0, tiled=True)]
 
     if long:
         whole = jnp.concatenate([long_gather(packed), taps_rows], axis=0)
@@ -249,6 +260,7 @@
         here_one = chain(after(shards[0], here[-1]))
         across_one = others(here_one)
         block_one = here_one + across_one
+    block_two = [lax.all_gather(after(shards[1], here[-1]), "dp", axis=0, tiled=True)]
     mix = [whole, swap(whole, "tensor", 1), whole_y, swap(whole_y, "tensor", 1)]
 
     lane = jnp.arange(width, dtype=jnp.int32)
@@ -296,7 +308,7 @@
     normed_two, scale_two = normalize(resid)
     hidden_two = (normed_two * gain_two).astype(BF)
     hid_y = swap(hidden_two, "tensor", 2)
-    tile = min(rows, 256)
+    tile = min(rows // 2, 256)
 
     def weight_grads(d_gu, act, earlier):
         parts = []
@@ -306,39 +318,42 @@
             parts.append(jnp.concatenate(grads, axis=1))
         return parts
 
-    def over_x(parts):
+    def over_x(parts, *late):
         if long:
             return parts
-        total = parts[1].astype(F32) + swap(parts[0], "dp", 1).astype(F32)
+        total = parts[1].astype(F32) + after(swap(parts[0], "dp", 1), *late).astype(F32)
         return total.reshape(deep, block, -1)
 
-    hid = [jnp.concatenate([hidden_two, swap(hidden_two, "tensor", 1)], axis=0)]
-    cots = [jnp.concatenate([cot, swap(cot, "tensor", 1)], axis=0)]
-    near = ffn(after(hid[0], *block_two), cots[0], block_one, order, (), (), 0, tile)
+    hid = [[hidden_two, swap(hidden_two, "tensor", 1)]]
+    cots = [[cot, swap(cot, "tensor", 1)]]
+    hid[0][0] = after(hid[0][0], *block_two)
+    near = ffn(hid[0], cots[0], block_one, order, (), (), 0, tile)
     hid_y, cot_y = lax.optimization_barrier((hid_y, cot_y, near[0]))[:2]
-    hid.append(jnp.concatenate([hid_y, swap(hid_y, "tensor", 1)], axis=0))
-    cots.append(jnp.concatenate([cot_y, swap(cot_y, "tensor", 1)], axis=0))
-    hid_all, cot_all = jnp.concatenate(hid, axis=0), jnp.concatenate(cots, axis=0)
-    far = ffn(hid[1], cots[1], block_one, order, (), tuple(near[2:]), 1, tile)
-    parts_one = weight_grads(*far[2:], ((), ()))
-    sums_one = over_x(parts_one)
-    far_two = ffn(after(hid[1], *parts_one), cots[1], block_two, order, tuple(far[:2]), (), 1, tile)
-    d_far = far_two[0][:rows].astype(F32) + swap(far_two[0][rows:], "tensor", 1).astype(F32)
-    d_far = d_far.astype(BF)
+    hid.append([hid_y, swap(hid_y, "tensor", 1)])
+    cots.append([cot_y, swap(cot_y, "tensor", 1)])
+    far = ffn(hid[1], cots[1], block_one, order, (), tuple(near[1:]), 1, tile)
+    hid_all, cot_all = jnp.concatenate(hid[0] + hid[1], axis=0), jnp.concatenate(cots[0] + cots[1], axis=0)
+    parts_one = weight_grads(*far[1:], ((), ()))
+    far_two = ffn(
+        [after(hid[1][0], *parts_one), hid[1][1]], cots[1], block_two, order, (far[0],), (), 1, tile
+    )
+
+    far_core = swap(far_two[0][rows:], "tensor", 1)
+    sum_far = (far_two[0][:rows].astype(F32) + far_core.astype(F32)).astype(BF)
+    d_far, out_far = sum_far[:, :width], sum_far[:, width:]
     d_y = [swap(part, "tensor", 2) for part in (d_far[: rows // 2], d_far[rows // 2 :])]
     near_two = ffn(
-        after(hid[0], d_far), cots[0], block_two, order, tuple(near[:2]), tuple(far_two[2:]), 0, tile
+        [after(hid[0][0], far_core), hid[0][1]], cots[0], block_two, order, (near[0],), tuple(far_two[1:]), 0, tile
     )
-    parts_two = weight_grads(*near_two[2:], ((d_y[0],), ()))
-    sums_two = over_x(parts_two)
-
-    d_hidden_two = near_two[0][:rows].astype(F32) + swap(near_two[0][rows:], "tensor", 1).astype(F32)
-    d_hidden_two = d_hidden_two + jnp.concatenate(d_y, axis=0).astype(F32)
+    parts_two = weight_grads(*near_two[1:], ((d_y[0],), ()))
+    sums_one, sums_two = over_x(parts_one, near_two[1]), over_x(parts_two)
+
+    near_core = swap(near_two[0][rows:], "tensor", 1)
+    sum_near = near_two[0][:rows].astype(F32) + near_core.astype(F32)
+    d_hidden_two = sum_near[:, :width] + jnp.concatenate(d_y, axis=0).astype(F32)
     d_hidden_two = after(d_hidden_two, parts_two[1])
-    out_far = far_two[1][:rows].astype(F32) + swap(far_two[1][rows:], "tensor", 1).astype(F32)
-    out_y = swap(after(out_far.astype(BF), *d_y), "tensor", 2)
-    out_own = near_two[1][:rows].astype(F32) + swap(near_two[1][rows:], "tensor", 1).astype(F32)
-    out_own = out_own + out_y.astype(F32)
+    out_y = swap(after(out_far, *d_y), "tensor", 2)
+    out_own = sum_near[:, width:] + out_y.astype(F32)
     block_out = reorder((resid + out_own).astype(BF), perm_back)
 
     d_resid = cot.astype(F32) + norm_back(d_hidden_two * gain_two, normed_two, scale_two)
@@ -350,23 +365,33 @@
     following = shift(first, -1)
     following = by_xor([following[i] for i in range(4)], me_t)
 
-    def over_z(sums):
-        sums = sums.reshape(deep, block, -1)
-        low = sums.astype(BF)
-        total = sums[0]
-        for k in range(1, deep):
-            total = total + ring(low[k], "dp", -2 * k).astype(F32)
-        return total
-
+    def add_z(sums):
+        return sum(
+            [sums[0]] + [ring(sums[k].astype(BF), "dp", -2 * k).astype(F32) for k in range(1, deep)]
+        )
+
+    def fold(sums, late):
+        if long:
+            return sums, late
+        part = sums.shape[0] // 2
+        got = ring(sums[part:].astype(BF), "dp", -2 * part)
+        got, late = lax.optimization_barrier((got, late))
+        return sums[:part] + got.astype(F32), late
+
+    sums_one, d_conv[0] = fold(sums_one, d_conv[0])
     d_cs = [(d_gated[r] * saved[r][6]).astype(BF) for r in range(4)]
+
+    def sides(values, r):
+        return jnp.concatenate([values[r], values[r + 2]], axis=1)
+
+    gates = [saved[r][7] for r in range(4)]
     right = [
         jnp.concatenate(
-            [tn(hidden_one, d_cs[r]).astype(BF), tn(d_mix, saved[r][7]).astype(BF)], axis=1
+            [tn(hidden_one, sides(d_cs, r)).astype(BF), tn(d_mix, sides(gates, r)).astype(BF)], axis=1
         )
-        for r in range(4)
+        for r in (1, 0)
     ]
-    right_near = right[0].astype(F32) + swap(right[1], "tensor", 1).astype(F32)
-    right_far = right[2].astype(F32) + swap(right[3], "tensor", 1).astype(F32)
+    right_core = swap(right[0], "tensor", 1)
 
     d_bvs = []
     for r in range(4):
@@ -378,11 +403,18 @@
             + taps[2] * next_two * ahead[2:]
         )
         d_bvs.append(jnp.concatenate([d_bx * v_part, d_bx * b_part], axis=1).astype(BF))
-    hidden_late = after(hidden_one, right[1], right[3], sums_one[0], out_y)
-    left = [tn(hidden_late, d_bvs[r]).astype(BF) for r in range(4)]
-    left_near = left[0].astype(F32) + swap(left[1], "tensor", 1).astype(F32)
-    left_far = left[2].astype(F32) + swap(left[3], "tensor", 1).astype(F32)
-
+    sums_one, hidden_late = fold(sums_one, after(hidden_one, *right, sums_two, out_y))
+    left = [tn(hidden_late, sides(d_bvs, r)).astype(BF) for r in (1, 0)]
+    left_core = swap(left[0], "tensor", 1)
+
+    side = 2 * channels
+    right_all = right[1].astype(F32) + right_core.astype(F32)
+    right_near, right_far = (
+        jnp.concatenate([right_all[:, i : i + channels], right_all[:, i + side : i + side + channels]], axis=1)
+        for i in (0, channels)
+    )
+    left_all = left[1].astype(F32) + left_core.astype(F32)
+    left_near, left_far = left_all[:, :side], left_all[:, side:]
     left_y = swap(left_far.astype(BF), "tensor", 2)
     left_sum = left_near + left_y.astype(F32)
     if long:
@@ -395,12 +427,14 @@
         right_x = swap(jnp.concatenate([right_near[half:], right_far[half:]], axis=0).astype(BF), "dp", 1)
         right_near = right_near[:half] + right_x[:half].astype(F32)
         right_far = right_far[:half] + right_x[half:].astype(F32)
+        sums_two, right_far = fold(sums_two, right_far)
         right_sum = right_near + swap(right_far.astype(BF), "tensor", 2).astype(F32)
         left_sum = left_sum[:half] + swap(left_sum[half:].astype(BF), "dp", 1).astype(F32)
-
-        mix_sum = jnp.concatenate([over_z(left_sum), over_z(right_sum)], axis=1)
-        ffn_grads = [over_z(sums_one), over_z(sums_two)]
-        d_late = lax.optimization_barrier((d_cs, left[0], left[2], left[1], left[3]))[0]
+        total = jnp.concatenate([left_sum, right_sum], axis=1).reshape(deep, block, -1)
+        sums_two, total = fold(sums_two, total)
+        mix_sum = add_z(total)
+        ffn_grads = [sums_one[0], sums_two[0]]
+        d_late = lax.optimization_barrier((d_cs, *left))[0]
 
     d_hidden_one = 0.0
     for r, group in enumerate(mix):
@@ -416,7 +450,18 @@
     ]
     conv_all = jnp.stack(by_xor(conv_parts, me_t), axis=1)
     gain_parts = reorder_f32(jnp.stack([part_gain_one, part_gain_two]), perm_back)
-    small = sum_all(jnp.concatenate([gain_parts, conv_all.reshape(-1, width)], axis=0))
+    small = jnp.concatenate([gain_parts, conv_all.reshape(-1, width)], axis=0)
+    if long:
+        small = lax.psum(small, ("dp", "tensor"))
+    else:
+        small = small + swap(small, "tensor", 1)
+        bit = deep // 2
+        while bit:
+            small = small + ring(small, "dp", 2 * bit)
+            bit //= 2
+        small = after(small, right_x)
+        got = [swap(small, "dp", 1), swap(small, "tensor", 2), cross(small)]
+        small = sum(lax.optimization_barrier((small, *got, total))[:4])
     grad_conv = lax.dynamic_slice(small, (2, me_t * channels), (small.shape[0] - 2, channels))
 
     grad_in = jnp.stack([mix_sum[:, i * channels : (i + 1) * channels] for i in (0, 2, 1)], axis=1)

time: 530 us -> 507 us (0.957); the launches traced: 522 us -> 504 us
  blocking collectives: 41 us -> 0 us
  waiting for transfers between devices: 148 us -> 116 us
  starting transfers between devices: 67.2 us -> 89.7 us
  local copies, waits for them, and re-layouts: 57.1 us -> 79.3 us
  Pallas kernels: 55.9 us -> 70.4 us
  other arithmetic: 60.2 us -> 52.5 us
    ppermute x18 -> x15, waiting for transfers between devices: 112 us -> 53.4 us  [ring(): lax.ppermute(value, axis, [(i, (i + by) % peers) for i in range(peers)])]
    all_gather x1 -> x0, blocking collectives: 41 us -> none  [sum_all(): return jnp.sum(lax.all_gather(value, ('dp', 'tensor'), axis=0), axis=0)]
    ppermute x37 -> x36, starting transfers between devices: 31.8 us -> 66 us  [swap(): return lax.ppermute(value, axis, [(i, i ^ bit) for i in range(peers)])]
    ppermute x37 -> x36, waiting for transfers between devices: 35.4 us -> 50.4 us  [swap(): return lax.ppermute(value, axis, [(i, i ^ bit) for i in range(peers)])]
    pallas_call x4, Pallas kernels: 55.9 us -> 70.4 us  [ffn(): pl.pallas_call(kernel, grid_spec=pltpu.PrefetchScalarGridSpec(num_scalar_...]
    ppermute x18 -> x15, starting transfers between devices: 32.8 us -> 18.9 us  [ring(): lax.ppermute(value, axis, [(i, (i + by) % peers) for i in range(peers)])]
    slice x10 -> x13, local copies, waits for them, and re-layouts: 4.43 us -> 17.5 us  [the longest x4 7.57 us: fold(): return (sums[:part] + got.astype(F32), late)]
    all_gather x1, waiting for transfers between devices: 0.01 us -> 12.5 us  [body(): lax.all_gather(after(shards[1], here[-1]), 'dp', axis=0, tiled=True)]
  transfers between devices with their start and end apart: 58 -> 55, of which waited for: 19 -> 17; matrix products, arithmetic and copies ran while one was open for 31% -> 33% of each run, Pallas kernels for 8% -> 6%
where the time goes in v1:
time: 507 us; the launch traced here: 504 us
  waiting for transfers between devices  116 us (23%)
  starting transfers between devices  89.7 us (18%)
  local copies, waits for them, and re-layouts  79.3 us (16%)
  matrix products  78.1 us (15%)
  Pallas kernels  70.4 us (14%)
  other arithmetic  52.5 us (10%)
  between operations  18 us (4%)
    pallas_call x4, Pallas kernels, ffn(): pl.pallas_call(kernel, grid_spec=pltpu.PrefetchScalarGridSpec(num_scalar_...  70.4 us
    ppermute x36, starting transfers between devices, swap(): return lax.ppermute(value, axis, [(i, i ^ bit) for i in range(peers)])  66 us
    ppermute x15, waiting for transfers between devices, ring(): lax.ppermute(value, axis, [(i, (i + by) % peers) for i in range(peers)])  53.4 us
    ppermute x36, waiting for transfers between devices, swap(): return lax.ppermute(value, axis, [(i, i ^ bit) for i in range(peers)])  50.4 us
    dot_general x14, matrix products, tn(): lax.dot_general(left, right, (((0,), (0,)), ((), ())), preferred_element_...  45.5 us
    unnamed x283, local copies, waits for them, and re-layouts  33.5 us
    dot_general x16, matrix products, nn(): return jnp.dot(left, right, preferred_element_type=F32)  23.2 us
    ppermute x15, starting transfers between devices, ring(): lax.ppermute(value, axis, [(i, (i + by) % peers) for i in range(peers)])  18.9 us
  transfers between devices with their start and end apart: 55, of which 17 were waited for; matrix products, arithmetic and copies ran while one was open for 33% of the time, Pallas kernels for 6%

profile of v1, /device:TPU:0, one launch (start us, length us, event | category | flops | bytes accessed | tf_op | source)
XLA Modules:
  0.0 504.2 jit_solution(70596011187483819)
XLA Ops:
  10.3 2.9 collective-permute-start.4
  38.2 2.5 collective-permute-start.5
  41.5 3.3 collective-permute-done.2
  45.4 2.7 concatenate.238
  53.3 7.2 %collective-permute-done.3 = bf16[128,1024]{1,0:T(8,128)(2,1)S(1)} collective-permute-done((bf16[128,1024]{1,0:T(8,128)(2,1)S(1)}, bf16[128,1024]{1,0:T(8,128)(2,1)S(1)}, u32[]{:S(2)}, u32[]{:S(2)}) %collective-permute-start.3) | collective-permute-done | bytes 262176 | tf_op jit(solution)/shard_map/ppermute | solution.py:22
  70.3 2.4 fusion.56
  75.3 4.4 collective-permute-done.12
  79.7 2.9 collective-permute-done.15.refs_8_
  82.6 11.7 %collective-permute-done.14.refs_6_ = bf16[128,1536]{1,0:T(8,128)(2,1)} collective-permute-done((bf16[128,1536]{1,0:T(8,128)(2,1)S(1)}, bf16[128,1536]{1,0:T(8,128)(2,1)}, u32[]{:S(2)}, u32[]{:S(2)}) %collective-permute-start.14) | collective-permute-done | bytes 393248 | tf_op jit(solution)/shard_map/ppermute | solution.py:22
  112.7 16.1 %collective-permute-done.22.refs_9_ = bf16[128,1536]{1,0:T(8,128)(2,1)S(1)} collective-permute-done((bf16[128,1536]{1,0:T(8,128)(2,1)S(1)}, bf16[128,1536]{1,0:T(8,128)(2,1)S(1)}, u32[]{:S(2)}, u32[]{:S(2)}) %collective-permute-start.22) | collective-permute-done | bytes 393248 | tf_op jit(solution)/shard_map/ppermute | solution.py:17
  133.2 12.5 %all-gather.2.cloned.1.call-done.refs_4_ = bf16[1024,1920]{1,0:T(8,128)(2,1)} async-done(((bf16[128,1920]{1,0:T(8,128)(2,1)}), bf16[1024,1920]{1,0:T(8,128)(2,1)}) %all-gather.2.cloned.1.call-update) | async-done | bytes 3932176 | tf_op jit(solution)/shard_map/all_gather | solution.py:263
  145.7 3.0 collective-permute-done.24.refs_11_
  152.0 13.4 %shard_map.169 = (f32[1024,2048]{1,0:T(8,128)}, bf16[2048,1024]{1,0:T(8,128)(2,1)}, bf16[2048,512]{1,0:T(8,128)(2,1)}) custom-call(s32[8]{0:T(128)S(1)} %get-tuple-element.198.order_ref, bf16[512,1024]{1,0:T(8,128)(2,1)S(1)} %multiply_convert_fusion.1.refs_0_, bf16[512,1024]{1,0:T(8,128)(2,1)S(1)} %collective-permute-done.19.refs_1_, ...), custom_call_target="tpu_custom_call" | custom-call | flops 6442450944 | bytes 15728640 | tf_op jit(solution)/shard_map/pallas_call | solution.py:162
  174.3 13.6 %shard_map.170 = (f32[1024,2048]{1,0:T(8,128)}, bf16[2048,1024]{1,0:T(8,128)(2,1)}, bf16[2048,512]{1,0:T(8,128)(2,1)}) custom-call(s32[8]{0:T(128)S(1)} %get-tuple-element.198.order_ref, bf16[512,1024]{1,0:T(8,128)(2,1)} %collective-permute-done.17.refs_0_, ...), custom_call_target="tpu_custom_call", output_to_operand_aliasing={{1}: (13, {}), {2}: (14, {})} | custom-call | flops 6442450944 | bytes 15728640 | tf_op jit(solution)/shard_map/pallas_call | solution.py:162
  187.9 3.0 fusion.67
  191.0 3.9 fusion.40
  196.6 27.7 %shard_map.171 = (bf16[1024,2048]{1,0:T(8,128)(2,1)}, bf16[2048,1280]{1,0:T(8,128)(2,1)}, bf16[2048,640]{1,0:T(8,128)(2,1)}) custom-call(s32[8]{0:T(128)S(1)} %get-tuple-element.198.order_ref, bf16[512,1024]{1,0:T(8,128)(2,1)} %collective-permute-done.17.refs_0_, bf16[512,1024]{1,0:T(8,128)(2,1)S(1)} %collective-permute-done.25.refs_1_, ...), custom_call_target="tpu_custom_call" | custom-call | flops 8053063680 | bytes 16515072 | tf_op jit(solution)/shard_map/pallas_call | solution.py:162
  224.4 3.2 slice.651
  231.6 5.5 %fusion.37 = bf16[512,1024]{1,0:T(8,128)(2,1)S(1)} fusion(bf16[2048,1024]{1,0:T(8,128)(2,1)} %get-tuple-element.98, bf16[2048,1024]{1,0:T(8,128)(2,1)} %constant_dynamic-update-slice_fusion.17), kind=kOutput, calls=%fused_computation.87 | convolution fusion | flops 2148007936 | bytes 7340032 | tf_op jit(solution)/shard_map/dot_general | solution.py:42
  238.5 15.7 %shard_map.172 = (bf16[1024,2048]{1,0:T(8,128)(2,1)}, bf16[2048,1280]{1,0:T(8,128)(2,1)}, bf16[2048,640]{1,0:T(8,128)(2,1)}) custom-call(s32[8]{0:T(128)S(1)} %get-tuple-element.198.order_ref, bf16[512,1024]{1,0:T(8,128)(2,1)S(1)} %multiply_convert_fusion.1.refs_0_, bf16[512,1024]{1,0:T(8,128)(2,1)S(1)} %copy-done.5, ...), custom_call_target="tpu_custom_call", output_to_operand_aliasing={{1}: (7, {}), {2}: (8, {})} | custom-call | flops 8053063680 | bytes 16515072 | tf_op jit(solution)/shard_map/pallas_call | solution.py:162
  254.2 7.3 %convolution_convert_fusion.1 = bf16[512,1280]{1,0:T(8,128)(2,1)} fusion(bf16[2048,1280]{1,0:T(8,128)(2,1)} %get-tuple-element.109, bf16[2048,1024]{1,0:T(8,128)(2,1)} %constant_dynamic-update-slice_fusion.17), kind=kOutput, calls=%fused_computation.18 | convolution fusion | flops 2685009920 | bytes 8650752 | tf_op jit(solution)/shard_map/dot_general | solution.py:42
  261.5 5.3 %collective-permute-done.32 = bf16[512,1536]{1,0:T(8,128)(2,1)S(1)} collective-permute-done((bf16[512,1536]{1,0:T(8,128)(2,1)S(1)}, bf16[512,1536]{1,0:T(8,128)(2,1)S(1)}, u32[]{:S(2)}, u32[]{:S(2)}) %collective-permute-start.32) | collective-permute-done | bytes 1572896 | tf_op jit(solution)/shard_map/ppermute | solution.py:17
  266.8 2.5 add_convert_fusion
  279.2 4.4 fusion.58
  283.5 11.9 %collective-permute-done.29 = bf16[256,1024]{1,0:T(8,128)(2,1)} collective-permute-done((bf16[256,1024]{1,0:T(8,128)(2,1)}, bf16[256,1024]{1,0:T(8,128)(2,1)}, u32[]{:S(2)}, u32[]{:S(2)}) %collective-permute-start.29) | collective-permute-done | bytes 524320 | tf_op jit(solution)/shard_map/ppermute | solution.py:17
  297.2 3.6 fusion.61
  300.8 6.2 %convolution_convert_fusion = bf16[512,1280]{1,0:T(8,128)(2,1)S(1)} fusion(bf16[2048,1280]{1,0:T(8,128)(2,1)} %get-tuple-element.109, bf16[2048,1024]{1,0:T(8,128)(2,1)} %constant_dynamic-update-slice_fusion.17), kind=kOutput, calls=%fused_computation.17 | convolution fusion | flops 2685009920 | bytes 8650752 | tf_op jit(solution)/shard_map/dot_general | solution.py:42
  317.7 2.5 collective-permute-start.35
  330.3 2.5 fusion.36
  337.6 2.7 convolution_convert_fusion.3
  341.0 2.6 convolution_convert_fusion.2
  347.8 3.0 multiply_reduce_fusion.1
  354.8 2.9 fusion.2
  363.8 3.1 convert_add_fusion.1
  369.3 15.6 %collective-permute-start.40 = (bf16[1024,512]{0,1:T(8,128)(2,1)}, bf16[1024,512]{0,1:T(8,128)(2,1)}, u32[]{:S(2)}, u32[]{:S(2)}) collective-permute-start(bf16[1024,512]{0,1:T(8,128)(2,1)} %pad_maximum_fusion.12), channel_id=1, source_target_pairs={{0,4},{4,0},{8,12},{12,8},{16,20},{20,16},{24,28},{28,24},{1,5},{5... | collective-permute-start | bytes 3145736 | tf_op jit(solution)/shard_map/ppermute | solution.py:17
  384.8 2.6 convert_add_fusion
  393.8 2.8 fusion.34
  396.5 13.5 %collective-permute-done.37 = f32[5,1024]{1,0:T(8,128)S(1)} collective-permute-done((f32[5,1024]{1,0:T(8,128)S(1)}, f32[5,1024]{1,0:T(8,128)S(1)}, u32[]{:S(2)}, u32[]{:S(2)}) %collective-permute-start.37) | collective-permute-done | bytes 20512 | tf_op jit(solution)/shard_map/ppermute | solution.py:22
  413.7 3.0 slice.829
  416.7 2.9 copy.80
  421.0 15.5 %collective-permute-start.42 = (f32[5,1024]{1,0:T(8,128)S(1)}, f32[5,1024]{1,0:T(8,128)}, u32[]{:S(2)}, u32[]{:S(2)}) collective-permute-start(f32[5,1024]{1,0:T(8,128)S(1)} %add.311), channel_id=1, source_target_pairs={{0,2},{1,3},{2,0},{3,1},{4,6},{5,7},{6,4},{7,5},{8,10},{9,11},{10,... | collective-permute-start | bytes 61448 | tf_op jit(solution)/shard_map/ppermute | solution.py:17
  446.0 6.5 %collective-permute-done.50 = bf16[512,512]{0,1:T(8,128)(2,1)S(1)} collective-permute-done((bf16[512,512]{0,1:T(8,128)(2,1)S(1)}, bf16[512,512]{0,1:T(8,128)(2,1)S(1)}, u32[]{:S(2)}, u32[]{:S(2)}) %collective-permute-start.50) | collective-permute-done | bytes 524320 | tf_op jit(solution)/shard_map/ppermute | solution.py:17
  452.5 3.7 collective-permute-start.46
  461.2 4.3 collective-permute-done.46
  472.2 4.3 collective-permute-start.51
  477.1 2.8 pad_maximum_fusion.8
  483.8 5.5 %collective-permute-done.53 = bf16[128,1024]{0,1:T(8,128)(2,1)S(1)} collective-permute-done((bf16[128,1024]{0,1:T(8,128)(2,1)S(1)}, bf16[128,1024]{0,1:T(8,128)(2,1)S(1)}, u32[]{:S(2)}, u32[]{:S(2)}) %collective-permute-start.53) | collective-permute-done | bytes 262176 | tf_op jit(solution)/shard_map/ppermute | solution.py:22
  489.2 6.1 %collective-permute-done.52 = bf16[128,1024]{0,1:T(8,128)(2,1)S(1)} collective-permute-done((bf16[128,1024]{0,1:T(8,128)(2,1)S(1)}, bf16[128,1024]{0,1:T(8,128)(2,1)S(1)}, u32[]{:S(2)}, u32[]{:S(2)}) %collective-permute-start.52) | collective-permute-done | bytes 262176 | tf_op jit(solution)/shard_map/ppermute | solution.py:22
  (525 shorter events, 178.9 us)
Async XLA Ops:
  7.2 138.5 %all-gather.2.cloned.1.call-start = ((), (), s32[]{:S(2)}) async-start(), calls=%async_computation | async-start | bytes 4423680 | tf_op jit(solution)/shard_map/all_gather | solution.py:263
  10.3 20.0 %collective-permute-start.4 = (bf16[128,1024]{1,0:T(8,128)(2,1)}, bf16[128,1024]{1,0:T(8,128)(2,1)S(1)}, u32[]{:S(2)}, u32[]{:S(2)}) collective-permute-start(bf16[128,1024]{1,0:T(8,128)(2,1)} %get-tuple-element.245), channel_id=1, source_target_pairs={{0,4},{4,0},{8,12},{12,8},{16,20},{20,16},{24,28},{28,24},{1,5},{5... | collective-permute-start | bytes 786440 | tf_op jit(solution)/shard_map/ppermute | solution.py:17
  13.3 15.5 %collective-permute-start.1 = (bf16[128,1024]{1,0:T(8,128)(2,1)}, bf16[128,1024]{1,0:T(8,128)(2,1)S(1)}, u32[]{:S(2)}, u32[]{:S(2)}) collective-permute-start(bf16[128,1024]{1,0:T(8,128)(2,1)} %get-tuple-element.245), channel_id=1, source_target_pairs={{0,8},{4,12},{8,16},{12,20},{16,24},{20,28},{24,0},{28,4},{1,9},{5... | collective-permute-start | bytes 786440 | tf_op jit(solution)/shard_map/ppermute | solution.py:22
  31.3 33.5 %collective-permute-start.10 = (bf16[256,1024]{1,0:T(8,128)(2,1)}, bf16[256,1024]{1,0:T(8,128)(2,1)}, u32[]{:S(2)}, u32[]{:S(2)}) collective-permute-start(bf16[256,1024]{1,0:T(8,128)(2,1)} %pad_maximum_fusion.19), channel_id=1, source_target_pairs={{0,2},{1,3},{2,0},{3,1},{4,6},{5,7},{6,4},{7,5},{8,10},{9,11},{10,... | collective-permute-start | bytes 1572872 | tf_op jit(solution)/shard_map/ppermute | solution.py:17
  34.2 76.9 %collective-permute-start.20 = (bf16[512,1024]{1,0:T(8,128)(2,1)S(1)}, bf16[512,1024]{1,0:T(8,128)(2,1)}, u32[]{:S(2)}, u32[]{:S(2)}) collective-permute-start(bf16[512,1024]{1,0:T(8,128)(2,1)S(1)} %fusion.35.refs_2_), channel_id=1, source_target_pairs={{0,1},{1,0},{2,3},{3,2},{4,5},{5,4},{6,7},{7,6},{8,9},{9,8},{10,11... | collective-permute-start | bytes 3145736 | tf_op jit(solution)/shard_map/ppermute | solution.py:17
  34.6 10.2 %collective-permute-start.2 = (bf16[128,1024]{1,0:T(8,128)(2,1)S(1)}, bf16[128,1024]{1,0:T(8,128)(2,1)S(1)}, u32[]{:S(2)}, u32[]{:S(2)}) collective-permute-start(bf16[128,1024]{1,0:T(8,128)(2,1)S(1)} %collective-permute-done.1), channel_id=1, source_target_pairs={{0,8},{4,12},{8,16},{12,20},{16,24},{20,28},{24,0},{28,4},{1,9},{5... | collective-permute-start | bytes 786440 | tf_op jit(solution)/shard_map/ppermute | solution.py:22
  38.2 10.1 %collective-permute-start.5 = (bf16[128,1024]{1,0:T(8,128)(2,1)S(1)}, bf16[128,1024]{1,0:T(8,128)(2,1)S(1)}, u32[]{:S(2)}, u32[]{:S(2)}) collective-permute-start(bf16[128,1024]{1,0:T(8,128)(2,1)S(1)} %collective-permute-done.1), channel_id=1, source_target_pairs={{0,4},{4,0},{8,12},{12,8},{16,20},{20,16},{24,28},{28,24},{1,5},{5... | collective-permute-start | bytes 786440 | tf_op jit(solution)/shard_map/ppermute | solution.py:17
  49.1 23.7 %collective-permute-start.11 = (bf16[256,1024]{1,0:T(8,128)(2,1)}, bf16[256,1024]{1,0:T(8,128)(2,1)}, u32[]{:S(2)}, u32[]{:S(2)}) collective-permute-start(bf16[256,1024]{1,0:T(8,128)(2,1)} %pad_maximum_fusion.20), channel_id=1, source_target_pairs={{0,2},{1,3},{2,0},{3,1},{4,6},{5,7},{6,4},{7,5},{8,10},{9,11},{10,... | collective-permute-start | bytes 1572872 | tf_op jit(solution)/shard_map/ppermute | solution.py:17
  50.5 10.0 %collective-permute-start.6 = (bf16[128,1024]{1,0:T(8,128)(2,1)S(1)}, bf16[128,1024]{1,0:T(8,128)(2,1)S(1)}, u32[]{:S(2)}, u32[]{:S(2)}) collective-permute-start(bf16[128,1024]{1,0:T(8,128)(2,1)S(1)} %collective-permute-done.2), channel_id=1, source_target_pairs={{0,4},{4,0},{8,12},{12,8},{16,20},{20,16},{24,28},{28,24},{1,5},{5... | collective-permute-start | bytes 786440 | tf_op jit(solution)/shard_map/ppermute | solution.py:17
  60.5 12.8 %collective-permute-start.9 = (bf16[128,1536]{1,0:T(8,128)(2,1)S(1)}, bf16[128,1536]{1,0:T(8,128)(2,1)S(1)}, u32[]{:S(2)}, u32[]{:S(2)}) collective-permute-start(bf16[128,1536]{1,0:T(8,128)(2,1)S(1)} %pad_maximum_fusion.23.refs_4_), channel_id=1, source_target_pairs={{0,8},{4,12},{8,16},{12,20},{16,24},{20,28},{24,0},{28,4},{1,9},{5... | collective-permute-start | bytes 1179656 | tf_op jit(solution)/shard_map/ppermute | solution.py:22
  64.8 14.9 %collective-permute-start.12 = (bf16[256,1024]{1,0:T(8,128)(2,1)S(1)}, bf16[256,1024]{1,0:T(8,128)(2,1)S(1)}, u32[]{:S(2)}, u32[]{:S(2)}) collective-permute-start(bf16[256,1024]{1,0:T(8,128)(2,1)S(1)} %pad_maximum_fusion.21), channel_id=1, source_target_pairs={{0,2},{1,3},{2,0},{3,1},{4,6},{5,7},{6,4},{7,5},{8,10},{9,11},{10,... | collective-permute-start | bytes 1572872 | tf_op jit(solution)/shard_map/ppermute | solution.py:17
  68.6 25.8 %collective-permute-start.13 = (bf16[272,1024]{1,0:T(8,128)(2,1)S(1)}, bf16[272,1024]{1,0:T(8,128)(2,1)S(1)}, u32[]{:S(2)}, u32[]{:S(2)}) collective-permute-start(bf16[272,1024]{1,0:T(8,128)(2,1)S(1)} %pad_maximum_fusion.14), channel_id=1, source_target_pairs={{0,2},{1,3},{2,0},{3,1},{4,6},{5,7},{6,4},{7,5},{8,10},{9,11},{10,... | collective-permute-start | bytes 1671176 | tf_op jit(solution)/shard_map/ppermute | solution.py:17
  72.8 9.8 %collective-permute-start.15 = (bf16[128,1536]{1,0:T(8,128)(2,1)S(1)}, bf16[128,1536]{1,0:T(8,128)(2,1)S(1)}, u32[]{:S(2)}, u32[]{:S(2)}) collective-permute-start(bf16[128,1536]{1,0:T(8,128)(2,1)S(1)} %pad_maximum_fusion.23.refs_4_), channel_id=1, source_target_pairs={{0,4},{4,0},{8,12},{12,8},{16,20},{20,16},{24,28},{28,24},{1,5},{5... | collective-permute-start | bytes 1179656 | tf_op jit(solution)/shard_map/ppermute | solution.py:17
  73.3 21.1 %collective-permute-start.14 = (bf16[128,1536]{1,0:T(8,128)(2,1)S(1)}, bf16[128,1536]{1,0:T(8,128)(2,1)}, u32[]{:S(2)}, u32[]{:S(2)}) collective-permute-start(bf16[128,1536]{1,0:T(8,128)(2,1)S(1)} %collective-permute-done.9.refs_5_), channel_id=1, source_target_pairs={{0,8},{4,12},{8,16},{12,20},{16,24},{20,28},{24,0},{28,4},{1,9},{5... | collective-permute-start | bytes 1179656 | tf_op jit(solution)/shard_map/ppermute | solution.py:22
  79.7 17.9 %collective-permute-start.8 = (bf16[1040,1024]{1,0:T(8,128)(2,1)S(1)}, bf16[1040,1024]{1,0:T(8,128)(2,1)S(1)}, u32[]{:S(2)}, u32[]{:S(2)}) collective-permute-start(bf16[1040,1024]{1,0:T(8,128)(2,1)S(1)} %copy-done.94), channel_id=1, source_target_pairs={{0,1},{1,0},{2,3},{3,2},{4,5},{5,4},{6,7},{7,6},{8,9},{9,8},{10,11... | collective-permute-start | bytes 6389768 | tf_op jit(solution)/shard_map/ppermute | solution.py:17
  108.1 40.6 %collective-permute-start.19 = (bf16[512,1024]{1,0:T(8,128)(2,1)S(1)}, bf16[512,1024]{1,0:T(8,128)(2,1)S(1)}, u32[]{:S(2)}, u32[]{:S(2)}) collective-permute-start(bf16[512,1024]{1,0:T(8,128)(2,1)S(1)} %multiply_convert_fusion.1.refs_0_), channel_id=1, source_target_pairs={{0,1},{1,0},{2,3},{3,2},{4,5},{5,4},{6,7},{7,6},{8,9},{9,8},{10,11... | collective-permute-start | bytes 3145736 | tf_op jit(solution)/shard_map/ppermute | solution.py:17
  108.8 20.1 %collective-permute-start.22 = (bf16[128,1536]{1,0:T(8,128)(2,1)S(1)}, bf16[128,1536]{1,0:T(8,128)(2,1)S(1)}, u32[]{:S(2)}, u32[]{:S(2)}) collective-permute-start(bf16[128,1536]{1,0:T(8,128)(2,1)S(1)} %collective-permute-done.9.refs_5_), channel_id=1, source_target_pairs={{0,4},{4,0},{8,12},{12,8},{16,20},{20,16},{24,28},{28,24},{1,5},{5... | collective-permute-start | bytes 1179656 | tf_op jit(solution)/shard_map/ppermute | solution.py:17
  110.3 21.2 %collective-permute-start.21 = (bf16[128,1536]{1,0:T(8,128)(2,1)}, bf16[128,1536]{1,0:T(8,128)(2,1)}, u32[]{:S(2)}, u32[]{:S(2)}) collective-permute-start(bf16[128,1536]{1,0:T(8,128)(2,1)} %collective-permute-done.14.refs_6_), channel_id=1, source_target_pairs={{0,8},{4,12},{8,16},{12,20},{16,24},{20,28},{24,0},{28,4},{1,9},{5... | collective-permute-start | bytes 1179656 | tf_op jit(solution)/shard_map/ppermute | solution.py:22
  110.6 54.8 %collective-permute-start.18 = (bf16[512,1024]{1,0:T(8,128)(2,1)S(1)}, bf16[512,1024]{1,0:T(8,128)(2,1)}, u32[]{:S(2)}, u32[]{:S(2)}) collective-permute-start(bf16[512,1024]{1,0:T(8,128)(2,1)S(1)} %fusion.35.refs_2_), channel_id=1, source_target_pairs={{0,2},{1,3},{2,0},{3,1},{4,6},{5,7},{6,4},{7,5},{8,10},{9,11},{10,... | collective-permute-start | bytes 3145736 | tf_op jit(solution)/shard_map/ppermute | solution.py:17
  111.2 54.2 %collective-permute-start.17 = (bf16[512,1024]{1,0:T(8,128)(2,1)S(1)}, bf16[512,1024]{1,0:T(8,128)(2,1)}, u32[]{:S(2)}, u32[]{:S(2)}) collective-permute-start(bf16[512,1024]{1,0:T(8,128)(2,1)S(1)} %multiply_convert_fusion.1.refs_0_), channel_id=1, source_target_pairs={{0,2},{1,3},{2,0},{3,1},{4,6},{5,7},{6,4},{7,5},{8,10},{9,11},{10,... | collective-permute-start | bytes 3145736 | tf_op jit(solution)/shard_map/ppermute | solution.py:17
  129.6 16.1 %collective-permute-start.23 = (bf16[128,1536]{1,0:T(8,128)(2,1)}, bf16[128,1536]{1,0:T(8,128)(2,1)}, u32[]{:S(2)}, u32[]{:S(2)}) collective-permute-start(bf16[128,1536]{1,0:T(8,128)(2,1)} %collective-permute-done.14.refs_6_), channel_id=1, source_target_pairs={{0,4},{4,0},{8,12},{12,8},{16,20},{20,16},{24,28},{28,24},{1,5},{5... | collective-permute-start | bytes 1179656 | tf_op jit(solution)/shard_map/ppermute | solution.py:17
  131.5 17.2 %collective-permute-start.24 = (bf16[128,1536]{1,0:T(8,128)(2,1)}, bf16[128,1536]{1,0:T(8,128)(2,1)}, u32[]{:S(2)}, u32[]{:S(2)}) collective-permute-start(bf16[128,1536]{1,0:T(8,128)(2,1)} %collective-permute-done.21.refs_7_), channel_id=1, source_target_pairs={{0,4},{4,0},{8,12},{12,8},{16,20},{20,16},{24,28},{28,24},{1,5},{5... | collective-permute-start | bytes 1179656 | tf_op jit(solution)/shard_map/ppermute | solution.py:17
  227.6 10.9 %collective-permute-start.27 = (bf16[512,2048]{1,0:T(8,128)(2,1)}, bf16[512,2048]{1,0:T(8,128)(2,1)}, u32[]{:S(2)}, u32[]{:S(2)}) collective-permute-start(bf16[512,2048]{1,0:T(8,128)(2,1)} %slice.651), channel_id=1, source_target_pairs={{0,1},{1,0},{2,3},{3,2},{4,5},{5,4},{6,7},{7,6},{8,9},{9,8},{10,11... | collective-permute-start | bytes 6291464 | tf_op jit(solution)/shard_map/ppermute | solution.py:17
  230.1 36.7 %collective-permute-start.32 = (bf16[512,1536]{1,0:T(8,128)(2,1)S(1)}, bf16[512,1536]{1,0:T(8,128)(2,1)S(1)}, u32[]{:S(2)}, u32[]{:S(2)}) collective-permute-start(bf16[512,1536]{1,0:T(8,128)(2,1)S(1)} %copy-done.57), channel_id=1, source_target_pairs={{0,4},{4,0},{8,12},{12,8},{16,20},{20,16},{24,28},{28,24},{1,5},{5... | collective-permute-start | bytes 4718600 | tf_op jit(solution)/shard_map/ppermute | solution.py:17
  270.4 25.0 %collective-permute-start.30 = (bf16[256,1024]{1,0:T(8,128)(2,1)}, bf16[256,1024]{1,0:T(8,128)(2,1)}, u32[]{:S(2)}, u32[]{:S(2)}) collective-permute-start(bf16[256,1024]{1,0:T(8,128)(2,1)} %get-tuple-element.207), channel_id=1, source_target_pairs={{0,2},{1,3},{2,0},{3,1},{4,6},{5,7},{6,4},{7,5},{8,10},{9,11},{10,... | collective-permute-start | bytes 1572872 | tf_op jit(solution)/shard_map/ppermute | solution.py:17
  272.1 23.3 %collective-permute-start.29 = (bf16[256,1024]{1,0:T(8,128)(2,1)}, bf16[256,1024]{1,0:T(8,128)(2,1)}, u32[]{:S(2)}, u32[]{:S(2)}) collective-permute-start(bf16[256,1024]{1,0:T(8,128)(2,1)} %get-tuple-element.208), channel_id=1, source_target_pairs={{0,2},{1,3},{2,0},{3,1},{4,6},{5,7},{6,4},{7,5},{8,10},{9,11},{10,... | collective-permute-start | bytes 1572872 | tf_op jit(solution)/shard_map/ppermute | solution.py:17
  274.0 33.5 %collective-permute-start.28 = (bf16[512,2048]{1,0:T(8,128)(2,1)}, bf16[512,2048]{1,0:T(8,128)(2,1)}, u32[]{:S(2)}, u32[]{:S(2)}) collective-permute-start(bf16[512,2048]{1,0:T(8,128)(2,1)} %slice.653), channel_id=1, source_target_pairs={{0,1},{1,0},{2,3},{3,2},{4,5},{5,4},{6,7},{7,6},{8,9},{9,8},{10,11... | collective-permute-start | bytes 6291464 | tf_op jit(solution)/shard_map/ppermute | solution.py:17
  277.7 39.7 %collective-permute-start.33 = (bf16[2,128,1536]{1,2,0:T(8,128)(2,1)S(1)}, bf16[2,128,1536]{1,2,0:T(8,128)(2,1)S(1)}, u32[]{:S(2)}, u32[]{:S(2)}) collective-permute-start(bf16[2,128,1536]{1,2,0:T(8,128)(2,1)S(1)} %copy.76), channel_id=1, source_target_pairs={{0,16},{4,20},{8,24},{12,28},{16,0},{20,4},{24,8},{28,12},{1,17},{... | collective-permute-start | bytes 2359304 | tf_op jit(solution)/shard_map/ppermute | solution.py:22
  295.5 34.9 %collective-permute-start.31 = (bf16[512,1024]{1,0:T(8,128)(2,1)S(1)}, bf16[512,1024]{1,0:T(8,128)(2,1)S(1)}, u32[]{:S(2)}, u32[]{:S(2)}) collective-permute-start(bf16[512,1024]{1,0:T(8,128)(2,1)S(1)} %copy-done.62), channel_id=1, source_target_pairs={{0,2},{1,3},{2,0},{3,1},{4,6},{5,7},{6,4},{7,5},{8,10},{9,11},{10,... | collective-permute-start | bytes 3145736 | tf_op jit(solution)/shard_map/ppermute | solution.py:17
  307.2 50.5 %collective-permute-start.44 = (bf16[512,1920]{1,0:T(8,128)(2,1)S(1)}, bf16[512,1920]{1,0:T(8,128)(2,1)S(1)}, u32[]{:S(2)}, u32[]{:S(2)}) collective-permute-start(bf16[512,1920]{1,0:T(8,128)(2,1)S(1)} %pad_maximum_fusion.5), channel_id=1, source_target_pairs={{0,4},{4,0},{8,12},{12,8},{16,20},{20,16},{24,28},{28,24},{1,5},{5... | collective-permute-start | bytes 5898248 | tf_op jit(solution)/shard_map/ppermute | solution.py:17
  317.7 19.1 %collective-permute-start.35 = (bf16[1,128,1536]{1,2,0:T(8,128)(2,1)S(1)}, bf16[1,128,1536]{1,2,0:T(8,128)(2,1)S(1)}, u32[]{:S(2)}, u32[]{:S(2)}) collective-permute-start(bf16[1,128,1536]{1,2,0:T(8,128)(2,1)S(1)} %slice.1227), channel_id=1, source_target_pairs={{0,24},{4,28},{8,0},{12,4},{16,8},{20,12},{24,16},{28,20},{1,25},{... | collective-permute-start | bytes 1179656 | tf_op jit(solution)/shard_map/ppermute | solution.py:22
  324.2 10.5 %collective-permute-start.34 = (f32[4,2,256]{2,1,0:T(2,128)S(1)}, f32[4,2,256]{2,1,0:T(2,128)S(1)}, u32[]{:S(2)}, u32[]{:S(2)}) collective-permute-start(f32[4,2,256]{2,1,0:T(2,128)S(1)} %pad_maximum_fusion.27), channel_id=1, source_target_pairs={{1,0},{2,1},{3,2},{4,3},{5,4},{6,5},{7,6},{8,7},{9,8},{10,9},{11,1... | collective-permute-start | bytes 24584 | tf_op jit(solution)/shard_map/ppermute | solution.py:28
  327.4 36.4 %collective-permute-start.39 = (bf16[1024,1024]{0,1:T(8,128)(2,1)S(1)}, bf16[1024,1024]{0,1:T(8,128)(2,1)}, u32[]{:S(2)}, u32[]{:S(2)}) collective-permute-start(bf16[1024,1024]{0,1:T(8,128)(2,1)S(1)} %pad_maximum_fusion.1), channel_id=1, source_target_pairs={{0,1},{1,0},{2,3},{3,2},{4,5},{5,4},{6,7},{7,6},{8,9},{9,8},{10,11... | collective-permute-start | bytes 6291464 | tf_op jit(solution)/shard_map/ppermute | solution.py:17
  340.3 44.6 %collective-permute-start.47 = (bf16[1024,1024]{0,1:T(8,128)(2,1)}, bf16[1024,1024]{0,1:T(8,128)(2,1)}, u32[]{:S(2)}, u32[]{:S(2)}) collective-permute-start(bf16[1024,1024]{0,1:T(8,128)(2,1)} %convolution_convert_fusion.3), channel_id=1, source_target_pairs={{0,1},{1,0},{2,3},{3,2},{4,5},{5,4},{6,7},{7,6},{8,9},{9,8},{10,11... | collective-permute-start | bytes 6291464 | tf_op jit(solution)/shard_map/ppermute | solution.py:17
  353.8 38.2 %collective-permute-start.36 = (f32[5,1024]{1,0:T(8,128)S(1)}, f32[5,1024]{1,0:T(8,128)S(1)}, u32[]{:S(2)}, u32[]{:S(2)}) collective-permute-start(f32[5,1024]{1,0:T(8,128)S(1)} %pad_maximum_fusion.26), channel_id=1, source_target_pairs={{0,1},{1,0},{2,3},{3,2},{4,5},{5,4},{6,7},{7,6},{8,9},{9,8},{10,11... | collective-permute-start | bytes 61448 | tf_op jit(solution)/shard_map/ppermute | solution.py:17
  363.0 76.1 %collective-permute-start.45 = (bf16[2,128,1920]{1,2,0:T(8,128)(2,1)}, bf16[2,128,1920]{1,2,0:T(8,128)(2,1)}, u32[]{:S(2)}, u32[]{:S(2)}) collective-permute-start(bf16[2,128,1920]{1,2,0:T(8,128)(2,1)} %copy.79), channel_id=1, source_target_pairs={{0,16},{4,20},{8,24},{12,28},{16,0},{20,4},{24,8},{28,12},{1,17},{... | collective-permute-start | bytes 2949128 | tf_op jit(solution)/shard_map/ppermute | solution.py:22
  369.3 50.3 %collective-permute-start.40 = (bf16[1024,512]{0,1:T(8,128)(2,1)}, bf16[1024,512]{0,1:T(8,128)(2,1)}, u32[]{:S(2)}, u32[]{:S(2)}) collective-permute-start(bf16[1024,512]{0,1:T(8,128)(2,1)} %pad_maximum_fusion.12), channel_id=1, source_target_pairs={{0,4},{4,0},{8,12},{12,8},{16,20},{20,16},{24,28},{28,24},{1,5},{5... | collective-permute-start | bytes 3145736 | tf_op jit(solution)/shard_map/ppermute | solution.py:17
  390.7 50.5 %collective-permute-start.48 = (bf16[1024,512]{0,1:T(8,128)(2,1)}, bf16[1024,512]{0,1:T(8,128)(2,1)}, u32[]{:S(2)}, u32[]{:S(2)}) collective-permute-start(bf16[1024,512]{0,1:T(8,128)(2,1)} %slice.1222), channel_id=1, source_target_pairs={{0,2},{1,3},{2,0},{3,1},{4,6},{5,7},{6,4},{7,5},{8,10},{9,11},{10,... | collective-permute-start | bytes 3145736 | tf_op jit(solution)/shard_map/ppermute | solution.py:17
  392.0 18.1 %collective-permute-start.37 = (f32[5,1024]{1,0:T(8,128)S(1)}, f32[5,1024]{1,0:T(8,128)S(1)}, u32[]{:S(2)}, u32[]{:S(2)}) collective-permute-start(f32[5,1024]{1,0:T(8,128)S(1)} %fusion.202), channel_id=1, source_target_pairs={{0,16},{4,20},{8,24},{12,28},{16,0},{20,4},{24,8},{28,12},{1,17},{... | collective-permute-start | bytes 61448 | tf_op jit(solution)/shard_map/ppermute | solution.py:22
  419.6 48.4 %collective-permute-start.43 = (f32[5,1024]{1,0:T(8,128)S(1)}, f32[5,1024]{1,0:T(8,128)S(1)}, u32[]{:S(2)}, u32[]{:S(2)}) collective-permute-start(f32[5,1024]{1,0:T(8,128)S(1)} %add.311), channel_id=1, source_target_pairs={{0,6},{1,7},{2,4},{3,5},{4,2},{5,3},{6,0},{7,1},{8,14},{9,15},{10,... | collective-permute-start | bytes 61448 | tf_op jit(solution)/shard_map/ppermute | solution.py:34
  421.0 47.0 %collective-permute-start.42 = (f32[5,1024]{1,0:T(8,128)S(1)}, f32[5,1024]{1,0:T(8,128)}, u32[]{:S(2)}, u32[]{:S(2)}) collective-permute-start(f32[5,1024]{1,0:T(8,128)S(1)} %add.311), channel_id=1, source_target_pairs={{0,2},{1,3},{2,0},{3,1},{4,6},{5,7},{6,4},{7,5},{8,10},{9,11},{10,... | collective-permute-start | bytes 61448 | tf_op jit(solution)/shard_map/ppermute | solution.py:17
  436.5 32.2 %collective-permute-start.41 = (f32[5,1024]{1,0:T(8,128)S(1)}, f32[5,1024]{1,0:T(8,128)}, u32[]{:S(2)}, u32[]{:S(2)}) collective-permute-start(f32[5,1024]{1,0:T(8,128)S(1)} %add.311), channel_id=1, source_target_pairs={{0,4},{4,0},{8,12},{12,8},{16,20},{20,16},{24,28},{28,24},{1,5},{5... | collective-permute-start | bytes 61448 | tf_op jit(solution)/shard_map/ppermute | solution.py:17
  439.1 13.4 %collective-permute-start.50 = (bf16[512,512]{0,1:T(8,128)(2,1)S(1)}, bf16[512,512]{0,1:T(8,128)(2,1)S(1)}, u32[]{:S(2)}, u32[]{:S(2)}) collective-permute-start(bf16[512,512]{0,1:T(8,128)(2,1)S(1)} %fusion.80), channel_id=1, source_target_pairs={{0,2},{1,3},{2,0},{3,1},{4,6},{5,7},{6,4},{7,5},{8,10},{9,11},{10,... | collective-permute-start | bytes 1572872 | tf_op jit(solution)/shard_map/ppermute | solution.py:17
  443.5 14.0 %collective-permute-start.49 = (bf16[512,512]{0,1:T(8,128)(2,1)S(1)}, bf16[512,512]{0,1:T(8,128)(2,1)S(1)}, u32[]{:S(2)}, u32[]{:S(2)}) collective-permute-start(bf16[512,512]{0,1:T(8,128)(2,1)S(1)} %slice.1225), channel_id=1, source_target_pairs={{0,4},{4,0},{8,12},{12,8},{16,20},{20,16},{24,28},{28,24},{1,5},{5... | collective-permute-start | bytes 1572872 | tf_op jit(solution)/shard_map/ppermute | solution.py:17
  452.5 13.0 %collective-permute-start.46 = (bf16[1,128,1920]{1,2,0:T(8,128)(2,1)}, bf16[1,128,1920]{1,2,0:T(8,128)(2,1)}, u32[]{:S(2)}, u32[]{:S(2)}) collective-permute-start(bf16[1,128,1920]{1,2,0:T(8,128)(2,1)} %slice.1226), channel_id=1, source_target_pairs={{0,24},{4,28},{8,0},{12,4},{16,8},{20,12},{24,16},{28,20},{1,25},{... | collective-permute-start | bytes 1474568 | tf_op jit(solution)/shard_map/ppermute | solution.py:22
  472.2 11.6 %collective-permute-start.51 = (bf16[128,1024]{0,1:T(8,128)(2,1)S(1)}, bf16[128,1024]{0,1:T(8,128)(2,1)S(1)}, u32[]{:S(2)}, u32[]{:S(2)}) collective-permute-start(bf16[128,1024]{0,1:T(8,128)(2,1)S(1)} %get-tuple-element.211), channel_id=1, source_target_pairs={{0,24},{4,28},{8,0},{12,4},{16,8},{20,12},{24,16},{28,20},{1,25},{... | collective-permute-start | bytes 786440 | tf_op jit(solution)/shard_map/ppermute | solution.py:22
  476.5 12.7 %collective-permute-start.53 = (bf16[128,1024]{0,1:T(8,128)(2,1)S(1)}, bf16[128,1024]{0,1:T(8,128)(2,1)S(1)}, u32[]{:S(2)}, u32[]{:S(2)}) collective-permute-start(bf16[128,1024]{0,1:T(8,128)(2,1)S(1)} %get-tuple-element.212), channel_id=1, source_target_pairs={{0,8},{4,12},{8,16},{12,20},{16,24},{20,28},{24,0},{28,4},{1,9},{5... | collective-permute-start | bytes 786440 | tf_op jit(solution)/shard_map/ppermute | solution.py:22
  476.5 18.9 %collective-permute-start.52 = (bf16[128,1024]{0,1:T(8,128)(2,1)S(1)}, bf16[128,1024]{0,1:T(8,128)(2,1)S(1)}, u32[]{:S(2)}, u32[]{:S(2)}) collective-permute-start(bf16[128,1024]{0,1:T(8,128)(2,1)S(1)} %get-tuple-element.213), channel_id=1, source_target_pairs={{0,16},{4,20},{8,24},{12,28},{16,0},{20,4},{24,8},{28,12},{1,17},{... | collective-permute-start | bytes 786440 | tf_op jit(solution)/shard_map/ppermute | solution.py:22
  (138 other events, 1088.5 us)
Sparse Core Ops, SparseCore 0:
  60.6 85.0 all-gather.1

commit v2 on v1

v2 whole, which is shorter than its diff:
```python
import jax
import jax.numpy as jnp
from jax import lax
from jax.experimental import pallas as pl
from jax.experimental.pallas import tpu as pltpu
from jax.sharding import PartitionSpec as P

epsilon = 1e-05
HALO = 16
LONG = 8
BF = jnp.bfloat16
F32 = jnp.float32


def swap(value, axis, bit):
    peers = lax.axis_size(axis)
    return lax.ppermute(value, axis, [(i, i ^ bit) for i in range(peers)])


def ring(value, axis, by):
    peers = lax.axis_size(axis)
    return lax.ppermute(value, axis, [(i, (i + by) % peers) for i in range(peers)])


def shift(value, by):
    peers = lax.axis_size("dp") * lax.axis_size("tensor")
    pairs = [(i, i + by) for i in range(peers) if 0 <= i + by < peers]
    return lax.ppermute(value, ("dp", "tensor"), pairs)


def cross(value):
    inner = lax.axis_size("tensor")
    peers = lax.axis_size("dp") * inner
    return lax.ppermute(value, ("dp", "tensor"), [(i, i ^ (inner + 2)) for i in range(peers)])


def nn(left, right):
    return jnp.dot(left, right, preferred_element_type=F32)


def tn(left, right):
    return lax.dot_general(left, right, (((0,), (0,)), ((), ())), preferred_element_type=F32)


def nt(left, right):
    return lax.dot_general(left, right, (((1,), (1,)), ((), ())), preferred_element_type=F32)


def normalize(values):
    scale_vec = lax.rsqrt(jnp.mean(values * values, axis=-1, keepdims=True) + epsilon)
    return (values * scale_vec, scale_vec)


def norm_back(d_normed, normed, scale_vec):
    return scale_vec * (d_normed - normed * jnp.mean(d_normed * normed, axis=-1, keepdims=True))


def after(value, *others):
    return lax.optimization_barrier((value,) + others)[0]


def reorder(values, perm):
    return nn(values, perm).astype(BF)


def reorder_f32(values, perm):
    high = lax.optimization_barrier(values.astype(BF))
    low = (values - high.astype(F32)).astype(BF)
    return nn(high, perm) + nn(low, perm)


def blocks_order():
    steps, me = lax.axis_size("dp") // 2, lax.axis_index("dp")
    index = jnp.arange(2 * steps, dtype=jnp.int32)
    order = ((me // 2 - index % steps) % steps) * 2 + ((me % 2) ^ (index // steps))
    inverse = ((index % 2) ^ (me % 2)) * steps + (me // 2 - index // 2) % steps
    return order, inverse


def long_gather(shard):
    whole = lax.all_gather(shard, "dp", axis=0)[blocks_order()[0]]
    return whole.reshape(-1, shard.shape[1])


def long_scatter(near, far):
    total = jnp.concatenate([near, far], axis=0)
    peers = lax.axis_size("dp")
    total = total.reshape(peers, total.shape[0] // peers, -1)[blocks_order()[1]].reshape(total.shape)
    return lax.psum_scatter(total, "dp", scatter_dimension=0, tiled=True).astype(F32)


def chain(shard):
    here = [shard]
    for _ in range(lax.axis_size("dp") // 2 - 1):
        here.append(ring(here[-1], "dp", 2))
    return here


def others(here):
    return [swap(piece, "dp", 1) for piece in here]


def ffn(hidden, cot, weights, before, kept, part, tile):
    slot_rows, width = hidden[0].shape
    rows = 2 * slot_rows
    size = weights.shape[1] // 3
    steps = rows // tile
    skip = part * steps
    wide = [2 * size, size] + ([] if before else [width, width])

    def kernel(*refs):
        slots, w_ref, refs = refs[:4], refs[4], refs[5:]
        if before:
            h_ref, g_ref = refs[-2:]
            refs = refs[:-2]
        else:
            h_ref, g_ref = refs[-2:]
        outs = refs[len(before) + len(kept) :]
        d_gu_ref, act_ref = outs[4:6]

        def at(slot):
            return pl.when(pl.program_id(0) // (steps // 2) == slot)

        for slot in (0, 1):

            @at(slot)
            def _(slot=slot):
                h_ref[...] = slots[slot][...]
                g_ref[...] = slots[2 + slot][...]

        gate_up = nn(h_ref[...], w_ref[:, : 2 * size])
        d_act = nn(g_ref[...], w_ref[:, 2 * size :])
        gate, up = gate_up[:, :size], gate_up[:, size:]
        sigma = 1.0 / (1.0 + jnp.exp(-gate))
        silu = gate * sigma
        act = (silu * up).astype(BF)
        act_ref[...] = act
        d_gu_ref[:, :size] = (d_act * up * (sigma * (1.0 + gate * (1.0 - sigma)))).astype(BF)
        d_gu_ref[:, size:] = (d_act * silu).astype(BF)
        sums = [nt(d_gu_ref[...], w_ref[:, : 2 * size]), nt(act, w_ref[:, 2 * size :])]
        for slot in (0, 1):

            @at(slot)
            def _(slot=slot):
                for i, value in enumerate(sums):
                    at_ref = outs[2 * slot + i]
                    if before:
                        value = value + refs[2 * slot + i][...]
                    at_ref[...] = value.astype(at_ref.dtype)

    whole = pl.BlockSpec(memory_space=pl.ANY)
    near = pl.BlockSpec((tile, width), lambda i: (jnp.minimum(i, steps // 2 - 1), 0))
    far = pl.BlockSpec((tile, width), lambda i: (jnp.maximum(i - steps // 2, 0), 0))
    kind = BF if before else F32
    aliased = 5 + len(before)
    return pl.pallas_call(
        kernel,
        grid=(steps,),
        in_specs=[near, far] * 2
        + [pl.BlockSpec(weights.shape, lambda i: (0, 0))]
        + [near, near, far, far][: len(before)]
        + [whole] * len(kept),
        out_specs=[near, near, far, far] + [pl.BlockSpec((tile, n), lambda i: (i + skip, 0)) for n in wide],
        out_shape=[jax.ShapeDtypeStruct((slot_rows, width), kind)] * 4
        + [jax.ShapeDtypeStruct((2 * rows, n), BF) for n in wide],
        scratch_shapes=[pltpu.VMEM((tile, width), BF)] * (2 if before else 0),
        input_output_aliases={aliased + i: 4 + i for i in range(len(kept))},
        compiler_params=pltpu.CompilerParams(vmem_limit_bytes=48 << 20),
        cost_estimate=pl.CostEstimate(
            flops=12 * rows * width * size,
            bytes_accessed=rows * width * 12 + width * size * 6,
            transcendentals=rows * size,
        ),
    )(*hidden, *cot, weights, *before, *kept)


def by_xor(groups, me):
    one = [jnp.where((me & 1) == 1, groups[i ^ 1], groups[i]) for i in range(4)]
    return [jnp.where((me & 2) == 2, one[i ^ 2], one[i]) for i in range(4)]


def body(
    tokens_in,
    doc_ids,
    gain_mixer,
    in_weight,
    conv_weight,
    out_weight,
    gain_ffn,
    gate_up_weight,
    down_weight,
    cotangent,
):
    rows, width = tokens_in.shape
    dp_count = lax.axis_size("dp")
    block = width // dp_count
    channels = in_weight.shape[2]
    units = gate_up_weight.shape[2]
    me_t = lax.axis_index("tensor")
    deep = dp_count // 2
    half = width // 2
    long = deep > LONG

    tail = tokens_in[rows - HALO :]
    linked = (doc_ids[(me_t + 1) * rows - 2] == doc_ids[(me_t + 1) * rows - 1]).astype(BF)
    tail = tail * jnp.ones((HALO, 1), BF).at[HALO - 2, 0].set(linked)
    halo = shift(tail, 1)

    packed = jnp.concatenate(
        [in_weight[:, 0], in_weight[:, 2], in_weight[:, 1], out_weight.T], axis=1
    )
    taps_rows = jnp.zeros((HALO, 4 * channels), BF).at[:3, :channels].set(conv_weight)
    cut = units // 2 // 128 * 128
    bounds = [(0, cut), (cut, units)]


    def gather_block(lo, hi, *earlier):
        gate_up, down = lax.optimization_barrier((gate_up_weight, down_weight) + earlier)[:2]
        shard = jnp.concatenate([gate_up[:, 0, lo:hi], gate_up[:, 1, lo:hi], down[lo:hi].T], axis=1)
        return lax.all_gather(shard, "dp", axis=0, tiled=True)

    cot_y = swap(after(cotangent, halo), "tensor", 2)
    if long:
        whole = jnp.concatenate([long_gather(packed), taps_rows], axis=0)
        whole_y = swap(whole, "tensor", 2)
        here = [packed] * 3
    else:
        here = chain(packed)
        across = others(here)
        pairs = [jnp.concatenate(pair, axis=0) for pair in zip(here, across)]
        pairs[-1] = jnp.concatenate([here[-1], across[-1], taps_rows], axis=0)
        pairs[-1] = after(pairs[-1], cot_y)
        pairs_y = [swap(pair, "tensor", 2) for pair in pairs]
        whole = jnp.concatenate(here + across + [taps_rows], axis=0)
        whole_y = jnp.concatenate(
            [pair[:block] for pair in pairs_y]
            + [pair[block : 2 * block] for pair in pairs_y]
            + [pairs_y[-1][2 * block :]],
            axis=0,
        )
    blocks = [gather_block(*bounds[0]), gather_block(*bounds[1], here[2])]
    mix = [whole, swap(whole, "tensor", 1), whole_y, swap(whole_y, "tensor", 1)]

    lane = jnp.arange(width, dtype=jnp.int32)
    order = blocks_order()[0]
    source = jnp.repeat(order, block) * block + lane % block
    perm = (lane[:, None] == source[None, :]).astype(BF)
    perm_back = (source[:, None] == lane[None, :]).astype(BF)
    doc_ids = after(doc_ids, here[-1])
    last = doc_ids.shape[0]
    ids = jnp.concatenate([doc_ids[:1], doc_ids[:1], doc_ids, doc_ids[last - 1 :], doc_ids[last - 1 :]])
    ids = lax.dynamic_slice(ids, (me_t * rows,), (rows + 4,))
    one_all = (ids[1:] == ids[:-1]).astype(F32)[:, None]
    two_all = (ids[2:] == ids[:-2]).astype(F32)[:, None]
    keep_one, keep_two = one_all[1 : rows + 1], two_all[:rows]
    next_one, next_two = one_all[2 : rows + 2], two_all[2 : rows + 2]
    gain_one, gain_two = gain_mixer.astype(F32), gain_ffn.astype(F32)
    cot = cotangent
    extended = after(jnp.concatenate([halo, tokens_in], axis=0), here[1])
    normed_ext, scale_ext = normalize(extended.astype(F32))
    hidden_ext = reorder((normed_ext * gain_one).astype(BF), perm)
    scale_one = scale_ext[HALO:]
    hidden_one = hidden_ext[HALO:]
    tokens_f = tokens_in.astype(F32)

    saved = []
    mixed = 0.0
    for group in mix:
        taps = group[width : width + 3, :channels].astype(F32)
        projected = nn(hidden_ext, group[:width, : 3 * channels])
        b_part = projected[:, :channels]
        v_part = projected[:, channels : 2 * channels]
        c_part = projected[HALO:, 2 * channels :]
        bx = b_part * v_part
        bx0, bx1, bx2 = bx[HALO:], keep_one * bx[HALO - 1 : -1], keep_two * bx[HALO - 2 : -2]
        conv_out = taps[0] * bx0 + taps[1] * bx1 + taps[2] * bx2
        gated = (c_part * conv_out).astype(BF)
        mixed = mixed + nt(gated, group[:width, 3 * channels :])
        saved.append((b_part[HALO:], c_part, v_part[HALO:], bx0, bx1, bx2, conv_out, gated, taps))
    resid = tokens_f + reorder_f32(mixed, perm_back)
    normed_two, scale_two = normalize(resid)
    hidden_two = (normed_two * gain_two).astype(BF)
    hid_y = swap(hidden_two, "tensor", 2)
    tile = min(rows // 2, 256)

    def weight_grads(d_gu, act, *earlier):
        tokens, grads = lax.optimization_barrier((hid_all, cot_all) + earlier)[:2]
        grads = jnp.concatenate([tn(tokens, d_gu).astype(BF), tn(grads, act).astype(BF)], axis=1)
        return grads, lax.psum_scatter(grads, "dp", scatter_dimension=0, tiled=True)

    hid = [[hidden_two, swap(hidden_two, "tensor", 1)]]
    cots = [[cot, swap(cot, "tensor", 1)]]
    near = ffn(hid[0], cots[0], blocks[0], (), (), 0, tile)
    hid_y, cot_y = lax.optimization_barrier((hid_y, cot_y, near[0]))[:2]
    hid.append([hid_y, swap(hid_y, "tensor", 1)])
    cots.append([cot_y, swap(cot_y, "tensor", 1)])
    far = ffn(hid[1], cots[1], blocks[0], (), tuple(near[4:]), 1, tile)
    hid_all, cot_all = far[6:]
    parts_one, sums_one = weight_grads(*far[4:6], blocks[1])
    hid[1][0] = after(hid[1][0], parts_one)
    far_two = ffn(hid[1], cots[1], blocks[1], tuple(far[:4]), (), 1, tile)
    far_core = [swap(value, "tensor", 1) for value in far_two[2:4]]
    d_far, out_far = (
        (value.astype(F32) + got.astype(F32)).astype(BF) for value, got in zip(far_two, far_core)
    )
    d_y = swap(d_far, "tensor", 2)
    hid[0][0] = after(hid[0][0], far_core[0])
    near_two = ffn(hid[0], cots[0], blocks[1], tuple(near[:4]), tuple(far_two[4:]), 0, tile)
    parts_two, sums_two = weight_grads(*near_two[4:])

    near_core = [swap(value, "tensor", 1) for value in near_two[2:4]]
    d_hidden_two, out_own = (
        value.astype(F32) + got.astype(F32) for value, got in zip(near_two, near_core)
    )
    d_hidden_two = after(d_hidden_two + d_y.astype(F32), parts_two)
    d_resid = cot.astype(F32) + norm_back(d_hidden_two * gain_two, normed_two, scale_two)
    d_mix = reorder(d_resid.astype(BF), perm)

    d_gated = [nn(d_mix, group[:width, 3 * channels :]) for group in mix]
    d_conv = [back * keep[1] for back, keep in zip(d_gated, saved)]
    first = jnp.stack(by_xor([value[:2] for value in d_conv], me_t))
    following = shift(first, -1)
    following = by_xor([following[i] for i in range(4)], me_t)

    def add_z(sums):
        return sum(
            [sums[0]] + [ring(sums[k].astype(BF), "dp", -2 * k).astype(F32) for k in range(1, deep)]
        )

    d_cs = [(d_gated[r] * saved[r][6]).astype(BF) for r in range(4)]

    def sides(values, r):
        return jnp.concatenate([values[r], values[r + 2]], axis=1)

    gates = [saved[r][7] for r in range(4)]
    right = [
        jnp.concatenate(
            [tn(hidden_one, sides(d_cs, r)).astype(BF), tn(d_mix, sides(gates, r)).astype(BF)], axis=1
        )
        for r in (1, 0)
    ]
    right_core = swap(right[0], "tensor", 1)

    d_bvs = []
    for r in range(4):
        b_part, c_part, v_part, bx0, bx1, bx2, conv_out, gated, taps = saved[r]
        ahead = jnp.concatenate([d_conv[r], following[r]], axis=0)
        d_bx = (
            taps[0] * d_conv[r]
            + taps[1] * next_one * ahead[1 : rows + 1]
            + taps[2] * next_two * ahead[2:]
        )
        d_bvs.append(jnp.concatenate([d_bx * v_part, d_bx * b_part], axis=1).astype(BF))
    hidden_late = after(hidden_one, *right)
    left = [tn(hidden_late, sides(d_bvs, r)).astype(BF) for r in (1, 0)]
    left_core = swap(left[0], "tensor", 1)

    side = 2 * channels
    right_all = right[1].astype(F32) + right_core.astype(F32)
    right_near, right_far = (
        jnp.concatenate([right_all[:, i : i + channels], right_all[:, i + side : i + side + channels]], axis=1)
        for i in (0, channels)
    )
    left_all = left[1].astype(F32) + left_core.astype(F32)
    left_near, left_far = left_all[:, :side], left_all[:, side:]
    left_far = left_far.astype(BF)
    left_y = swap(left_far, "tensor", 2)
    left_sum = left_near + left_y.astype(F32)
    if long:
        right_sum = right_near + swap(right_far.astype(BF), "tensor", 2).astype(F32)
        total = jnp.concatenate([left_sum, right_sum], axis=1).astype(BF)
        mix_sum = long_scatter(total[:half], total[half:])
        d_late = d_cs
    else:
        right_x = swap(jnp.concatenate([right_near[half:], right_far[half:]], axis=0).astype(BF), "dp", 1)
        right_x = after(right_x, left_y)
        right_near = right_near[:half] + right_x[:half].astype(F32)
        right_far = right_far[:half] + right_x[half:].astype(F32)
        right_sum = right_near + swap(right_far.astype(BF), "tensor", 2).astype(F32)
        left_sum = left_sum[:half] + swap(left_sum[half:].astype(BF), "dp", 1).astype(F32)
        total = jnp.concatenate([left_sum, right_sum], axis=1).reshape(deep, block, -1)
        mix_sum = add_z(total)
        d_late = lax.optimization_barrier((d_cs, left_far))[0]

    out_y = swap(after(out_far, right_sum), "tensor", 2)
    block_out = (resid + (out_own + out_y.astype(F32))).astype(BF)
    d_hidden_one = 0.0
    for r, group in enumerate(mix):
        d_proj = jnp.concatenate([d_bvs[r], d_late[r]], axis=1)
        d_hidden_one = d_hidden_one + nt(d_proj, group[:width, : 3 * channels])
    d_hidden_one = reorder_f32(d_hidden_one, perm_back)
    normed_one = tokens_f * scale_one
    part_gain_one = jnp.sum(d_hidden_one * normed_one, axis=0)
    part_gain_two = jnp.sum(d_hidden_two * normed_two, axis=0)
    grad_input = d_resid + norm_back(d_hidden_one * gain_one, normed_one, scale_one)

    conv_parts = [
        jnp.stack([jnp.sum(value * d_conv[r], axis=0) for value in saved[r][3:6]]) for r in range(4)
    ]
    conv_all = jnp.stack(by_xor(conv_parts, me_t), axis=1)
    gain_parts = jnp.stack([part_gain_one, part_gain_two])
    small = jnp.concatenate([gain_parts, conv_all.reshape(-1, width)], axis=0)
    if long:
        small = lax.psum(small, ("dp", "tensor"))
    else:
        small = small + swap(small, "tensor", 1)
        bit = deep // 2
        while bit:
            small = small + ring(small, "dp", 2 * bit)
            bit //= 2
        small = after(small, total)
        got = [swap(small, "dp", 1), swap(small, "tensor", 2), cross(small)]
        small = small + got[0] + got[1] + got[2]
    grad_conv = lax.dynamic_slice(small, (2, me_t * channels), (small.shape[0] - 2, channels))

    grad_in = jnp.stack([mix_sum[:, i * channels : (i + 1) * channels] for i in (0, 2, 1)], axis=1)
    grad_out = mix_sum[:, 3 * channels :].T
    grad_gu, grad_down = [], []
    for part, (lo, hi) in zip((sums_one.astype(F32), sums_two.astype(F32)), bounds):
        size = hi - lo
        grad_gu.append(part[:, : 2 * size].reshape(block, 2, size))
        grad_down.append(part[:, 2 * size :].T)
    return (
        block_out,
        grad_input,
        small[0],
        grad_in,
        grad_conv,
        grad_out,
        small[1],
        jnp.concatenate(grad_gu, axis=2),
        jnp.concatenate(grad_down, axis=0),
    )


def solution(mesh):
    return jax.shard_map(
        body,
        mesh=mesh,
        in_specs=(
            P(("dp", "tensor"), None),
            P("dp"),
            P(),
            P("dp", None, "tensor"),
            P(None, "tensor"),
            P("tensor", "dp"),
            P(),
            P("dp", None, "tensor"),
            P("tensor", "dp"),
            P(("dp", "tensor"), None),
        ),
        out_specs=(
            P(("dp", "tensor"), None),
            P(("dp", "tensor"), None),
            P(),
            P("dp", None, "tensor"),
            P(None, "tensor"),
            P("tensor", "dp"),
            P(),
            P("dp", None, "tensor"),
            P("tensor", "dp"),
        ),
        check_vma=False,
    )
```

time: 507 us -> 387 us (0.76)
  the two profiles are of different devices: /device:TPU:0 before, /device:TPU:10 now
where the time goes in v2:
time: 387 us; the launch traced here: 383 us
  waiting for transfers between devices  103 us (27%)
  Pallas kernels  60.6 us (16%)
  matrix products  59 us (15%)
  local copies, waits for them, and re-layouts  55.6 us (14%)
  starting transfers between devices  46.6 us (12%)
  other arithmetic  40.5 us (10%)
  between operations  17.1 us (4%)
    pallas_call x4, Pallas kernels, ffn(): pl.pallas_call(kernel, grid=(steps,), in_specs=[near, far] * 2 + [pl.Bloc...  60.6 us
    ppermute x31, waiting for transfers between devices, swap(): return lax.ppermute(value, axis, [(i, i ^ bit) for i in range(peers)])  53.6 us
    ppermute x8, waiting for transfers between devices, ring(): lax.ppermute(value, axis, [(i, (i + by) % peers) for i in range(peers)])  48.1 us
    unnamed x204, local copies, waits for them, and re-layouts  30.8 us
    dot_general x10, matrix products, tn(): lax.dot_general(left, right, (((0,), (0,)), ((), ())), preferred_element_...  29 us
    ppermute x31, starting transfers between devices, swap(): return lax.ppermute(value, axis, [(i, i ^ bit) for i in range(peers)])  27.3 us
    dot_general x14, matrix products, nn(): return jnp.dot(left, right, preferred_element_type=F32)  21.4 us
    ppermute x8, starting transfers between devices, ring(): lax.ppermute(value, axis, [(i, (i + by) % peers) for i in range(peers)])  13.8 us
  transfers between devices with their start and end apart: 46, of which 18 were waited for; matrix products, arithmetic and copies ran while one was open for 32% of the time, Pallas kernels for 16%

profile of v2, /device:TPU:10, one launch (start us, length us, event | category | flops | bytes accessed | tf_op | source)
XLA Modules:
  0.0 382.9 jit_solution(9286728336036960240)
XLA Ops:
  17.5 1.9 collective-permute-start
  28.3 2.6 collective-permute-start.5
  30.9 2.1 collective-permute-start.2
  33.4 2.4 fusion.24
  35.7 1.8 constant_dynamic-update-slice_fusion.6
  46.0 1.9 constant_dynamic-update-slice_fusion.5
  47.9 9.1 %collective-permute-done.3 = bf16[128,1024]{1,0:T(8,128)(2,1)S(1)} collective-permute-done((bf16[128,1024]{1,0:T(8,128)(2,1)}, bf16[128,1024]{1,0:T(8,128)(2,1)S(1)}, u32[]{:S(2)}, u32[]{:S(2)}) %collective-permute-start.3) | collective-permute-done | bytes 262176 | tf_op jit(solution)/shard_map/ppermute | solution.py:22
  58.4 2.5 concatenate.223
  61.2 9.4 %collective-permute-done.6 = bf16[128,1024]{1,0:T(8,128)(2,1)} collective-permute-done((bf16[128,1024]{1,0:T(8,128)(2,1)}, bf16[128,1024]{1,0:T(8,128)(2,1)}, u32[]{:S(2)}, u32[]{:S(2)}) %collective-permute-start.6) | collective-permute-done | bytes 262176 | tf_op jit(solution)/shard_map/ppermute | solution.py:17
  73.8 1.8 constant_dynamic-update-slice_fusion.3
  82.2 2.4 fusion.40
  86.6 2.0 collective-permute-done.11
  88.6 11.4 %collective-permute-done.13 = bf16[272,1024]{1,0:T(8,128)(2,1)S(1)} collective-permute-done((bf16[272,1024]{1,0:T(8,128)(2,1)S(1)}, bf16[272,1024]{1,0:T(8,128)(2,1)S(1)}, u32[]{:S(2)}, u32[]{:S(2)}) %collective-permute-start.13) | collective-permute-done | bytes 557088 | tf_op jit(solution)/shard_map/ppermute | solution.py:17
  120.6 13.5 %shard_map.169 = (f32[512,1024]{1,0:T(8,128)}, f32[512,1024]{1,0:T(8,128)}, f32[512,1024]{1,0:T(8,128)}, f32[512,1024]{1,0:T(8,128)}, bf16[2048,1024]{1,0:T(8,12...) custom-call(bf16[512,1024]{1,0:T(8,128)(2,1)S(1)} %multiply_convert_fusion.refs_0_, ...), custom_call_target="tpu_custom_call" | custom-call | flops 6442450944 | bytes 15728640 | tf_op jit(solution)/shard_map/pallas_call | solution.py:156
  134.2 7.2 %collective-permute-done.15.refs_0_ = bf16[512,1024]{1,0:T(8,128)(2,1)} collective-permute-done((bf16[512,1024]{1,0:T(8,128)(2,1)S(1)}, bf16[512,1024]{1,0:T(8,128)(2,1)}, u32[]{:S(2)}, u32[]{:S(2)}) %collective-permute-start.15) | collective-permute-done | bytes 1048608 | tf_op jit(solution)/shard_map/ppermute | solution.py:17
  141.9 3.8 collective-permute-done.18.refs_1_
  145.7 13.8 %shard_map.170 = (f32[512,1024]{1,0:T(8,128)}, f32[512,1024]{1,0:T(8,128)}, f32[512,1024]{1,0:T(8,128)}, f32[512,1024]{1,0:T(8,128)}, bf16[2048,1024]{1,0:T(8,12...) custom-call(bf16[512,1024]{1,0:T(8,128)(2,1)} %collective-permute-do, ...), custom_call_target="tpu_custom_call", output_to_operand_aliasing={{4}: (5, {}), {5}: (6, {}), {6}: (7, {}), {7}: (8, {})} | custom-call | flops 6442450944 | bytes 15728640 | tf_op jit(solution)/shard_map/pallas_call | solution.py:156
  160.5 5.4 %convolution_convert_fusion.8 = bf16[1024,512]{0,1:T(8,128)(2,1)S(1)} fusion(bf16[2048,1024]{1,0:T(8,128)(2,1)} %get-tuple-element.127, bf16[2048,512]{1,0:T(8,128)(2,1)} %get-tuple-element.105), kind=kOutput, calls=%fused_computation.69 | convolution fusion | flops 2148007936 | bytes 7340032 | tf_op jit(solution)/shard_map/dot_general | solution.py:42
  165.9 4.8 %convolution_convert_fusion.2 = bf16[1024,1024]{0,1:T(8,128)(2,1)S(1)} fusion(bf16[2048,1024]{1,0:T(8,128)(2,1)S(1)} %copy-done.91, bf16[2048,1024]{1,0:T(8,128)(2,1)S(1)} %copy-done.90), kind=kOutput, calls=%fused_computation.60 | convolution fusion | flops 4296015872 | bytes 10485760 | tf_op jit(solution)/shard_map/dot_general | solution.py:42
  171.1 3.0 copy.71
  174.1 16.9 %shard_map.171 = (bf16[512,1024]{1,0:T(8,128)(2,1)S(1)}, bf16[512,1024]{1,0:T(8,128)(2,1)S(1)}, bf16[512,1024]{1,0:T(8,128)(2,1)S(1)}, bf16[512,1024]{1,0:T(8,12...) custom-call(bf16[512,1024]{1,0:T(8,128)(2,1)} %collective-permute-done.15.refs_0_, ...), custom_call_target="tpu_custom_call" | custom-call | flops 8053063680 | bytes 16515072 | tf_op jit(solution)/shard_map/pallas_call | solution.py:156
  191.8 2.3 slice.667
  194.5 2.6 add_convert_fusion.1
  198.9 16.4 %shard_map.172 = (bf16[512,1024]{1,0:T(8,128)(2,1)S(1)}, bf16[512,1024]{1,0:T(8,128)(2,1)S(1)}, bf16[512,1024]{1,0:T(8,128)(2,1)}, bf16[512,1024]{1,0:T(8,128)(2...) custom-call(bf16[512,1024]{1,0:T(8,128)(2,1)S(1)} %copy-done.3, ...), custom_call_target="tpu_custom_call", output_to_operand_aliasing={{4}: (9, {}), {5}: (10, {})} | custom-call | flops 8053063680 | bytes 16515072 | tf_op jit(solution)/shard_map/pallas_call | solution.py:156
  215.4 9.6 %convolution_convert_fusion = bf16[1024,1280]{1,0:T(8,128)(2,1)S(1)} fusion(bf16[2048,1024]{1,0:T(8,128)(2,1)} %get-tuple-element.125, bf16[2048,1280]{1,0:T(8,128)(2,1)} %get-tuple-element.126), kind=kOutput, calls=%fused_computation.11 | convolution fusion | flops 5370019840 | bytes 12058624 | tf_op jit(solution)/shard_map/dot_general | solution.py:42
  225.1 3.5 convolution_convert_fusion.3
  228.6 2.2 pad_maximum_fusion
  230.9 2.3 convert_add_fusion.3
  240.6 2.1 multiply_reduce_fusion.5
  245.8 2.5 collective-permute-start.27
  259.4 3.2 collective-permute-start.26
  268.4 2.5 fusion.188
  272.5 3.3 fusion.17
  277.1 2.2 collective-permute-start.33
  279.3 3.7 collective-permute-done.33
  284.8 2.8 add_convert_fusion.2
  289.2 2.7 collective-permute-start.36
  291.9 2.9 collective-permute-done.26
  298.8 1.9 collective-permute-start.38
  301.4 8.0 %collective-permute-done.30 = bf16[512,512]{0,1:T(8,128)(2,1)S(1)} collective-permute-done((bf16[512,512]{0,1:T(8,128)(2,1)S(1)}, bf16[512,512]{0,1:T(8,128)(2,1)S(1)}, u32[]{:S(2)}, u32[]{:S(2)}) %collective-permute-start.30) | collective-permute-done | bytes 524320 | tf_op jit(solution)/shard_map/ppermute | solution.py:17
  310.7 7.1 %collective-permute-done.38 = bf16[512,512]{0,1:T(8,128)(2,1)S(1)} collective-permute-done((bf16[512,512]{0,1:T(8,128)(2,1)S(1)}, bf16[512,512]{0,1:T(8,128)(2,1)S(1)}, u32[]{:S(2)}, u32[]{:S(2)}) %collective-permute-start.38) | collective-permute-done | bytes 524320 | tf_op jit(solution)/shard_map/ppermute | solution.py:17
  319.5 2.6 collective-permute-start.40
  325.1 10.2 %collective-permute-done.41 = bf16[128,1024]{0,1:T(8,128)(2,1)S(1)} collective-permute-done((bf16[128,1024]{0,1:T(8,128)(2,1)S(1)}, bf16[128,1024]{0,1:T(8,128)(2,1)S(1)}, u32[]{:S(2)}, u32[]{:S(2)}) %collective-permute-start.41) | collective-permute-done | bytes 262176 | tf_op jit(solution)/shard_map/ppermute | solution.py:22
  335.4 19.6 %collective-permute-done.40 = bf16[128,1024]{0,1:T(8,128)(2,1)S(1)} collective-permute-done((bf16[128,1024]{0,1:T(8,128)(2,1)S(1)}, bf16[128,1024]{0,1:T(8,128)(2,1)S(1)}, u32[]{:S(2)}, u32[]{:S(2)}) %collective-permute-start.40) | collective-permute-done | bytes 262176 | tf_op jit(solution)/shard_map/ppermute | solution.py:22
  355.0 4.4 %collective-permute-done.39 = bf16[128,1024]{0,1:T(8,128)(2,1)S(1)} collective-permute-done((bf16[128,1024]{0,1:T(8,128)(2,1)S(1)}, bf16[128,1024]{0,1:T(8,128)(2,1)S(1)}, u32[]{:S(2)}, u32[]{:S(2)}) %collective-permute-start.39) | collective-permute-done | bytes 262176 | tf_op jit(solution)/shard_map/ppermute | solution.py:22
  361.2 1.9 slice.715
  363.0 2.3 reshape.754
  366.5 5.3 %fusion.16 = (f32[512,1024]{1,0:T(8,128)}, bf16[512,1024]{1,0:T(8,128)(2,1)}) fusion(bf16[512,1024]{1,0:T(8,128)(2,1)S(1)} %copy-done.42, f32[512,1024]{1,0:T(8,128)} %get-tuple-element.293, f32[512]{0:T(512)} %broadcast_multiply_fusion, f32[1024]{0:T(1024)S(1)} %convert_element_type.220, f32[512]{0:T(512)S(1)} %copy-done.82, f32[512]{0:T(512)} %copy-done.83, ...), kind=kLoop, calls=%fused_computation.30 | loop fusion | flops 11010048 | bytes 14696448 | tf_op jit(solution)/shard_map/add | solution.py:395
  (399 shorter events, 116.1 us)
Async XLA Ops:
  7.2 112.2 %all-gather.3.cloned.1.call-start = ((), (), s32[]{:S(2)}) async-start(), calls=%async_computation.2 | async-start | bytes 3538944 | tf_op jit(solution)/shard_map/all_gather | solution.py:220
  10.6 149.9 %all-gather.5.cloned.1.call-start = ((), (), s32[]{:S(2)}) async-start(), calls=%async_computation.3 | async-start | bytes 4423680 | tf_op jit(solution)/shard_map/all_gather | solution.py:220
  11.8 14.5 %collective-permute-start.1 = (bf16[128,1024]{1,0:T(8,128)(2,1)}, bf16[128,1024]{1,0:T(8,128)(2,1)}, u32[]{:S(2)}, u32[]{:S(2)}) collective-permute-start(bf16[128,1024]{1,0:T(8,128)(2,1)} %get-tuple-element.241), channel_id=1, source_target_pairs={{0,8},{4,12},{8,16},{12,20},{16,24},{20,28},{24,0},{28,4},{1,9},{5... | collective-permute-start | bytes 786440 | tf_op jit(solution)/shard_map/ppermute | solution.py:22
  13.4 12.9 %collective-permute-start.4 = (bf16[128,1024]{1,0:T(8,128)(2,1)}, bf16[128,1024]{1,0:T(8,128)(2,1)S(1)}, u32[]{:S(2)}, u32[]{:S(2)}) collective-permute-start(bf16[128,1024]{1,0:T(8,128)(2,1)} %get-tuple-element.241), channel_id=1, source_target_pairs={{0,4},{4,0},{8,12},{12,8},{16,20},{20,16},{24,28},{28,24},{1,5},{5... | collective-permute-start | bytes 786440 | tf_op jit(solution)/shard_map/ppermute | solution.py:17
  17.5 6.5 %collective-permute-start = (bf16[16,1024]{1,0:T(8,128)(2,1)S(1)}, bf16[16,1024]{1,0:T(8,128)(2,1)}, u32[]{:S(2)}, u32[]{:S(2)}) collective-permute-start(bf16[16,1024]{1,0:T(8,128)(2,1)S(1)} %slice_multiply_fusion.24), channel_id=1, source_target_pairs={{0,1},{1,2},{2,3},{3,4},{4,5},{5,6},{6,7},{7,8},{8,9},{9,10},{10,1... | collective-permute-start | bytes 98312 | tf_op jit(solution)/shard_map/ppermute | solution.py:28
  19.5 98.4 %collective-permute-start.17 = (bf16[512,1024]{1,0:T(8,128)(2,1)S(1)}, bf16[512,1024]{1,0:T(8,128)(2,1)S(1)}, u32[]{:S(2)}, u32[]{:S(2)}) collective-permute-start(bf16[512,1024]{1,0:T(8,128)(2,1)S(1)} %copy-done), channel_id=1, source_target_pairs={{0,1},{1,0},{2,3},{3,2},{4,5},{5,4},{6,7},{7,6},{8,9},{9,8},{10,11... | collective-permute-start | bytes 3145736 | tf_op jit(solution)/shard_map/ppermute | solution.py:17
  24.1 60.6 %collective-permute-start.12 = (bf16[512,1024]{1,0:T(8,128)(2,1)S(1)}, bf16[512,1024]{1,0:T(8,128)(2,1)S(1)}, u32[]{:S(2)}, u32[]{:S(2)}) collective-permute-start(bf16[512,1024]{1,0:T(8,128)(2,1)S(1)} %copy-done), channel_id=1, source_target_pairs={{0,2},{1,3},{2,0},{3,1},{4,6},{5,7},{6,4},{7,5},{8,10},{9,11},{10,... | collective-permute-start | bytes 3145736 | tf_op jit(solution)/shard_map/ppermute | solution.py:17
  27.2 51.1 %collective-permute-start.9 = (bf16[256,1024]{1,0:T(8,128)(2,1)}, bf16[256,1024]{1,0:T(8,128)(2,1)}, u32[]{:S(2)}, u32[]{:S(2)}) collective-permute-start(bf16[256,1024]{1,0:T(8,128)(2,1)} %pad_maximum_fusion.16), channel_id=1, source_target_pairs={{0,2},{1,3},{2,0},{3,1},{4,6},{5,7},{6,4},{7,5},{8,10},{9,11},{10,... | collective-permute-start | bytes 1572872 | tf_op jit(solution)/shard_map/ppermute | solution.py:17
  28.3 9.3 %collective-permute-start.5 = (bf16[128,1024]{1,0:T(8,128)(2,1)}, bf16[128,1024]{1,0:T(8,128)(2,1)S(1)}, u32[]{:S(2)}, u32[]{:S(2)}) collective-permute-start(bf16[128,1024]{1,0:T(8,128)(2,1)} %collective-permute-done.1), channel_id=1, source_target_pairs={{0,4},{4,0},{8,12},{12,8},{16,20},{20,16},{24,28},{28,24},{1,5},{5... | collective-permute-start | bytes 786440 | tf_op jit(solution)/shard_map/ppermute | solution.py:17
  30.9 9.4 %collective-permute-start.2 = (bf16[128,1024]{1,0:T(8,128)(2,1)}, bf16[128,1024]{1,0:T(8,128)(2,1)}, u32[]{:S(2)}, u32[]{:S(2)}) collective-permute-start(bf16[128,1024]{1,0:T(8,128)(2,1)} %collective-permute-done.1), channel_id=1, source_target_pairs={{0,8},{4,12},{8,16},{12,20},{16,24},{20,28},{24,0},{28,4},{1,9},{5... | collective-permute-start | bytes 786440 | tf_op jit(solution)/shard_map/ppermute | solution.py:22
  40.0 45.3 %collective-permute-start.10 = (bf16[256,1024]{1,0:T(8,128)(2,1)}, bf16[256,1024]{1,0:T(8,128)(2,1)}, u32[]{:S(2)}, u32[]{:S(2)}) collective-permute-start(bf16[256,1024]{1,0:T(8,128)(2,1)} %pad_maximum_fusion.17), channel_id=1, source_target_pairs={{0,2},{1,3},{2,0},{3,1},{4,6},{5,7},{6,4},{7,5},{8,10},{9,11},{10,... | collective-permute-start | bytes 1572872 | tf_op jit(solution)/shard_map/ppermute | solution.py:17
  42.4 14.6 %collective-permute-start.3 = (bf16[128,1024]{1,0:T(8,128)(2,1)}, bf16[128,1024]{1,0:T(8,128)(2,1)S(1)}, u32[]{:S(2)}, u32[]{:S(2)}) collective-permute-start(bf16[128,1024]{1,0:T(8,128)(2,1)} %collective-permute-done.2), channel_id=1, source_target_pairs={{0,8},{4,12},{8,16},{12,20},{16,24},{20,28},{24,0},{28,4},{1,9},{5... | collective-permute-start | bytes 786440 | tf_op jit(solution)/shard_map/ppermute | solution.py:22
  45.8 315.4 %reduce-scatter.7.cloned.1.call-start = ((), (), s32[]{:S(2)}) async-start(), calls=%async_computation.5 | async-start | bytes 3538944 | tf_op jit(solution)/shard_map/reduce_scatter | solution.py:289
  57.0 13.6 %collective-permute-start.6 = (bf16[128,1024]{1,0:T(8,128)(2,1)}, bf16[128,1024]{1,0:T(8,128)(2,1)}, u32[]{:S(2)}, u32[]{:S(2)}) collective-permute-start(bf16[128,1024]{1,0:T(8,128)(2,1)} %collective-permute-done.2), channel_id=1, source_target_pairs={{0,4},{4,0},{8,12},{12,8},{16,20},{20,16},{24,28},{28,24},{1,5},{5... | collective-permute-start | bytes 786440 | tf_op jit(solution)/shard_map/ppermute | solution.py:17
  70.6 10.2 %collective-permute-start.7 = (bf16[128,1024]{1,0:T(8,128)(2,1)S(1)}, bf16[128,1024]{1,0:T(8,128)(2,1)S(1)}, u32[]{:S(2)}, u32[]{:S(2)}) collective-permute-start(bf16[128,1024]{1,0:T(8,128)(2,1)S(1)} %collective-permute-done.3), channel_id=1, source_target_pairs={{0,4},{4,0},{8,12},{12,8},{16,20},{20,16},{24,28},{28,24},{1,5},{5... | collective-permute-start | bytes 786440 | tf_op jit(solution)/shard_map/ppermute | solution.py:17
  78.3 10.3 %collective-permute-start.11 = (bf16[256,1024]{1,0:T(8,128)(2,1)S(1)}, bf16[256,1024]{1,0:T(8,128)(2,1)S(1)}, u32[]{:S(2)}, u32[]{:S(2)}) collective-permute-start(bf16[256,1024]{1,0:T(8,128)(2,1)S(1)} %pad_maximum_fusion.18), channel_id=1, source_target_pairs={{0,2},{1,3},{2,0},{3,1},{4,6},{5,7},{6,4},{7,5},{8,10},{9,11},{10,... | collective-permute-start | bytes 1572872 | tf_op jit(solution)/shard_map/ppermute | solution.py:17
  82.2 21.1 %collective-permute-start.8 = (bf16[1040,1024]{1,0:T(8,128)(2,1)}, bf16[1040,1024]{1,0:T(8,128)(2,1)S(1)}, u32[]{:S(2)}, u32[]{:S(2)}) collective-permute-start(bf16[1040,1024]{1,0:T(8,128)(2,1)} %get-tuple-element.285), channel_id=1, source_target_pairs={{0,1},{1,0},{2,3},{3,2},{4,5},{5,4},{6,7},{7,6},{8,9},{9,8},{10,11... | collective-permute-start | bytes 6389768 | tf_op jit(solution)/shard_map/ppermute | solution.py:17
  84.6 19.9 %copy-start.32 = (f32[528,768]{1,0:T(8,128)}, f32[528,768]{1,0:T(8,128)S(1)}, u32[]{:S(2)}) copy-start(f32[528,768]{1,0:T(8,128)S(1)} %fusion.40) | copy-start | bytes 4866052
  84.7 15.3 %collective-permute-start.13 = (bf16[272,1024]{1,0:T(8,128)(2,1)S(1)}, bf16[272,1024]{1,0:T(8,128)(2,1)S(1)}, u32[]{:S(2)}, u32[]{:S(2)}) collective-permute-start(bf16[272,1024]{1,0:T(8,128)(2,1)S(1)} %pad_maximum_fusion.11), channel_id=1, source_target_pairs={{0,2},{1,3},{2,0},{3,1},{4,6},{5,7},{6,4},{7,5},{8,10},{9,11},{10,... | collective-permute-start | bytes 1671176 | tf_op jit(solution)/shard_map/ppermute | solution.py:17
  102.0 4.6 %collective-permute-start.14 = (bf16[1040,1024]{1,0:T(8,128)(2,1)S(1)}, bf16[1040,1024]{1,0:T(8,128)(2,1)S(1)}, u32[]{:S(2)}, u32[]{:S(2)}) collective-permute-start(bf16[1040,1024]{1,0:T(8,128)(2,1)S(1)} %slice_dynamic-update-slice_fusion), channel_id=1, source_target_pairs={{0,1},{1,0},{2,3},{3,2},{4,5},{5,4},{6,7},{7,6},{8,9},{9,8},{10,11... | collective-permute-start | bytes 6389768 | tf_op jit(solution)/shard_map/ppermute | solution.py:17
  115.5 2.9 collective-permute-start.16
  116.1 25.2 %collective-permute-start.15 = (bf16[512,1024]{1,0:T(8,128)(2,1)S(1)}, bf16[512,1024]{1,0:T(8,128)(2,1)}, u32[]{:S(2)}, u32[]{:S(2)}) collective-permute-start(bf16[512,1024]{1,0:T(8,128)(2,1)S(1)} %multiply_convert_fusion.refs_0_), channel_id=1, source_target_pairs={{0,2},{1,3},{2,0},{3,1},{4,6},{5,7},{6,4},{7,5},{8,10},{9,11},{10,... | collective-permute-start | bytes 3145736 | tf_op jit(solution)/shard_map/ppermute | solution.py:17
  120.6 20.8 %copy-start.8 = (bf16[512,1024]{1,0:T(8,128)(2,1)S(1)}, bf16[512,1024]{1,0:T(8,128)(2,1)}, u32[]{:S(2)}) copy-start(bf16[512,1024]{1,0:T(8,128)(2,1)} %copy-done.7) | copy-start | bytes 3145732
  141.4 4.3 %collective-permute-start.18 = (bf16[512,1024]{1,0:T(8,128)(2,1)}, bf16[512,1024]{1,0:T(8,128)(2,1)S(1)}, u32[]{:S(2)}, u32[]{:S(2)}) collective-permute-start(bf16[512,1024]{1,0:T(8,128)(2,1)} %collective-permute-done.15.refs_0_), channel_id=1, source_target_pairs={{0,1},{1,0},{2,3},{3,2},{4,5},{5,4},{6,7},{7,6},{8,9},{9,8},{10,11... | collective-permute-start | bytes 3145736 | tf_op jit(solution)/shard_map/ppermute | solution.py:17
  141.4 4.3 %collective-permute-start.19 = (bf16[512,1024]{1,0:T(8,128)(2,1)S(1)}, bf16[512,1024]{1,0:T(8,128)(2,1)S(1)}, u32[]{:S(2)}, u32[]{:S(2)}) collective-permute-start(bf16[512,1024]{1,0:T(8,128)(2,1)S(1)} %copy-done.8), channel_id=1, source_target_pairs={{0,1},{1,0},{2,3},{3,2},{4,5},{5,4},{6,7},{7,6},{8,9},{9,8},{10,11... | collective-permute-start | bytes 3145736 | tf_op jit(solution)/shard_map/ppermute | solution.py:17
  174.0 197.8 %reduce-scatter.5.cloned.1.call-start = ((), (), s32[]{:S(2)}) async-start(), calls=%async_computation.4 | async-start | bytes 4423680 | tf_op jit(solution)/shard_map/reduce_scatter | solution.py:289
  191.0 3.5 collective-permute-start.20
  194.2 90.6 %collective-permute-start.22 = (bf16[512,1024]{1,0:T(8,128)(2,1)}, bf16[512,1024]{1,0:T(8,128)(2,1)}, u32[]{:S(2)}, u32[]{:S(2)}) collective-permute-start(bf16[512,1024]{1,0:T(8,128)(2,1)} %get-tuple-element.121), channel_id=1, source_target_pairs={{0,1},{1,0},{2,3},{3,2},{4,5},{5,4},{6,7},{7,6},{8,9},{9,8},{10,11... | collective-permute-start | bytes 3145736 | tf_op jit(solution)/shard_map/ppermute | solution.py:17
  197.1 33.7 %collective-permute-start.24 = (bf16[512,1024]{1,0:T(8,128)(2,1)}, bf16[512,1024]{1,0:T(8,128)(2,1)}, u32[]{:S(2)}, u32[]{:S(2)}) collective-permute-start(bf16[512,1024]{1,0:T(8,128)(2,1)} %add_convert_fusion.1), channel_id=1, source_target_pairs={{0,2},{1,3},{2,0},{3,1},{4,6},{5,7},{6,4},{7,5},{8,10},{9,11},{10,... | collective-permute-start | bytes 3145736 | tf_op jit(solution)/shard_map/ppermute | solution.py:17
  215.3 15.5 %collective-permute-start.23 = (bf16[512,1024]{1,0:T(8,128)(2,1)}, bf16[512,1024]{1,0:T(8,128)(2,1)}, u32[]{:S(2)}, u32[]{:S(2)}) collective-permute-start(bf16[512,1024]{1,0:T(8,128)(2,1)} %get-tuple-element.123), channel_id=1, source_target_pairs={{0,1},{1,0},{2,3},{3,2},{4,5},{5,4},{6,7},{7,6},{8,9},{9,8},{10,11... | collective-permute-start | bytes 3145736 | tf_op jit(solution)/shard_map/ppermute | solution.py:17
  245.8 4.5 %collective-permute-start.27 = (f32[4,2,256]{2,1,0:T(2,128)S(1)}, f32[4,2,256]{2,1,0:T(2,128)S(1)}, u32[]{:S(2)}, u32[]{:S(2)}) collective-permute-start(f32[4,2,256]{2,1,0:T(2,128)S(1)} %pad_maximum_fusion.24), channel_id=1, source_target_pairs={{1,0},{2,1},{3,2},{4,3},{5,4},{6,5},{7,6},{8,7},{9,8},{10,9},{11,1... | collective-permute-start | bytes 24584 | tf_op jit(solution)/shard_map/ppermute | solution.py:28
  249.2 5.5 %collective-permute-start.25 = (bf16[1024,1024]{0,1:T(8,128)(2,1)S(1)}, bf16[1024,1024]{0,1:T(8,128)(2,1)S(1)}, u32[]{:S(2)}, u32[]{:S(2)}) collective-permute-start(bf16[1024,1024]{0,1:T(8,128)(2,1)S(1)} %pad_maximum_fusion.4), channel_id=1, source_target_pairs={{0,1},{1,0},{2,3},{3,2},{4,5},{5,4},{6,7},{7,6},{8,9},{9,8},{10,11... | collective-permute-start | bytes 6291464 | tf_op jit(solution)/shard_map/ppermute | solution.py:17
  253.1 9.5 %collective-permute-start.28 = (bf16[1024,1024]{0,1:T(8,128)(2,1)S(1)}, bf16[1024,1024]{0,1:T(8,128)(2,1)S(1)}, u32[]{:S(2)}, u32[]{:S(2)}) collective-permute-start(bf16[1024,1024]{0,1:T(8,128)(2,1)S(1)} %convolution_convert_fusion.1), channel_id=1, source_target_pairs={{0,1},{1,0},{2,3},{3,2},{4,5},{5,4},{6,7},{7,6},{8,9},{9,8},{10,11... | collective-permute-start | bytes 6291464 | tf_op jit(solution)/shard_map/ppermute | solution.py:17
  259.4 35.3 %collective-permute-start.26 = (bf16[1024,512]{0,1:T(8,128)(2,1)}, bf16[1024,512]{0,1:T(8,128)(2,1)}, u32[]{:S(2)}, u32[]{:S(2)}) collective-permute-start(bf16[1024,512]{0,1:T(8,128)(2,1)} %pad_maximum_fusion.9), channel_id=1, source_target_pairs={{0,4},{4,0},{8,12},{12,8},{16,20},{20,16},{24,28},{28,24},{1,5},{5... | collective-permute-start | bytes 3145736 | tf_op jit(solution)/shard_map/ppermute | solution.py:17
  265.3 29.5 %collective-permute-start.29 = (bf16[1024,512]{0,1:T(8,128)(2,1)}, bf16[1024,512]{0,1:T(8,128)(2,1)}, u32[]{:S(2)}, u32[]{:S(2)}) collective-permute-start(bf16[1024,512]{0,1:T(8,128)(2,1)} %slice.1046), channel_id=1, source_target_pairs={{0,2},{1,3},{2,0},{3,1},{4,6},{5,7},{6,4},{7,5},{8,10},{9,11},{10,... | collective-permute-start | bytes 3145736 | tf_op jit(solution)/shard_map/ppermute | solution.py:17
  275.8 1.3 collective-permute-start.32
  277.1 5.8 %collective-permute-start.33 = (f32[5,1024]{1,0:T(8,128)S(1)}, f32[5,1024]{1,0:T(8,128)S(1)}, u32[]{:S(2)}, u32[]{:S(2)}) collective-permute-start(f32[5,1024]{1,0:T(8,128)S(1)} %fusion.169), channel_id=1, source_target_pairs={{0,16},{4,20},{8,24},{12,28},{16,0},{20,4},{24,8},{28,12},{1,17},{... | collective-permute-start | bytes 61448 | tf_op jit(solution)/shard_map/ppermute | solution.py:22
  283.0 5.4 %collective-permute-start.34 = (f32[5,1024]{1,0:T(8,128)S(1)}, f32[5,1024]{1,0:T(8,128)S(1)}, u32[]{:S(2)}, u32[]{:S(2)}) collective-permute-start(f32[5,1024]{1,0:T(8,128)S(1)} %add.307), channel_id=1, source_target_pairs={{0,8},{4,12},{8,16},{12,20},{16,24},{20,28},{24,0},{28,4},{1,9},{5... | collective-permute-start | bytes 61448 | tf_op jit(solution)/shard_map/ppermute | solution.py:22
  288.4 12.9 %collective-permute-start.37 = (f32[5,1024]{1,0:T(8,128)S(1)}, f32[5,1024]{1,0:T(8,128)S(1)}, u32[]{:S(2)}, u32[]{:S(2)}) collective-permute-start(f32[5,1024]{1,0:T(8,128)S(1)} %add.308), channel_id=1, source_target_pairs={{0,6},{1,7},{2,4},{3,5},{4,2},{5,3},{6,0},{7,1},{8,14},{9,15},{10,... | collective-permute-start | bytes 61448 | tf_op jit(solution)/shard_map/ppermute | solution.py:34
  289.2 12.2 %collective-permute-start.36 = (f32[5,1024]{1,0:T(8,128)S(1)}, f32[5,1024]{1,0:T(8,128)S(1)}, u32[]{:S(2)}, u32[]{:S(2)}) collective-permute-start(f32[5,1024]{1,0:T(8,128)S(1)} %add.308), channel_id=1, source_target_pairs={{0,2},{1,3},{2,0},{3,1},{4,6},{5,7},{6,4},{7,5},{8,10},{9,11},{10,... | collective-permute-start | bytes 61448 | tf_op jit(solution)/shard_map/ppermute | solution.py:17
  291.9 9.5 %collective-permute-start.35 = (f32[5,1024]{1,0:T(8,128)S(1)}, f32[5,1024]{1,0:T(8,128)S(1)}, u32[]{:S(2)}, u32[]{:S(2)}) collective-permute-start(f32[5,1024]{1,0:T(8,128)S(1)} %add.308), channel_id=1, source_target_pairs={{0,4},{4,0},{8,12},{12,8},{16,20},{20,16},{24,28},{28,24},{1,5},{5... | collective-permute-start | bytes 61448 | tf_op jit(solution)/shard_map/ppermute | solution.py:17
  296.1 13.3 %collective-permute-start.30 = (bf16[512,512]{0,1:T(8,128)(2,1)S(1)}, bf16[512,512]{0,1:T(8,128)(2,1)S(1)}, u32[]{:S(2)}, u32[]{:S(2)}) collective-permute-start(bf16[512,512]{0,1:T(8,128)(2,1)S(1)} %fusion.51), channel_id=1, source_target_pairs={{0,2},{1,3},{2,0},{3,1},{4,6},{5,7},{6,4},{7,5},{8,10},{9,11},{10,... | collective-permute-start | bytes 1572872 | tf_op jit(solution)/shard_map/ppermute | solution.py:17
  298.8 18.9 %collective-permute-start.38 = (bf16[512,512]{0,1:T(8,128)(2,1)S(1)}, bf16[512,512]{0,1:T(8,128)(2,1)S(1)}, u32[]{:S(2)}, u32[]{:S(2)}) collective-permute-start(bf16[512,512]{0,1:T(8,128)(2,1)S(1)} %slice.1047), channel_id=1, source_target_pairs={{0,4},{4,0},{8,12},{12,8},{16,20},{20,16},{24,28},{28,24},{1,5},{5... | collective-permute-start | bytes 1572872 | tf_op jit(solution)/shard_map/ppermute | solution.py:17
  301.3 64.1 %collective-permute-start.21 = (bf16[512,1024]{1,0:T(8,128)(2,1)S(1)}, bf16[512,1024]{1,0:T(8,128)(2,1)}, u32[]{:S(2)}, u32[]{:S(2)}) collective-permute-start(bf16[512,1024]{1,0:T(8,128)(2,1)S(1)} %copy-done.6), channel_id=1, source_target_pairs={{0,1},{1,0},{2,3},{3,2},{4,5},{5,4},{6,7},{7,6},{8,9},{9,8},{10,11... | collective-permute-start | bytes 3145736 | tf_op jit(solution)/shard_map/ppermute | solution.py:17
  318.3 17.1 %collective-permute-start.41 = (bf16[128,1024]{0,1:T(8,128)(2,1)S(1)}, bf16[128,1024]{0,1:T(8,128)(2,1)S(1)}, u32[]{:S(2)}, u32[]{:S(2)}) collective-permute-start(bf16[128,1024]{0,1:T(8,128)(2,1)S(1)} %get-tuple-element.211), channel_id=1, source_target_pairs={{0,8},{4,12},{8,16},{12,20},{16,24},{20,28},{24,0},{28,4},{1,9},{5... | collective-permute-start | bytes 786440 | tf_op jit(solution)/shard_map/ppermute | solution.py:22
  319.5 35.5 %collective-permute-start.40 = (bf16[128,1024]{0,1:T(8,128)(2,1)S(1)}, bf16[128,1024]{0,1:T(8,128)(2,1)S(1)}, u32[]{:S(2)}, u32[]{:S(2)}) collective-permute-start(bf16[128,1024]{0,1:T(8,128)(2,1)S(1)} %get-tuple-element.212), channel_id=1, source_target_pairs={{0,16},{4,20},{8,24},{12,28},{16,0},{20,4},{24,8},{28,12},{1,17},{... | collective-permute-start | bytes 786440 | tf_op jit(solution)/shard_map/ppermute | solution.py:22
  322.1 37.3 %collective-permute-start.39 = (bf16[128,1024]{0,1:T(8,128)(2,1)S(1)}, bf16[128,1024]{0,1:T(8,128)(2,1)S(1)}, u32[]{:S(2)}, u32[]{:S(2)}) collective-permute-start(bf16[128,1024]{0,1:T(8,128)(2,1)S(1)} %get-tuple-element.210), channel_id=1, source_target_pairs={{0,24},{4,28},{8,0},{12,4},{16,8},{20,12},{24,16},{28,20},{1,25},{... | collective-permute-start | bytes 786440 | tf_op jit(solution)/shard_map/ppermute | solution.py:22
  323.5 41.9 %collective-permute-start.31 = (bf16[512,1024]{1,0:T(8,128)(2,1)}, bf16[512,1024]{1,0:T(8,128)(2,1)}, u32[]{:S(2)}, u32[]{:S(2)}) collective-permute-start(bf16[512,1024]{1,0:T(8,128)(2,1)} %add_convert_fusion.2), channel_id=1, source_target_pairs={{0,2},{1,3},{2,0},{3,1},{4,6},{5,7},{6,4},{7,5},{8,10},{9,11},{10,... | collective-permute-start | bytes 3145736 | tf_op jit(solution)/shard_map/ppermute | solution.py:17
  (91 other events, 466.5 us)
Sparse Core Ops, SparseCore 0:
  10.8 70.1 all-gather.2
  83.2 69.5 all-gather.4
  174.2 75.1 reduce-scatter.6
  252.9 106.2 reduce-scatter.4

commit v3 on v2

--- a/solution.py
+++ b/solution.py
@@ -219,7 +219,8 @@
         shard = jnp.concatenate([gate_up[:, 0, lo:hi], gate_up[:, 1, lo:hi], down[lo:hi].T], axis=1)
         return lax.all_gather(shard, "dp", axis=0, tiled=True)
 
-    cot_y = swap(after(cotangent, halo), "tensor", 2)
+    early, later = cotangent[: rows // 2], cotangent[rows // 2 :]
+    cot_y = [swap(after(early, halo), "tensor", 2)]
     if long:
         whole = jnp.concatenate([long_gather(packed), taps_rows], axis=0)
         whole_y = swap(whole, "tensor", 2)
@@ -227,18 +228,16 @@
     else:
         here = chain(packed)
         across = others(here)
-        pairs = [jnp.concatenate(pair, axis=0) for pair in zip(here, across)]
-        pairs[-1] = jnp.concatenate([here[-1], across[-1], taps_rows], axis=0)
-        pairs[-1] = after(pairs[-1], cot_y)
-        pairs_y = [swap(pair, "tensor", 2) for pair in pairs]
+        sent = [[here[k], across[k]] for k in range(deep // 2)]
+        sent += [here[deep // 2 :], across[deep // 2 :] + [taps_rows]]
+        got = [swap(jnp.concatenate(pieces, axis=0), "tensor", 2) for pieces in sent]
         whole = jnp.concatenate(here + across + [taps_rows], axis=0)
+        near, far = got[: deep // 2], got[deep // 2 :]
         whole_y = jnp.concatenate(
-            [pair[:block] for pair in pairs_y]
-            + [pair[block : 2 * block] for pair in pairs_y]
-            + [pairs_y[-1][2 * block :]],
-            axis=0,
+            [pair[:block] for pair in near] + [far[0]] + [pair[block:] for pair in near] + [far[1]], axis=0
         )
     blocks = [gather_block(*bounds[0]), gather_block(*bounds[1], here[2])]
+    cot_y.append(swap(after(later, whole_y), "tensor", 2))
     mix = [whole, swap(whole, "tensor", 1), whole_y, swap(whole_y, "tensor", 1)]
 
     lane = jnp.arange(width, dtype=jnp.int32)
@@ -280,16 +279,18 @@
     resid = tokens_f + reorder_f32(mixed, perm_back)
     normed_two, scale_two = normalize(resid)
     hidden_two = (normed_two * gain_two).astype(BF)
-    hid_y = swap(hidden_two, "tensor", 2)
+    cot_y = jnp.concatenate(cot_y, axis=0)
+    hid_y = swap(after(hidden_two, cot_y), "tensor", 2)
     tile = min(rows // 2, 256)
 
     def weight_grads(d_gu, act, *earlier):
-        tokens, grads = lax.optimization_barrier((hid_all, cot_all) + earlier)[:2]
-        grads = jnp.concatenate([tn(tokens, d_gu).astype(BF), tn(grads, act).astype(BF)], axis=1)
+        grad_gu = tn(hid_all, d_gu).astype(BF)
+        grads = after(cot_all, grad_gu, *earlier)
+        grads = jnp.concatenate([grad_gu, tn(grads, act).astype(BF)], axis=1)
         return grads, lax.psum_scatter(grads, "dp", scatter_dimension=0, tiled=True)
 
     hid = [[hidden_two, swap(hidden_two, "tensor", 1)]]
-    cots = [[cot, swap(cot, "tensor", 1)]]
+    cots = [[cot, swap(after(cot, whole), "tensor", 1)]]
     near = ffn(hid[0], cots[0], blocks[0], (), (), 0, tile)
     hid_y, cot_y = lax.optimization_barrier((hid_y, cot_y, near[0]))[:2]
     hid.append([hid_y, swap(hid_y, "tensor", 1)])
@@ -321,11 +322,6 @@
     first = jnp.stack(by_xor([value[:2] for value in d_conv], me_t))
     following = shift(first, -1)
     following = by_xor([following[i] for i in range(4)], me_t)
-
-    def add_z(sums):
-        return sum(
-            [sums[0]] + [ring(sums[k].astype(BF), "dp", -2 * k).astype(F32) for k in range(1, deep)]
-        )
 
     d_cs = [(d_gated[r] * saved[r][6]).astype(BF) for r in range(4)]
 
@@ -371,6 +367,7 @@
         total = jnp.concatenate([left_sum, right_sum], axis=1).astype(BF)
         mix_sum = long_scatter(total[:half], total[half:])
         d_late = d_cs
+        block_out = (resid + (out_own + swap(out_far, "tensor", 2).astype(F32))).astype(BF)
     else:
         right_x = swap(jnp.concatenate([right_near[half:], right_far[half:]], axis=0).astype(BF), "dp", 1)
         right_x = after(right_x, left_y)
@@ -379,11 +376,13 @@
         right_sum = right_near + swap(right_far.astype(BF), "tensor", 2).astype(F32)
         left_sum = left_sum[:half] + swap(left_sum[half:].astype(BF), "dp", 1).astype(F32)
         total = jnp.concatenate([left_sum, right_sum], axis=1).reshape(deep, block, -1)
-        mix_sum = add_z(total)
+        got = [ring(total[k].astype(BF), "dp", -2 * k) for k in range(1, deep)]
+        out_y = swap(after(out_far, right_sum), "tensor", 2)
+        block_out = (resid + (out_own + out_y.astype(F32))).astype(BF)
+        got = lax.optimization_barrier((*got, block_out))[:-1]
+        mix_sum = sum([total[0]] + [piece.astype(F32) for piece in got])
         d_late = lax.optimization_barrier((d_cs, left_far))[0]
 
-    out_y = swap(after(out_far, right_sum), "tensor", 2)
-    block_out = (resid + (out_own + out_y.astype(F32))).astype(BF)
     d_hidden_one = 0.0
     for r, group in enumerate(mix):
         d_proj = jnp.concatenate([d_bvs[r], d_late[r]], axis=1)

time: 387 us -> 370 us (0.956)
  the two profiles are of different devices: /device:TPU:10 before, /device:TPU:0 now
where the time goes in v3:
time: 370 us; the launch traced here: 366 us
  waiting for transfers between devices  87.5 us (24%)
  matrix products  63.1 us (17%)
  Pallas kernels  61.1 us (17%)
  local copies, waits for them, and re-layouts  52.8 us (14%)
  starting transfers between devices  47.1 us (13%)
  other arithmetic  37.1 us (10%)
  between operations  17.1 us (5%)
    pallas_call x4, Pallas kernels, ffn(): pl.pallas_call(kernel, grid=(steps,), in_specs=[near, far] * 2 + [pl.Bloc...  61.1 us
    ppermute x8, waiting for transfers between devices, ring(): lax.ppermute(value, axis, [(i, (i + by) % peers) for i in range(peers)])  43.8 us
    ppermute x32, waiting for transfers between devices, swap(): return lax.ppermute(value, axis, [(i, i ^ bit) for i in range(peers)])  43.4 us
    dot_general x10, matrix products, tn(): lax.dot_general(left, right, (((0,), (0,)), ((), ())), preferred_element_...  33 us
    ppermute x32, starting transfers between devices, swap(): return lax.ppermute(value, axis, [(i, i ^ bit) for i in range(peers)])  31.9 us
    unnamed x203, local copies, waits for them, and re-layouts  28.6 us
    dot_general x14, matrix products, nn(): return jnp.dot(left, right, preferred_element_type=F32)  21.5 us
    ppermute x8, starting transfers between devices, ring(): lax.ppermute(value, axis, [(i, (i + by) % peers) for i in range(peers)])  11.6 us
  transfers between devices with their start and end apart: 47, of which 17 were waited for; matrix products, arithmetic and copies ran while one was open for 34% of the time, Pallas kernels for 17%

profile of v3, /device:TPU:0, one launch (start us, length us, event | category | flops | bytes accessed | tf_op | source)
XLA Modules:
  0.0 365.7 jit_solution(2019353287450176016)
XLA Ops:
  11.7 3.0 collective-permute-start.1
  22.2 3.6 collective-permute-start.14
  26.7 1.9 collective-permute-start.5
  28.7 2.4 collective-permute-start.2
  31.4 2.4 fusion.24
  37.2 7.4 %collective-permute-done.2 = bf16[128,1024]{1,0:T(8,128)(2,1)} collective-permute-done((bf16[128,1024]{1,0:T(8,128)(2,1)S(1)}, bf16[128,1024]{1,0:T(8,128)(2,1)}, u32[]{:S(2)}, u32[]{:S(2)}) %collective-permute-start.2) | collective-permute-done | bytes 262176 | tf_op jit(solution)/shard_map/ppermute | solution.py:22
  47.1 1.9 constant_dynamic-update-slice_fusion.5
  49.0 7.2 %collective-permute-done.3 = bf16[128,1024]{1,0:T(8,128)(2,1)S(1)} collective-permute-done((bf16[128,1024]{1,0:T(8,128)(2,1)}, bf16[128,1024]{1,0:T(8,128)(2,1)S(1)}, u32[]{:S(2)}, u32[]{:S(2)}) %collective-permute-start.3) | collective-permute-done | bytes 262176 | tf_op jit(solution)/shard_map/ppermute | solution.py:22
  56.8 2.6 concatenate.225
  60.6 3.0 collective-permute-start.11
  68.1 7.5 %collective-permute-done.7 = bf16[128,1024]{1,0:T(8,128)(2,1)S(1)} collective-permute-done((bf16[128,1024]{1,0:T(8,128)(2,1)S(1)}, bf16[128,1024]{1,0:T(8,128)(2,1)S(1)}, u32[]{:S(2)}, u32[]{:S(2)}) %collective-permute-start.7) | collective-permute-done | bytes 262176 | tf_op jit(solution)/shard_map/ppermute | solution.py:17
  77.1 2.2 collective-permute-start.12
  79.3 2.4 fusion.40
  85.6 4.4 %collective-permute-done.12 = bf16[272,1024]{1,0:T(8,128)(2,1)S(1)} collective-permute-done((bf16[272,1024]{1,0:T(8,128)(2,1)S(1)}, bf16[272,1024]{1,0:T(8,128)(2,1)S(1)}, u32[]{:S(2)}, u32[]{:S(2)}) %collective-permute-start.12) | collective-permute-done | bytes 557088 | tf_op jit(solution)/shard_map/ppermute | solution.py:17
  105.7 1.7 collective-permute-start.16
  111.9 13.4 %shard_map.169 = (f32[512,1024]{1,0:T(8,128)}, f32[512,1024]{1,0:T(8,128)}, f32[512,1024]{1,0:T(8,128)}, f32[512,1024]{1,0:T(8,128)}, bf16[2048,1024]{1,0:T(8,12...) custom-call(bf16[512,1024]{1,0:T(8,128)(2,1)S(1)} %multiply_convert_fusion.refs_0_, ...), custom_call_target="tpu_custom_call" | custom-call | flops 6442450944 | bytes 15728640 | tf_op jit(solution)/shard_map/pallas_call | solution.py:156
  125.4 6.0 %collective-permute-done.16.refs_0_ = bf16[512,1024]{1,0:T(8,128)(2,1)} collective-permute-done((bf16[512,1024]{1,0:T(8,128)(2,1)S(1)}, bf16[512,1024]{1,0:T(8,128)(2,1)}, u32[]{:S(2)}, u32[]{:S(2)}) %collective-permute-start.16) | collective-permute-done | bytes 1048608 | tf_op jit(solution)/shard_map/ppermute | solution.py:17
  131.9 3.8 %collective-permute-done.19.refs_1_ = bf16[512,1024]{1,0:T(8,128)(2,1)S(1)} collective-permute-done((bf16[512,1024]{1,0:T(8,128)(2,1)}, bf16[512,1024]{1,0:T(8,128)(2,1)S(1)}, u32[]{:S(2)}, u32[]{:S(2)}) %collective-permute-start.19) | collective-permute-done | bytes 1048608 | tf_op jit(solution)/shard_map/ppermute | solution.py:17
  135.7 14.2 %shard_map.170 = (f32[512,1024]{1,0:T(8,128)}, f32[512,1024]{1,0:T(8,128)}, f32[512,1024]{1,0:T(8,128)}, f32[512,1024]{1,0:T(8,128)}, bf16[2048,1024]{1,0:T(8,12...) custom-call(bf16[512,1024]{1,0:T(8,128)(2,1)} %collective-permute-do, ...), custom_call_target="tpu_custom_call", output_to_operand_aliasing={{4}: (5, {}), {5}: (6, {}), {6}: (7, {}), {7}: (8, {})} | custom-call | flops 6442450944 | bytes 15728640 | tf_op jit(solution)/shard_map/pallas_call | solution.py:156
  149.9 9.5 %convolution_convert_fusion.2 = bf16[1024,1024]{0,1:T(8,128)(2,1)} fusion(bf16[2048,1024]{1,0:T(8,128)(2,1)} %get-tuple-element.103, bf16[2048,1024]{1,0:T(8,128)(2,1)} %get-tuple-element.104), kind=kOutput, calls=%fused_computation.60 | convolution fusion | flops 4296015872 | bytes 10485760 | tf_op jit(solution)/shard_map/dot_general | solution.py:42
  159.6 4.7 %convolution_convert_fusion.8 = bf16[1024,512]{0,1:T(8,128)(2,1)S(1)} fusion(bf16[2048,1024]{1,0:T(8,128)(2,1)} %get-tuple-element.130, bf16[2048,512]{1,0:T(8,128)(2,1)S(1)} %copy-done.92), kind=kOutput, calls=%fused_computation.69 | convolution fusion | flops 2148007936 | bytes 7340032 | tf_op jit(solution)/shard_map/dot_general | solution.py:42
  164.6 3.0 copy.71
  167.7 17.1 %shard_map.171 = (bf16[512,1024]{1,0:T(8,128)(2,1)S(1)}, bf16[512,1024]{1,0:T(8,128)(2,1)S(1)}, bf16[512,1024]{1,0:T(8,128)(2,1)}, bf16[512,1024]{1,0:T(8,128)(2...) custom-call(bf16[512,1024]{1,0:T(8,128)(2,1)} %collective-permute-done.16.refs_0_, ...), custom_call_target="tpu_custom_call" | custom-call | flops 8053063680 | bytes 16515072 | tf_op jit(solution)/shard_map/pallas_call | solution.py:156
  185.5 2.3 slice.652
  191.2 16.4 %shard_map.172 = (bf16[512,1024]{1,0:T(8,128)(2,1)S(1)}, bf16[512,1024]{1,0:T(8,128)(2,1)S(1)}, bf16[512,1024]{1,0:T(8,128)(2,1)}, bf16[512,1024]{1,0:T(8,128)(2...) custom-call(bf16[512,1024]{1,0:T(8,128)(2,1)S(1)} %copy-done.3, ...), custom_call_target="tpu_custom_call", output_to_operand_aliasing={{4}: (9, {}), {5}: (10, {})} | custom-call | flops 8053063680 | bytes 16515072 | tf_op jit(solution)/shard_map/pallas_call | solution.py:156
  207.7 9.7 %convolution_convert_fusion = bf16[1024,1280]{1,0:T(8,128)(2,1)S(1)} fusion(bf16[2048,1024]{1,0:T(8,128)(2,1)} %get-tuple-element.103, bf16[2048,1280]{1,0:T(8,128)(2,1)} %get-tuple-element.129), kind=kOutput, calls=%fused_computation.11 | convolution fusion | flops 5370019840 | bytes 12058624 | tf_op jit(solution)/shard_map/dot_general | solution.py:42
  217.4 3.5 convolution_convert_fusion.3
  220.9 2.2 pad_maximum_fusion
  223.2 2.4 convert_add_fusion.3
  227.6 1.7 fusion.26
  233.0 2.1 multiply_reduce_fusion.5
  260.3 2.5 fusion.189
  264.4 3.3 fusion.17
  269.0 1.8 collective-permute-start.34
  270.8 2.8 add_convert_fusion.2
  273.6 2.7 collective-permute-done.34
  276.9 5.8 %collective-permute-done.35 = f32[5,1024]{1,0:T(8,128)S(1)} collective-permute-done((f32[5,1024]{1,0:T(8,128)S(1)}, f32[5,1024]{1,0:T(8,128)S(1)}, u32[]{:S(2)}, u32[]{:S(2)}) %collective-permute-start.35) | collective-permute-done | bytes 20512 | tf_op jit(solution)/shard_map/ppermute | solution.py:22
  287.6 1.8 collective-permute-start.31
  290.0 1.9 slice_add_fusion
  292.9 7.8 %collective-permute-done.31 = bf16[512,512]{0,1:T(8,128)(2,1)S(1)} collective-permute-done((bf16[512,512]{0,1:T(8,128)(2,1)S(1)}, bf16[512,512]{0,1:T(8,128)(2,1)S(1)}, u32[]{:S(2)}, u32[]{:S(2)}) %collective-permute-start.31) | collective-permute-done | bytes 524320 | tf_op jit(solution)/shard_map/ppermute | solution.py:17
  302.0 1.8 collective-permute-start.32
  305.0 5.2 %collective-permute-done.39 = bf16[512,512]{0,1:T(8,128)(2,1)S(1)} collective-permute-done((bf16[512,512]{0,1:T(8,128)(2,1)S(1)}, bf16[512,512]{0,1:T(8,128)(2,1)S(1)}, u32[]{:S(2)}, u32[]{:S(2)}) %collective-permute-start.39) | collective-permute-done | bytes 524320 | tf_op jit(solution)/shard_map/ppermute | solution.py:17
  311.5 3.1 collective-permute-start.40
  315.8 1.9 slice.700
  317.7 2.3 reshape.754
  320.0 5.7 %collective-permute-done.32 = bf16[512,1024]{1,0:T(8,128)(2,1)} collective-permute-done((bf16[512,1024]{1,0:T(8,128)(2,1)}, bf16[512,1024]{1,0:T(8,128)(2,1)}, u32[]{:S(2)}, u32[]{:S(2)}) %collective-permute-start.32) | collective-permute-done | bytes 1048608 | tf_op jit(solution)/shard_map/ppermute | solution.py:17
  325.7 5.4 %fusion.16 = (f32[512,1024]{1,0:T(8,128)}, bf16[512,1024]{1,0:T(8,128)(2,1)}) fusion(bf16[512,1024]{1,0:T(8,128)(2,1)S(1)} %copy-done.43, f32[512,1024]{1,0:T(8,128)} %get-tuple-element.301, f32[512]{0:T(512)} %broadcast_multiply_fusion, f32[1024]{0:T(1024)S(1)} %convert_element_type.220, f32[512]{0:T(512)S(1)} %copy-done.83, f32[512]{0:T(512)} %copy-done.84, ...), kind=kLoop, calls=%fused_computation.30 | loop fusion | flops 11010048 | bytes 14696448 | tf_op jit(solution)/shard_map/add | solution.py:394
  331.2 20.6 %collective-permute-done.41 = bf16[128,1024]{0,1:T(8,128)(2,1)} collective-permute-done((bf16[128,1024]{0,1:T(8,128)(2,1)}, bf16[128,1024]{0,1:T(8,128)(2,1)}, u32[]{:S(2)}, u32[]{:S(2)}) %collective-permute-start.41) | collective-permute-done | bytes 262176 | tf_op jit(solution)/shard_map/ppermute | solution.py:22
  (402 shorter events, 106.8 us)
Async XLA Ops:
  7.2 102.3 %all-gather.3.cloned.1.call-start = ((), (), s32[]{:S(2)}) async-start(), calls=%async_computation.2 | async-start | bytes 3538944 | tf_op jit(solution)/shard_map/all_gather | solution.py:220
  10.6 149.0 %all-gather.5.cloned.1.call-start = ((), (), s32[]{:S(2)}) async-start(), calls=%async_computation.3 | async-start | bytes 4423680 | tf_op jit(solution)/shard_map/all_gather | solution.py:220
  11.7 14.1 %collective-permute-start.1 = (bf16[128,1024]{1,0:T(8,128)(2,1)S(1)}, bf16[128,1024]{1,0:T(8,128)(2,1)S(1)}, u32[]{:S(2)}, u32[]{:S(2)}) collective-permute-start(bf16[128,1024]{1,0:T(8,128)(2,1)S(1)} %get-tuple-element.249), channel_id=1, source_target_pairs={{0,8},{4,12},{8,16},{12,20},{16,24},{20,28},{24,0},{28,4},{1,9},{5... | collective-permute-start | bytes 786440 | tf_op jit(solution)/shard_map/ppermute | solution.py:22
  14.7 11.1 %collective-permute-start.4 = (bf16[128,1024]{1,0:T(8,128)(2,1)S(1)}, bf16[128,1024]{1,0:T(8,128)(2,1)S(1)}, u32[]{:S(2)}, u32[]{:S(2)}) collective-permute-start(bf16[128,1024]{1,0:T(8,128)(2,1)S(1)} %get-tuple-element.249), channel_id=1, source_target_pairs={{0,4},{4,0},{8,12},{12,8},{16,20},{20,16},{24,28},{28,24},{1,5},{5... | collective-permute-start | bytes 786440 | tf_op jit(solution)/shard_map/ppermute | solution.py:17
  19.0 3.1 collective-permute-start
  22.2 82.0 %collective-permute-start.14 = (bf16[256,1024]{1,0:T(8,128)(2,1)}, bf16[256,1024]{1,0:T(8,128)(2,1)}, u32[]{:S(2)}, u32[]{:S(2)}) collective-permute-start(bf16[256,1024]{1,0:T(8,128)(2,1)} %get-tuple-element.90), channel_id=1, source_target_pairs={{0,2},{1,3},{2,0},{3,1},{4,6},{5,7},{6,4},{7,5},{8,10},{9,11},{10,... | collective-permute-start | bytes 1572872 | tf_op jit(solution)/shard_map/ppermute | solution.py:17
  26.7 40.4 %collective-permute-start.9 = (bf16[256,1024]{1,0:T(8,128)(2,1)}, bf16[256,1024]{1,0:T(8,128)(2,1)}, u32[]{:S(2)}, u32[]{:S(2)}) collective-permute-start(bf16[256,1024]{1,0:T(8,128)(2,1)} %pad_maximum_fusion.16), channel_id=1, source_target_pairs={{0,2},{1,3},{2,0},{3,1},{4,6},{5,7},{6,4},{7,5},{8,10},{9,11},{10,... | collective-permute-start | bytes 1572872 | tf_op jit(solution)/shard_map/ppermute | solution.py:17
  26.7 8.4 %collective-permute-start.5 = (bf16[128,1024]{1,0:T(8,128)(2,1)S(1)}, bf16[128,1024]{1,0:T(8,128)(2,1)S(1)}, u32[]{:S(2)}, u32[]{:S(2)}) collective-permute-start(bf16[128,1024]{1,0:T(8,128)(2,1)S(1)} %collective-permute-done.1), channel_id=1, source_target_pairs={{0,4},{4,0},{8,12},{12,8},{16,20},{20,16},{24,28},{28,24},{1,5},{5... | collective-permute-start | bytes 786440 | tf_op jit(solution)/shard_map/ppermute | solution.py:17
  28.7 15.9 %collective-permute-start.2 = (bf16[128,1024]{1,0:T(8,128)(2,1)S(1)}, bf16[128,1024]{1,0:T(8,128)(2,1)}, u32[]{:S(2)}, u32[]{:S(2)}) collective-permute-start(bf16[128,1024]{1,0:T(8,128)(2,1)S(1)} %collective-permute-done.1), channel_id=1, source_target_pairs={{0,8},{4,12},{8,16},{12,20},{16,24},{20,28},{24,0},{28,4},{1,9},{5... | collective-permute-start | bytes 786440 | tf_op jit(solution)/shard_map/ppermute | solution.py:22
  36.0 45.8 %collective-permute-start.10 = (bf16[256,1024]{1,0:T(8,128)(2,1)}, bf16[256,1024]{1,0:T(8,128)(2,1)}, u32[]{:S(2)}, u32[]{:S(2)}) collective-permute-start(bf16[256,1024]{1,0:T(8,128)(2,1)} %pad_maximum_fusion.17), channel_id=1, source_target_pairs={{0,2},{1,3},{2,0},{3,1},{4,6},{5,7},{6,4},{7,5},{8,10},{9,11},{10,... | collective-permute-start | bytes 1572872 | tf_op jit(solution)/shard_map/ppermute | solution.py:17
  44.9 11.3 %collective-permute-start.3 = (bf16[128,1024]{1,0:T(8,128)(2,1)}, bf16[128,1024]{1,0:T(8,128)(2,1)S(1)}, u32[]{:S(2)}, u32[]{:S(2)}) collective-permute-start(bf16[128,1024]{1,0:T(8,128)(2,1)} %collective-permute-done.2), channel_id=1, source_target_pairs={{0,8},{4,12},{8,16},{12,20},{16,24},{20,28},{24,0},{28,4},{1,9},{5... | collective-permute-start | bytes 786440 | tf_op jit(solution)/shard_map/ppermute | solution.py:22
  45.9 269.9 %reduce-scatter.7.cloned.1.call-start = ((), (), s32[]{:S(2)}) async-start(), calls=%async_computation.5 | async-start | bytes 3538944 | tf_op jit(solution)/shard_map/reduce_scatter | solution.py:290
  46.1 20.2 %collective-permute-start.6 = (bf16[128,1024]{1,0:T(8,128)(2,1)}, bf16[128,1024]{1,0:T(8,128)(2,1)S(1)}, u32[]{:S(2)}, u32[]{:S(2)}) collective-permute-start(bf16[128,1024]{1,0:T(8,128)(2,1)} %collective-permute-done.2), channel_id=1, source_target_pairs={{0,4},{4,0},{8,12},{12,8},{16,20},{20,16},{24,28},{28,24},{1,5},{5... | collective-permute-start | bytes 786440 | tf_op jit(solution)/shard_map/ppermute | solution.py:17
  60.6 22.8 %collective-permute-start.11 = (bf16[256,1024]{1,0:T(8,128)(2,1)S(1)}, bf16[256,1024]{1,0:T(8,128)(2,1)S(1)}, u32[]{:S(2)}, u32[]{:S(2)}) collective-permute-start(bf16[256,1024]{1,0:T(8,128)(2,1)S(1)} %pad_maximum_fusion.18), channel_id=1, source_target_pairs={{0,2},{1,3},{2,0},{3,1},{4,6},{5,7},{6,4},{7,5},{8,10},{9,11},{10,... | collective-permute-start | bytes 1572872 | tf_op jit(solution)/shard_map/ppermute | solution.py:17
  66.3 9.3 %collective-permute-start.7 = (bf16[128,1024]{1,0:T(8,128)(2,1)S(1)}, bf16[128,1024]{1,0:T(8,128)(2,1)S(1)}, u32[]{:S(2)}, u32[]{:S(2)}) collective-permute-start(bf16[128,1024]{1,0:T(8,128)(2,1)S(1)} %collective-permute-done.3), channel_id=1, source_target_pairs={{0,4},{4,0},{8,12},{12,8},{16,20},{20,16},{24,28},{28,24},{1,5},{5... | collective-permute-start | bytes 786440 | tf_op jit(solution)/shard_map/ppermute | solution.py:17
  77.1 12.9 %collective-permute-start.12 = (bf16[272,1024]{1,0:T(8,128)(2,1)S(1)}, bf16[272,1024]{1,0:T(8,128)(2,1)S(1)}, u32[]{:S(2)}, u32[]{:S(2)}) collective-permute-start(bf16[272,1024]{1,0:T(8,128)(2,1)S(1)} %pad_maximum_fusion.11), channel_id=1, source_target_pairs={{0,2},{1,3},{2,0},{3,1},{4,6},{5,7},{6,4},{7,5},{8,10},{9,11},{10,... | collective-permute-start | bytes 1671176 | tf_op jit(solution)/shard_map/ppermute | solution.py:17
  79.3 12.4 %collective-permute-start.8 = (bf16[1040,1024]{1,0:T(8,128)(2,1)}, bf16[1040,1024]{1,0:T(8,128)(2,1)S(1)}, u32[]{:S(2)}, u32[]{:S(2)}) collective-permute-start(bf16[1040,1024]{1,0:T(8,128)(2,1)} %get-tuple-element.293), channel_id=1, source_target_pairs={{0,1},{1,0},{2,3},{3,2},{4,5},{5,4},{6,7},{7,6},{8,9},{9,8},{10,11... | collective-permute-start | bytes 6389768 | tf_op jit(solution)/shard_map/ppermute | solution.py:17
  81.7 25.7 %collective-permute-start.18 = (bf16[512,1024]{1,0:T(8,128)(2,1)S(1)}, bf16[512,1024]{1,0:T(8,128)(2,1)S(1)}, u32[]{:S(2)}, u32[]{:S(2)}) collective-permute-start(bf16[512,1024]{1,0:T(8,128)(2,1)S(1)} %copy-done), channel_id=1, source_target_pairs={{0,1},{1,0},{2,3},{3,2},{4,5},{5,4},{6,7},{7,6},{8,9},{9,8},{10,11... | collective-permute-start | bytes 3145736 | tf_op jit(solution)/shard_map/ppermute | solution.py:17
  90.0 5.1 %collective-permute-start.13 = (bf16[1040,1024]{1,0:T(8,128)(2,1)S(1)}, bf16[1040,1024]{1,0:T(8,128)(2,1)S(1)}, u32[]{:S(2)}, u32[]{:S(2)}) collective-permute-start(bf16[1040,1024]{1,0:T(8,128)(2,1)S(1)} %constant_dynamic-update-slice_fusion.17), channel_id=1, source_target_pairs={{0,1},{1,0},{2,3},{3,2},{4,5},{5,4},{6,7},{7,6},{8,9},{9,8},{10,11... | collective-permute-start | bytes 6389768 | tf_op jit(solution)/shard_map/ppermute | solution.py:17
  90.1 15.6 %collective-permute-start.15 = (bf16[256,1024]{1,0:T(8,128)(2,1)S(1)}, bf16[256,1024]{1,0:T(8,128)(2,1)S(1)}, u32[]{:S(2)}, u32[]{:S(2)}) collective-permute-start(bf16[256,1024]{1,0:T(8,128)(2,1)S(1)} %copy-done.63), channel_id=1, source_target_pairs={{0,2},{1,3},{2,0},{3,1},{4,6},{5,7},{6,4},{7,5},{8,10},{9,11},{10,... | collective-permute-start | bytes 1572872 | tf_op jit(solution)/shard_map/ppermute | solution.py:17
  104.0 4.4 %collective-permute-start.17 = (bf16[512,1024]{1,0:T(8,128)(2,1)S(1)}, bf16[512,1024]{1,0:T(8,128)(2,1)S(1)}, u32[]{:S(2)}, u32[]{:S(2)}) collective-permute-start(bf16[512,1024]{1,0:T(8,128)(2,1)S(1)} %multiply_convert_fusion.refs_0_), channel_id=1, source_target_pairs={{0,1},{1,0},{2,3},{3,2},{4,5},{5,4},{6,7},{7,6},{8,9},{9,8},{10,11... | collective-permute-start | bytes 3145736 | tf_op jit(solution)/shard_map/ppermute | solution.py:17
  105.7 30.0 %copy-start.4 = (bf16[512,1024]{1,0:T(8,128)(2,1)}, bf16[512,1024]{1,0:T(8,128)(2,1)S(1)}, u32[]{:S(2)}) copy-start(bf16[512,1024]{1,0:T(8,128)(2,1)S(1)} %constant_dynamic-update-slice_fusion.19.refs_2_) | copy-start | bytes 3145732
  105.7 25.6 %collective-permute-start.16 = (bf16[512,1024]{1,0:T(8,128)(2,1)S(1)}, bf16[512,1024]{1,0:T(8,128)(2,1)}, u32[]{:S(2)}, u32[]{:S(2)}) collective-permute-start(bf16[512,1024]{1,0:T(8,128)(2,1)S(1)} %multiply_convert_fusion.refs_0_), channel_id=1, source_target_pairs={{0,2},{1,3},{2,0},{3,1},{4,6},{5,7},{6,4},{7,5},{8,10},{9,11},{10,... | collective-permute-start | bytes 3145736 | tf_op jit(solution)/shard_map/ppermute | solution.py:17
  131.3 4.3 %collective-permute-start.19 = (bf16[512,1024]{1,0:T(8,128)(2,1)}, bf16[512,1024]{1,0:T(8,128)(2,1)S(1)}, u32[]{:S(2)}, u32[]{:S(2)}) collective-permute-start(bf16[512,1024]{1,0:T(8,128)(2,1)} %collective-permute-done.16.refs_0_), channel_id=1, source_target_pairs={{0,1},{1,0},{2,3},{3,2},{4,5},{5,4},{6,7},{7,6},{8,9},{9,8},{10,11... | collective-permute-start | bytes 3145736 | tf_op jit(solution)/shard_map/ppermute | solution.py:17
  131.4 4.3 %collective-permute-start.20 = (bf16[512,1024]{1,0:T(8,128)(2,1)S(1)}, bf16[512,1024]{1,0:T(8,128)(2,1)S(1)}, u32[]{:S(2)}, u32[]{:S(2)}) collective-permute-start(bf16[512,1024]{1,0:T(8,128)(2,1)S(1)} %constant_dynamic-update-slice_fusion.19.refs_2_), channel_id=1, source_target_pairs={{0,1},{1,0},{2,3},{3,2},{4,5},{5,4},{6,7},{7,6},{8,9},{9,8},{10,11... | collective-permute-start | bytes 3145736 | tf_op jit(solution)/shard_map/ppermute | solution.py:17
  167.6 187.0 %reduce-scatter.5.cloned.1.call-start = ((), (), s32[]{:S(2)}) async-start(), calls=%async_computation.4 | async-start | bytes 4423680 | tf_op jit(solution)/shard_map/reduce_scatter | solution.py:290
  184.8 3.5 collective-permute-start.21
  187.8 83.0 %collective-permute-start.23 = (bf16[512,1024]{1,0:T(8,128)(2,1)}, bf16[512,1024]{1,0:T(8,128)(2,1)}, u32[]{:S(2)}, u32[]{:S(2)}) collective-permute-start(bf16[512,1024]{1,0:T(8,128)(2,1)} %get-tuple-element.125), channel_id=1, source_target_pairs={{0,1},{1,0},{2,3},{3,2},{4,5},{5,4},{6,7},{7,6},{8,9},{9,8},{10,11... | collective-permute-start | bytes 3145736 | tf_op jit(solution)/shard_map/ppermute | solution.py:17
  189.7 33.4 %collective-permute-start.25 = (bf16[512,1024]{1,0:T(8,128)(2,1)}, bf16[512,1024]{1,0:T(8,128)(2,1)}, u32[]{:S(2)}, u32[]{:S(2)}) collective-permute-start(bf16[512,1024]{1,0:T(8,128)(2,1)} %add_convert_fusion.1), channel_id=1, source_target_pairs={{0,2},{1,3},{2,0},{3,1},{4,6},{5,7},{6,4},{7,5},{8,10},{9,11},{10,... | collective-permute-start | bytes 3145736 | tf_op jit(solution)/shard_map/ppermute | solution.py:17
  207.6 15.6 %collective-permute-start.24 = (bf16[512,1024]{1,0:T(8,128)(2,1)}, bf16[512,1024]{1,0:T(8,128)(2,1)}, u32[]{:S(2)}, u32[]{:S(2)}) collective-permute-start(bf16[512,1024]{1,0:T(8,128)(2,1)} %get-tuple-element.127), channel_id=1, source_target_pairs={{0,1},{1,0},{2,3},{3,2},{4,5},{5,4},{6,7},{7,6},{8,9},{9,8},{10,11... | collective-permute-start | bytes 3145736 | tf_op jit(solution)/shard_map/ppermute | solution.py:17
  238.2 4.5 %collective-permute-start.28 = (f32[4,2,256]{2,1,0:T(2,128)S(1)}, f32[4,2,256]{2,1,0:T(2,128)S(1)}, u32[]{:S(2)}, u32[]{:S(2)}) collective-permute-start(f32[4,2,256]{2,1,0:T(2,128)S(1)} %pad_maximum_fusion.24), channel_id=1, source_target_pairs={{1,0},{2,1},{3,2},{4,3},{5,4},{6,5},{7,6},{8,7},{9,8},{10,9},{11,1... | collective-permute-start | bytes 24584 | tf_op jit(solution)/shard_map/ppermute | solution.py:28
  240.6 6.4 %collective-permute-start.26 = (bf16[1024,1024]{0,1:T(8,128)(2,1)S(1)}, bf16[1024,1024]{0,1:T(8,128)(2,1)S(1)}, u32[]{:S(2)}, u32[]{:S(2)}) collective-permute-start(bf16[1024,1024]{0,1:T(8,128)(2,1)S(1)} %pad_maximum_fusion.4), channel_id=1, source_target_pairs={{0,1},{1,0},{2,3},{3,2},{4,5},{5,4},{6,7},{7,6},{8,9},{9,8},{10,11... | collective-permute-start | bytes 6291464 | tf_op jit(solution)/shard_map/ppermute | solution.py:17
  245.5 7.4 %collective-permute-start.29 = (bf16[1024,1024]{0,1:T(8,128)(2,1)S(1)}, bf16[1024,1024]{0,1:T(8,128)(2,1)S(1)}, u32[]{:S(2)}, u32[]{:S(2)}) collective-permute-start(bf16[1024,1024]{0,1:T(8,128)(2,1)S(1)} %convolution_convert_fusion.1), channel_id=1, source_target_pairs={{0,1},{1,0},{2,3},{3,2},{4,5},{5,4},{6,7},{7,6},{8,9},{9,8},{10,11... | collective-permute-start | bytes 6291464 | tf_op jit(solution)/shard_map/ppermute | solution.py:17
  251.8 34.2 %collective-permute-start.27 = (bf16[1024,512]{0,1:T(8,128)(2,1)}, bf16[1024,512]{0,1:T(8,128)(2,1)}, u32[]{:S(2)}, u32[]{:S(2)}) collective-permute-start(bf16[1024,512]{0,1:T(8,128)(2,1)} %pad_maximum_fusion.9), channel_id=1, source_target_pairs={{0,4},{4,0},{8,12},{12,8},{16,20},{20,16},{24,28},{28,24},{1,5},{5... | collective-permute-start | bytes 3145736 | tf_op jit(solution)/shard_map/ppermute | solution.py:17
  255.6 30.7 %collective-permute-start.30 = (bf16[1024,512]{0,1:T(8,128)(2,1)}, bf16[1024,512]{0,1:T(8,128)(2,1)}, u32[]{:S(2)}, u32[]{:S(2)}) collective-permute-start(bf16[1024,512]{0,1:T(8,128)(2,1)} %slice.1027), channel_id=1, source_target_pairs={{0,2},{1,3},{2,0},{3,1},{4,6},{5,7},{6,4},{7,5},{8,10},{9,11},{10,... | collective-permute-start | bytes 3145736 | tf_op jit(solution)/shard_map/ppermute | solution.py:17
  267.7 1.3 collective-permute-start.33
  267.8 52.2 %collective-permute-start.22 = (bf16[512,1024]{1,0:T(8,128)(2,1)}, bf16[512,1024]{1,0:T(8,128)(2,1)}, u32[]{:S(2)}, u32[]{:S(2)}) collective-permute-start(bf16[512,1024]{1,0:T(8,128)(2,1)} %copy-done.5), channel_id=1, source_target_pairs={{0,1},{1,0},{2,3},{3,2},{4,5},{5,4},{6,7},{7,6},{8,9},{9,8},{10,11... | collective-permute-start | bytes 3145736 | tf_op jit(solution)/shard_map/ppermute | solution.py:17
  269.0 7.3 %collective-permute-start.34 = (f32[5,1024]{1,0:T(8,128)S(1)}, f32[5,1024]{1,0:T(8,128)S(1)}, u32[]{:S(2)}, u32[]{:S(2)}) collective-permute-start(f32[5,1024]{1,0:T(8,128)S(1)} %fusion.169), channel_id=1, source_target_pairs={{0,16},{4,20},{8,24},{12,28},{16,0},{20,4},{24,8},{28,12},{1,17},{... | collective-permute-start | bytes 61448 | tf_op jit(solution)/shard_map/ppermute | solution.py:22
  276.4 6.4 %collective-permute-start.35 = (f32[5,1024]{1,0:T(8,128)S(1)}, f32[5,1024]{1,0:T(8,128)S(1)}, u32[]{:S(2)}, u32[]{:S(2)}) collective-permute-start(f32[5,1024]{1,0:T(8,128)S(1)} %add.307), channel_id=1, source_target_pairs={{0,8},{4,12},{8,16},{12,20},{16,24},{20,28},{24,0},{28,4},{1,9},{5... | collective-permute-start | bytes 61448 | tf_op jit(solution)/shard_map/ppermute | solution.py:22
  282.8 6.6 %collective-permute-start.38 = (f32[5,1024]{1,0:T(8,128)S(1)}, f32[5,1024]{1,0:T(8,128)S(1)}, u32[]{:S(2)}, u32[]{:S(2)}) collective-permute-start(f32[5,1024]{1,0:T(8,128)S(1)} %add.308), channel_id=1, source_target_pairs={{0,6},{1,7},{2,4},{3,5},{4,2},{5,3},{6,0},{7,1},{8,14},{9,15},{10,... | collective-permute-start | bytes 61448 | tf_op jit(solution)/shard_map/ppermute | solution.py:34
  283.3 6.1 %collective-permute-start.37 = (f32[5,1024]{1,0:T(8,128)S(1)}, f32[5,1024]{1,0:T(8,128)S(1)}, u32[]{:S(2)}, u32[]{:S(2)}) collective-permute-start(f32[5,1024]{1,0:T(8,128)S(1)} %add.308), channel_id=1, source_target_pairs={{0,2},{1,3},{2,0},{3,1},{4,6},{5,7},{6,4},{7,5},{8,10},{9,11},{10,... | collective-permute-start | bytes 61448 | tf_op jit(solution)/shard_map/ppermute | solution.py:17
  286.0 3.9 %collective-permute-start.36 = (f32[5,1024]{1,0:T(8,128)S(1)}, f32[5,1024]{1,0:T(8,128)S(1)}, u32[]{:S(2)}, u32[]{:S(2)}) collective-permute-start(f32[5,1024]{1,0:T(8,128)S(1)} %add.308), channel_id=1, source_target_pairs={{0,4},{4,0},{8,12},{12,8},{16,20},{20,16},{24,28},{28,24},{1,5},{5... | collective-permute-start | bytes 61448 | tf_op jit(solution)/shard_map/ppermute | solution.py:17
  287.6 13.1 %collective-permute-start.31 = (bf16[512,512]{0,1:T(8,128)(2,1)S(1)}, bf16[512,512]{0,1:T(8,128)(2,1)S(1)}, u32[]{:S(2)}, u32[]{:S(2)}) collective-permute-start(bf16[512,512]{0,1:T(8,128)(2,1)S(1)} %fusion.51), channel_id=1, source_target_pairs={{0,2},{1,3},{2,0},{3,1},{4,6},{5,7},{6,4},{7,5},{8,10},{9,11},{10,... | collective-permute-start | bytes 1572872 | tf_op jit(solution)/shard_map/ppermute | solution.py:17
  291.9 18.3 %collective-permute-start.39 = (bf16[512,512]{0,1:T(8,128)(2,1)S(1)}, bf16[512,512]{0,1:T(8,128)(2,1)S(1)}, u32[]{:S(2)}, u32[]{:S(2)}) collective-permute-start(bf16[512,512]{0,1:T(8,128)(2,1)S(1)} %slice.1028), channel_id=1, source_target_pairs={{0,4},{4,0},{8,12},{12,8},{16,20},{20,16},{24,28},{28,24},{1,5},{5... | collective-permute-start | bytes 1572872 | tf_op jit(solution)/shard_map/ppermute | solution.py:17
  302.0 23.7 %collective-permute-start.32 = (bf16[512,1024]{1,0:T(8,128)(2,1)}, bf16[512,1024]{1,0:T(8,128)(2,1)}, u32[]{:S(2)}, u32[]{:S(2)}) collective-permute-start(bf16[512,1024]{1,0:T(8,128)(2,1)} %add_convert_fusion.2), channel_id=1, source_target_pairs={{0,2},{1,3},{2,0},{3,1},{4,6},{5,7},{6,4},{7,5},{8,10},{9,11},{10,... | collective-permute-start | bytes 3145736 | tf_op jit(solution)/shard_map/ppermute | solution.py:17
  311.5 19.7 %collective-permute-start.40 = (bf16[128,1024]{0,1:T(8,128)(2,1)}, bf16[128,1024]{0,1:T(8,128)(2,1)}, u32[]{:S(2)}, u32[]{:S(2)}) collective-permute-start(bf16[128,1024]{0,1:T(8,128)(2,1)} %get-tuple-element.218), channel_id=1, source_target_pairs={{0,24},{4,28},{8,0},{12,4},{16,8},{20,12},{24,16},{28,20},{1,25},{... | collective-permute-start | bytes 786440 | tf_op jit(solution)/shard_map/ppermute | solution.py:22
  314.6 37.2 %collective-permute-start.41 = (bf16[128,1024]{0,1:T(8,128)(2,1)}, bf16[128,1024]{0,1:T(8,128)(2,1)}, u32[]{:S(2)}, u32[]{:S(2)}) collective-permute-start(bf16[128,1024]{0,1:T(8,128)(2,1)} %get-tuple-element.217), channel_id=1, source_target_pairs={{0,16},{4,20},{8,24},{12,28},{16,0},{20,4},{24,8},{28,12},{1,17},{... | collective-permute-start | bytes 786440 | tf_op jit(solution)/shard_map/ppermute | solution.py:22
  314.6 37.2 %collective-permute-start.42 = (bf16[128,1024]{0,1:T(8,128)(2,1)}, bf16[128,1024]{0,1:T(8,128)(2,1)}, u32[]{:S(2)}, u32[]{:S(2)}) collective-permute-start(bf16[128,1024]{0,1:T(8,128)(2,1)} %get-tuple-element.216), channel_id=1, source_target_pairs={{0,8},{4,12},{8,16},{12,20},{16,24},{20,28},{24,0},{28,4},{1,9},{5... | collective-permute-start | bytes 786440 | tf_op jit(solution)/shard_map/ppermute | solution.py:22
  (92 other events, 521.9 us)
Sparse Core Ops, SparseCore 0:
  10.8 75.8 all-gather.2
  88.9 70.6 all-gather.4
  167.8 72.8 reduce-scatter.6
  244.1 109.1 reduce-scatter.4

commit v4 on v3

--- a/solution.py
+++ b/solution.py
@@ -283,10 +283,14 @@
     hid_y = swap(after(hidden_two, cot_y), "tensor", 2)
     tile = min(rows // 2, 256)
 
-    def weight_grads(d_gu, act, *earlier):
-        grad_gu = tn(hid_all, d_gu).astype(BF)
-        grads = after(cot_all, grad_gu, *earlier)
-        grads = jnp.concatenate([grad_gu, tn(grads, act).astype(BF)], axis=1)
+    def weight_grads(d_gu, act, *late):
+        if late:
+            grad_down = tn(cot_all, act).astype(BF)
+            grad_gu = tn(after(hid_all, grad_down), d_gu).astype(BF)
+        else:
+            grad_gu = tn(hid_all, d_gu).astype(BF)
+            grad_down = tn(after(cot_all, grad_gu), act).astype(BF)
+        grads = after(jnp.concatenate([grad_gu, grad_down], axis=1), *late)
         return grads, lax.psum_scatter(grads, "dp", scatter_dimension=0, tiled=True)
 
     hid = [[hidden_two, swap(hidden_two, "tensor", 1)]]

time: 370 us -> 366 us (0.989)
  matrix products: 63.1 us -> 59.1 us
    dot_general x10, matrix products: 33 us -> 29.1 us  [tn(): lax.dot_general(left, right, (((0,), (0,)), ((), ())), preferred_element_...]
  transfers between devices with their start and end apart: 47 -> 47, of which waited for: 17 -> 16; matrix products, arithmetic and copies ran while one was open for 34% -> 35% of each run, Pallas kernels for 17% -> 17%
where the time goes in v4:
time: 366 us; the launch traced here: 361 us
  waiting for transfers between devices  87.6 us (24%)
  Pallas kernels  61.1 us (17%)
  matrix products  59.1 us (16%)
  local copies, waits for them, and re-layouts  52.7 us (14%)
  starting transfers between devices  46.5 us (13%)
  other arithmetic  37 us (10%)
  between operations  17.1 us (5%)
    pallas_call x4, Pallas kernels, ffn(): pl.pallas_call(kernel, grid=(steps,), in_specs=[near, far] * 2 + [pl.Bloc...  61.1 us
    ppermute x8, waiting for transfers between devices, ring(): lax.ppermute(value, axis, [(i, (i + by) % peers) for i in range(peers)])  44.8 us
    ppermute x32, waiting for transfers between devices, swap(): return lax.ppermute(value, axis, [(i, i ^ bit) for i in range(peers)])  42.7 us
    ppermute x32, starting transfers between devices, swap(): return lax.ppermute(value, axis, [(i, i ^ bit) for i in range(peers)])  31.9 us
    dot_general x10, matrix products, tn(): lax.dot_general(left, right, (((0,), (0,)), ((), ())), preferred_element_...  29.1 us
    unnamed x203, local copies, waits for them, and re-layouts  28.6 us
    dot_general x14, matrix products, nn(): return jnp.dot(left, right, preferred_element_type=F32)  21.5 us
    ppermute x8, starting transfers between devices, ring(): lax.ppermute(value, axis, [(i, (i + by) % peers) for i in range(peers)])  11 us
  transfers between devices with their start and end apart: 47, of which 16 were waited for; matrix products, arithmetic and copies ran while one was open for 35% of the time, Pallas kernels for 17%

profile of v4, /device:TPU:0, one launch (start us, length us, event | category | flops | bytes accessed | tf_op | source)
XLA Modules:
  0.0 361.1 jit_solution(9065788895047171461)
XLA Ops:
  11.7 3.0 collective-permute-start.1
  22.2 3.6 %collective-permute-start.14 = (bf16[256,1024]{1,0:T(8,128)(2,1)}, bf16[256,1024]{1,0:T(8,128)(2,1)}, u32[]{:S(2)}, u32[]{:S(2)}) collective-permute-start(bf16[256,1024]{1,0:T(8,128)(2,1)} %get-tuple-element.91), channel_id=1, source_target_pairs={{0,2},{1,3},{2,0},{3,1},{4,6},{5,7},{6,4},{7,5},{8,10},{9,11},{10,... | collective-permute-start | bytes 1572872 | tf_op jit(solution)/shard_map/ppermute | solution.py:17
  26.7 1.9 collective-permute-start.5
  28.7 2.4 collective-permute-start.2
  31.4 2.4 fusion.24
  37.2 7.4 %collective-permute-done.2 = bf16[128,1024]{1,0:T(8,128)(2,1)} collective-permute-done((bf16[128,1024]{1,0:T(8,128)(2,1)S(1)}, bf16[128,1024]{1,0:T(8,128)(2,1)}, u32[]{:S(2)}, u32[]{:S(2)}) %collective-permute-start.2) | collective-permute-done | bytes 262176 | tf_op jit(solution)/shard_map/ppermute | solution.py:22
  47.1 1.9 constant_dynamic-update-slice_fusion.5
  49.0 7.2 %collective-permute-done.3 = bf16[128,1024]{1,0:T(8,128)(2,1)S(1)} collective-permute-done((bf16[128,1024]{1,0:T(8,128)(2,1)}, bf16[128,1024]{1,0:T(8,128)(2,1)S(1)}, u32[]{:S(2)}, u32[]{:S(2)}) %collective-permute-start.3) | collective-permute-done | bytes 262176 | tf_op jit(solution)/shard_map/ppermute | solution.py:22
  56.8 2.6 concatenate.225
  60.6 3.0 collective-permute-start.11
  68.1 7.5 %collective-permute-done.7 = bf16[128,1024]{1,0:T(8,128)(2,1)S(1)} collective-permute-done((bf16[128,1024]{1,0:T(8,128)(2,1)S(1)}, bf16[128,1024]{1,0:T(8,128)(2,1)S(1)}, u32[]{:S(2)}, u32[]{:S(2)}) %collective-permute-start.7) | collective-permute-done | bytes 262176 | tf_op jit(solution)/shard_map/ppermute | solution.py:17
  77.1 2.2 collective-permute-start.12
  79.3 2.4 fusion.40
  85.6 4.4 %collective-permute-done.12 = bf16[272,1024]{1,0:T(8,128)(2,1)S(1)} collective-permute-done((bf16[272,1024]{1,0:T(8,128)(2,1)S(1)}, bf16[272,1024]{1,0:T(8,128)(2,1)S(1)}, u32[]{:S(2)}, u32[]{:S(2)}) %collective-permute-start.12) | collective-permute-done | bytes 557088 | tf_op jit(solution)/shard_map/ppermute | solution.py:17
  102.1 1.6 multiply_reduce_fusion.2
  105.7 1.7 collective-permute-start.16
  111.9 13.4 %shard_map.169 = (f32[512,1024]{1,0:T(8,128)}, f32[512,1024]{1,0:T(8,128)}, f32[512,1024]{1,0:T(8,128)}, f32[512,1024]{1,0:T(8,128)}, bf16[2048,1024]{1,0:T(8,12...) custom-call(bf16[512,1024]{1,0:T(8,128)(2,1)S(1)} %multiply_convert_fusion.refs_0_, ...), custom_call_target="tpu_custom_call" | custom-call | flops 6442450944 | bytes 15728640 | tf_op jit(solution)/shard_map/pallas_call | solution.py:156
  125.4 6.0 %collective-permute-done.16.refs_0_ = bf16[512,1024]{1,0:T(8,128)(2,1)} collective-permute-done((bf16[512,1024]{1,0:T(8,128)(2,1)S(1)}, bf16[512,1024]{1,0:T(8,128)(2,1)}, u32[]{:S(2)}, u32[]{:S(2)}) %collective-permute-start.16) | collective-permute-done | bytes 1048608 | tf_op jit(solution)/shard_map/ppermute | solution.py:17
  131.9 3.8 %collective-permute-done.19.refs_1_ = bf16[512,1024]{1,0:T(8,128)(2,1)S(1)} collective-permute-done((bf16[512,1024]{1,0:T(8,128)(2,1)}, bf16[512,1024]{1,0:T(8,128)(2,1)S(1)}, u32[]{:S(2)}, u32[]{:S(2)}) %collective-permute-start.19) | collective-permute-done | bytes 1048608 | tf_op jit(solution)/shard_map/ppermute | solution.py:17
  135.7 14.2 %shard_map.170 = (f32[512,1024]{1,0:T(8,128)}, f32[512,1024]{1,0:T(8,128)}, f32[512,1024]{1,0:T(8,128)}, f32[512,1024]{1,0:T(8,128)}, bf16[2048,1024]{1,0:T(8,12...) custom-call(bf16[512,1024]{1,0:T(8,128)(2,1)} %collective-permute-do, ...), custom_call_target="tpu_custom_call", output_to_operand_aliasing={{4}: (5, {}), {5}: (6, {}), {6}: (7, {}), {7}: (8, {})} | custom-call | flops 6442450944 | bytes 15728640 | tf_op jit(solution)/shard_map/pallas_call | solution.py:156
  149.9 5.4 %convolution_convert_fusion.8 = bf16[1024,512]{0,1:T(8,128)(2,1)S(1)} fusion(bf16[2048,1024]{1,0:T(8,128)(2,1)} %get-tuple-element.132, bf16[2048,512]{1,0:T(8,128)(2,1)} %get-tuple-element.106), kind=kOutput, calls=%fused_computation.69 | convolution fusion | flops 2148007936 | bytes 7340032 | tf_op jit(solution)/shard_map/dot_general | solution.py:42
  155.3 4.8 %convolution_convert_fusion.2 = bf16[1024,1024]{0,1:T(8,128)(2,1)S(1)} fusion(bf16[2048,1024]{1,0:T(8,128)(2,1)S(1)} %copy-done.91, bf16[2048,1024]{1,0:T(8,128)(2,1)S(1)} %copy-done.90), kind=kOutput, calls=%fused_computation.60 | convolution fusion | flops 4296015872 | bytes 10485760 | tf_op jit(solution)/shard_map/dot_general | solution.py:42
  160.5 3.0 copy.71
  163.5 17.1 %shard_map.171 = (bf16[512,1024]{1,0:T(8,128)(2,1)S(1)}, bf16[512,1024]{1,0:T(8,128)(2,1)S(1)}, bf16[512,1024]{1,0:T(8,128)(2,1)}, bf16[512,1024]{1,0:T(8,128)(2...) custom-call(bf16[512,1024]{1,0:T(8,128)(2,1)} %collective-permute-done.16.refs_0_, ...), custom_call_target="tpu_custom_call" | custom-call | flops 8053063680 | bytes 16515072 | tf_op jit(solution)/shard_map/pallas_call | solution.py:156
  181.5 2.3 slice.652
  185.6 1.6 collective-permute-start.25
  187.2 16.4 %shard_map.172 = (bf16[512,1024]{1,0:T(8,128)(2,1)S(1)}, bf16[512,1024]{1,0:T(8,128)(2,1)S(1)}, bf16[512,1024]{1,0:T(8,128)(2,1)}, bf16[512,1024]{1,0:T(8,128)(2...) custom-call(bf16[512,1024]{1,0:T(8,128)(2,1)S(1)} %copy-done.3, ...), custom_call_target="tpu_custom_call", output_to_operand_aliasing={{4}: (9, {}), {5}: (10, {})} | custom-call | flops 8053063680 | bytes 16515072 | tf_op jit(solution)/shard_map/pallas_call | solution.py:156
  203.7 9.7 %convolution_convert_fusion = bf16[1024,1280]{1,0:T(8,128)(2,1)S(1)} fusion(bf16[2048,1024]{1,0:T(8,128)(2,1)} %get-tuple-element.107, bf16[2048,1280]{1,0:T(8,128)(2,1)} %get-tuple-element.131), kind=kOutput, calls=%fused_computation.11 | convolution fusion | flops 5370019840 | bytes 12058624 | tf_op jit(solution)/shard_map/dot_general | solution.py:42
  213.4 3.5 convolution_convert_fusion.3
  216.9 2.2 pad_maximum_fusion
  219.2 2.3 convert_add_fusion.3
  223.5 1.7 fusion.26
  228.9 2.1 multiply_reduce_fusion.5
  256.0 2.5 fusion.189
  260.1 3.3 fusion.17
  265.8 2.8 add_convert_fusion.2
  268.6 3.5 collective-permute-done.34
  272.7 6.0 %collective-permute-done.35 = f32[5,1024]{1,0:T(8,128)S(1)} collective-permute-done((f32[5,1024]{1,0:T(8,128)S(1)}, f32[5,1024]{1,0:T(8,128)S(1)}, u32[]{:S(2)}, u32[]{:S(2)}) %collective-permute-start.35) | collective-permute-done | bytes 20512 | tf_op jit(solution)/shard_map/ppermute | solution.py:22
  285.4 1.9 slice_add_fusion
  288.4 7.7 %collective-permute-done.31 = bf16[512,512]{0,1:T(8,128)(2,1)S(1)} collective-permute-done((bf16[512,512]{0,1:T(8,128)(2,1)S(1)}, bf16[512,512]{0,1:T(8,128)(2,1)S(1)}, u32[]{:S(2)}, u32[]{:S(2)}) %collective-permute-start.31) | collective-permute-done | bytes 524320 | tf_op jit(solution)/shard_map/ppermute | solution.py:17
  297.4 1.8 collective-permute-start.32
  300.5 5.3 %collective-permute-done.39 = bf16[512,512]{0,1:T(8,128)(2,1)S(1)} collective-permute-done((bf16[512,512]{0,1:T(8,128)(2,1)S(1)}, bf16[512,512]{0,1:T(8,128)(2,1)S(1)}, u32[]{:S(2)}, u32[]{:S(2)}) %collective-permute-start.39) | collective-permute-done | bytes 524320 | tf_op jit(solution)/shard_map/ppermute | solution.py:17
  307.1 2.9 collective-permute-start.40
  311.5 1.9 slice.700
  313.4 2.3 reshape.754
  315.8 5.4 %collective-permute-done.32 = bf16[512,1024]{1,0:T(8,128)(2,1)} collective-permute-done((bf16[512,1024]{1,0:T(8,128)(2,1)}, bf16[512,1024]{1,0:T(8,128)(2,1)}, u32[]{:S(2)}, u32[]{:S(2)}) %collective-permute-start.32) | collective-permute-done | bytes 1048608 | tf_op jit(solution)/shard_map/ppermute | solution.py:17
  321.1 5.4 %fusion.16 = (f32[512,1024]{1,0:T(8,128)}, bf16[512,1024]{1,0:T(8,128)(2,1)}) fusion(bf16[512,1024]{1,0:T(8,128)(2,1)S(1)} %copy-done.43, f32[512,1024]{1,0:T(8,128)} %get-tuple-element.303, f32[512]{0:T(512)} %broadcast_multiply_fusion, f32[1024]{0:T(1024)S(1)} %convert_element_type.220, f32[512]{0:T(512)S(1)} %copy-done.82, f32[512]{0:T(512)} %copy-done.83, ...), kind=kLoop, calls=%fused_computation.30 | loop fusion | flops 11010048 | bytes 14696448 | tf_op jit(solution)/shard_map/add | solution.py:398
  326.5 20.7 %collective-permute-done.41 = bf16[128,1024]{0,1:T(8,128)(2,1)} collective-permute-done((bf16[128,1024]{0,1:T(8,128)(2,1)}, bf16[128,1024]{0,1:T(8,128)(2,1)}, u32[]{:S(2)}, u32[]{:S(2)}) %collective-permute-start.41) | collective-permute-done | bytes 262176 | tf_op jit(solution)/shard_map/ppermute | solution.py:22
  (402 shorter events, 106.0 us)
Async XLA Ops:
  7.2 102.3 %all-gather.3.cloned.1.call-start = ((), (), s32[]{:S(2)}) async-start(), calls=%async_computation.2 | async-start | bytes 3538944 | tf_op jit(solution)/shard_map/all_gather | solution.py:220
  10.6 149.8 %all-gather.5.cloned.1.call-start = ((), (), s32[]{:S(2)}) async-start(), calls=%async_computation.3 | async-start | bytes 4423680 | tf_op jit(solution)/shard_map/all_gather | solution.py:220
  11.7 14.1 %collective-permute-start.1 = (bf16[128,1024]{1,0:T(8,128)(2,1)S(1)}, bf16[128,1024]{1,0:T(8,128)(2,1)S(1)}, u32[]{:S(2)}, u32[]{:S(2)}) collective-permute-start(bf16[128,1024]{1,0:T(8,128)(2,1)S(1)} %get-tuple-element.251), channel_id=1, source_target_pairs={{0,8},{4,12},{8,16},{12,20},{16,24},{20,28},{24,0},{28,4},{1,9},{5... | collective-permute-start | bytes 786440 | tf_op jit(solution)/shard_map/ppermute | solution.py:22
  14.7 11.1 %collective-permute-start.4 = (bf16[128,1024]{1,0:T(8,128)(2,1)S(1)}, bf16[128,1024]{1,0:T(8,128)(2,1)S(1)}, u32[]{:S(2)}, u32[]{:S(2)}) collective-permute-start(bf16[128,1024]{1,0:T(8,128)(2,1)S(1)} %get-tuple-element.251), channel_id=1, source_target_pairs={{0,4},{4,0},{8,12},{12,8},{16,20},{20,16},{24,28},{28,24},{1,5},{5... | collective-permute-start | bytes 786440 | tf_op jit(solution)/shard_map/ppermute | solution.py:17
  19.0 3.1 collective-permute-start
  22.2 82.0 %collective-permute-start.14 = (bf16[256,1024]{1,0:T(8,128)(2,1)}, bf16[256,1024]{1,0:T(8,128)(2,1)}, u32[]{:S(2)}, u32[]{:S(2)}) collective-permute-start(bf16[256,1024]{1,0:T(8,128)(2,1)} %get-tuple-element.91), channel_id=1, source_target_pairs={{0,2},{1,3},{2,0},{3,1},{4,6},{5,7},{6,4},{7,5},{8,10},{9,11},{10,... | collective-permute-start | bytes 1572872 | tf_op jit(solution)/shard_map/ppermute | solution.py:17
  26.7 40.4 %collective-permute-start.9 = (bf16[256,1024]{1,0:T(8,128)(2,1)}, bf16[256,1024]{1,0:T(8,128)(2,1)}, u32[]{:S(2)}, u32[]{:S(2)}) collective-permute-start(bf16[256,1024]{1,0:T(8,128)(2,1)} %pad_maximum_fusion.16), channel_id=1, source_target_pairs={{0,2},{1,3},{2,0},{3,1},{4,6},{5,7},{6,4},{7,5},{8,10},{9,11},{10,... | collective-permute-start | bytes 1572872 | tf_op jit(solution)/shard_map/ppermute | solution.py:17
  26.7 8.4 %collective-permute-start.5 = (bf16[128,1024]{1,0:T(8,128)(2,1)S(1)}, bf16[128,1024]{1,0:T(8,128)(2,1)S(1)}, u32[]{:S(2)}, u32[]{:S(2)}) collective-permute-start(bf16[128,1024]{1,0:T(8,128)(2,1)S(1)} %collective-permute-done.1), channel_id=1, source_target_pairs={{0,4},{4,0},{8,12},{12,8},{16,20},{20,16},{24,28},{28,24},{1,5},{5... | collective-permute-start | bytes 786440 | tf_op jit(solution)/shard_map/ppermute | solution.py:17
  28.7 15.9 %collective-permute-start.2 = (bf16[128,1024]{1,0:T(8,128)(2,1)S(1)}, bf16[128,1024]{1,0:T(8,128)(2,1)}, u32[]{:S(2)}, u32[]{:S(2)}) collective-permute-start(bf16[128,1024]{1,0:T(8,128)(2,1)S(1)} %collective-permute-done.1), channel_id=1, source_target_pairs={{0,8},{4,12},{8,16},{12,20},{16,24},{20,28},{24,0},{28,4},{1,9},{5... | collective-permute-start | bytes 786440 | tf_op jit(solution)/shard_map/ppermute | solution.py:22
  36.0 45.8 %collective-permute-start.10 = (bf16[256,1024]{1,0:T(8,128)(2,1)}, bf16[256,1024]{1,0:T(8,128)(2,1)}, u32[]{:S(2)}, u32[]{:S(2)}) collective-permute-start(bf16[256,1024]{1,0:T(8,128)(2,1)} %pad_maximum_fusion.17), channel_id=1, source_target_pairs={{0,2},{1,3},{2,0},{3,1},{4,6},{5,7},{6,4},{7,5},{8,10},{9,11},{10,... | collective-permute-start | bytes 1572872 | tf_op jit(solution)/shard_map/ppermute | solution.py:17
  44.9 11.3 %collective-permute-start.3 = (bf16[128,1024]{1,0:T(8,128)(2,1)}, bf16[128,1024]{1,0:T(8,128)(2,1)S(1)}, u32[]{:S(2)}, u32[]{:S(2)}) collective-permute-start(bf16[128,1024]{1,0:T(8,128)(2,1)} %collective-permute-done.2), channel_id=1, source_target_pairs={{0,8},{4,12},{8,16},{12,20},{16,24},{20,28},{24,0},{28,4},{1,9},{5... | collective-permute-start | bytes 786440 | tf_op jit(solution)/shard_map/ppermute | solution.py:22
  45.9 265.6 %reduce-scatter.7.cloned.1.call-start = ((), (), s32[]{:S(2)}) async-start(), calls=%async_computation.5 | async-start | bytes 3538944 | tf_op jit(solution)/shard_map/reduce_scatter | solution.py:294
  46.1 20.2 %collective-permute-start.6 = (bf16[128,1024]{1,0:T(8,128)(2,1)}, bf16[128,1024]{1,0:T(8,128)(2,1)S(1)}, u32[]{:S(2)}, u32[]{:S(2)}) collective-permute-start(bf16[128,1024]{1,0:T(8,128)(2,1)} %collective-permute-done.2), channel_id=1, source_target_pairs={{0,4},{4,0},{8,12},{12,8},{16,20},{20,16},{24,28},{28,24},{1,5},{5... | collective-permute-start | bytes 786440 | tf_op jit(solution)/shard_map/ppermute | solution.py:17
  60.6 22.8 %collective-permute-start.11 = (bf16[256,1024]{1,0:T(8,128)(2,1)S(1)}, bf16[256,1024]{1,0:T(8,128)(2,1)S(1)}, u32[]{:S(2)}, u32[]{:S(2)}) collective-permute-start(bf16[256,1024]{1,0:T(8,128)(2,1)S(1)} %pad_maximum_fusion.18), channel_id=1, source_target_pairs={{0,2},{1,3},{2,0},{3,1},{4,6},{5,7},{6,4},{7,5},{8,10},{9,11},{10,... | collective-permute-start | bytes 1572872 | tf_op jit(solution)/shard_map/ppermute | solution.py:17
  66.3 9.3 %collective-permute-start.7 = (bf16[128,1024]{1,0:T(8,128)(2,1)S(1)}, bf16[128,1024]{1,0:T(8,128)(2,1)S(1)}, u32[]{:S(2)}, u32[]{:S(2)}) collective-permute-start(bf16[128,1024]{1,0:T(8,128)(2,1)S(1)} %collective-permute-done.3), channel_id=1, source_target_pairs={{0,4},{4,0},{8,12},{12,8},{16,20},{20,16},{24,28},{28,24},{1,5},{5... | collective-permute-start | bytes 786440 | tf_op jit(solution)/shard_map/ppermute | solution.py:17
  77.1 12.9 %collective-permute-start.12 = (bf16[272,1024]{1,0:T(8,128)(2,1)S(1)}, bf16[272,1024]{1,0:T(8,128)(2,1)S(1)}, u32[]{:S(2)}, u32[]{:S(2)}) collective-permute-start(bf16[272,1024]{1,0:T(8,128)(2,1)S(1)} %pad_maximum_fusion.11), channel_id=1, source_target_pairs={{0,2},{1,3},{2,0},{3,1},{4,6},{5,7},{6,4},{7,5},{8,10},{9,11},{10,... | collective-permute-start | bytes 1671176 | tf_op jit(solution)/shard_map/ppermute | solution.py:17
  79.3 12.4 %collective-permute-start.8 = (bf16[1040,1024]{1,0:T(8,128)(2,1)}, bf16[1040,1024]{1,0:T(8,128)(2,1)S(1)}, u32[]{:S(2)}, u32[]{:S(2)}) collective-permute-start(bf16[1040,1024]{1,0:T(8,128)(2,1)} %get-tuple-element.295), channel_id=1, source_target_pairs={{0,1},{1,0},{2,3},{3,2},{4,5},{5,4},{6,7},{7,6},{8,9},{9,8},{10,11... | collective-permute-start | bytes 6389768 | tf_op jit(solution)/shard_map/ppermute | solution.py:17
  81.7 25.7 %collective-permute-start.18 = (bf16[512,1024]{1,0:T(8,128)(2,1)S(1)}, bf16[512,1024]{1,0:T(8,128)(2,1)S(1)}, u32[]{:S(2)}, u32[]{:S(2)}) collective-permute-start(bf16[512,1024]{1,0:T(8,128)(2,1)S(1)} %copy-done), channel_id=1, source_target_pairs={{0,1},{1,0},{2,3},{3,2},{4,5},{5,4},{6,7},{7,6},{8,9},{9,8},{10,11... | collective-permute-start | bytes 3145736 | tf_op jit(solution)/shard_map/ppermute | solution.py:17
  90.0 5.1 %collective-permute-start.13 = (bf16[1040,1024]{1,0:T(8,128)(2,1)S(1)}, bf16[1040,1024]{1,0:T(8,128)(2,1)S(1)}, u32[]{:S(2)}, u32[]{:S(2)}) collective-permute-start(bf16[1040,1024]{1,0:T(8,128)(2,1)S(1)} %constant_dynamic-update-slice_fusion.17), channel_id=1, source_target_pairs={{0,1},{1,0},{2,3},{3,2},{4,5},{5,4},{6,7},{7,6},{8,9},{9,8},{10,11... | collective-permute-start | bytes 6389768 | tf_op jit(solution)/shard_map/ppermute | solution.py:17
  90.1 15.6 %collective-permute-start.15 = (bf16[256,1024]{1,0:T(8,128)(2,1)S(1)}, bf16[256,1024]{1,0:T(8,128)(2,1)S(1)}, u32[]{:S(2)}, u32[]{:S(2)}) collective-permute-start(bf16[256,1024]{1,0:T(8,128)(2,1)S(1)} %copy-done.62), channel_id=1, source_target_pairs={{0,2},{1,3},{2,0},{3,1},{4,6},{5,7},{6,4},{7,5},{8,10},{9,11},{10,... | collective-permute-start | bytes 1572872 | tf_op jit(solution)/shard_map/ppermute | solution.py:17
  104.0 4.4 %collective-permute-start.17 = (bf16[512,1024]{1,0:T(8,128)(2,1)S(1)}, bf16[512,1024]{1,0:T(8,128)(2,1)S(1)}, u32[]{:S(2)}, u32[]{:S(2)}) collective-permute-start(bf16[512,1024]{1,0:T(8,128)(2,1)S(1)} %multiply_convert_fusion.refs_0_), channel_id=1, source_target_pairs={{0,1},{1,0},{2,3},{3,2},{4,5},{5,4},{6,7},{7,6},{8,9},{9,8},{10,11... | collective-permute-start | bytes 3145736 | tf_op jit(solution)/shard_map/ppermute | solution.py:17
  105.7 30.0 %copy-start.4 = (bf16[512,1024]{1,0:T(8,128)(2,1)}, bf16[512,1024]{1,0:T(8,128)(2,1)S(1)}, u32[]{:S(2)}) copy-start(bf16[512,1024]{1,0:T(8,128)(2,1)S(1)} %constant_dynamic-update-slice_fusion.19.refs_2_) | copy-start | bytes 3145732
  105.7 25.6 %collective-permute-start.16 = (bf16[512,1024]{1,0:T(8,128)(2,1)S(1)}, bf16[512,1024]{1,0:T(8,128)(2,1)}, u32[]{:S(2)}, u32[]{:S(2)}) collective-permute-start(bf16[512,1024]{1,0:T(8,128)(2,1)S(1)} %multiply_convert_fusion.refs_0_), channel_id=1, source_target_pairs={{0,2},{1,3},{2,0},{3,1},{4,6},{5,7},{6,4},{7,5},{8,10},{9,11},{10,... | collective-permute-start | bytes 3145736 | tf_op jit(solution)/shard_map/ppermute | solution.py:17
  131.3 4.3 %collective-permute-start.19 = (bf16[512,1024]{1,0:T(8,128)(2,1)}, bf16[512,1024]{1,0:T(8,128)(2,1)S(1)}, u32[]{:S(2)}, u32[]{:S(2)}) collective-permute-start(bf16[512,1024]{1,0:T(8,128)(2,1)} %collective-permute-done.16.refs_0_), channel_id=1, source_target_pairs={{0,1},{1,0},{2,3},{3,2},{4,5},{5,4},{6,7},{7,6},{8,9},{9,8},{10,11... | collective-permute-start | bytes 3145736 | tf_op jit(solution)/shard_map/ppermute | solution.py:17
  131.4 4.3 %collective-permute-start.20 = (bf16[512,1024]{1,0:T(8,128)(2,1)S(1)}, bf16[512,1024]{1,0:T(8,128)(2,1)S(1)}, u32[]{:S(2)}, u32[]{:S(2)}) collective-permute-start(bf16[512,1024]{1,0:T(8,128)(2,1)S(1)} %constant_dynamic-update-slice_fusion.19.refs_2_), channel_id=1, source_target_pairs={{0,1},{1,0},{2,3},{3,2},{4,5},{5,4},{6,7},{7,6},{8,9},{9,8},{10,11... | collective-permute-start | bytes 3145736 | tf_op jit(solution)/shard_map/ppermute | solution.py:17
  163.5 186.7 %reduce-scatter.5.cloned.1.call-start = ((), (), s32[]{:S(2)}) async-start(), calls=%async_computation.4 | async-start | bytes 4423680 | tf_op jit(solution)/shard_map/reduce_scatter | solution.py:294
  180.6 3.6 collective-permute-start.21
  183.8 82.0 %collective-permute-start.23 = (bf16[512,1024]{1,0:T(8,128)(2,1)}, bf16[512,1024]{1,0:T(8,128)(2,1)}, u32[]{:S(2)}, u32[]{:S(2)}) collective-permute-start(bf16[512,1024]{1,0:T(8,128)(2,1)} %get-tuple-element.127), channel_id=1, source_target_pairs={{0,1},{1,0},{2,3},{3,2},{4,5},{5,4},{6,7},{7,6},{8,9},{9,8},{10,11... | collective-permute-start | bytes 3145736 | tf_op jit(solution)/shard_map/ppermute | solution.py:17
  185.6 33.6 %collective-permute-start.25 = (bf16[512,1024]{1,0:T(8,128)(2,1)}, bf16[512,1024]{1,0:T(8,128)(2,1)}, u32[]{:S(2)}, u32[]{:S(2)}) collective-permute-start(bf16[512,1024]{1,0:T(8,128)(2,1)} %add_convert_fusion.1), channel_id=1, source_target_pairs={{0,2},{1,3},{2,0},{3,1},{4,6},{5,7},{6,4},{7,5},{8,10},{9,11},{10,... | collective-permute-start | bytes 3145736 | tf_op jit(solution)/shard_map/ppermute | solution.py:17
  203.6 15.6 %collective-permute-start.24 = (bf16[512,1024]{1,0:T(8,128)(2,1)}, bf16[512,1024]{1,0:T(8,128)(2,1)}, u32[]{:S(2)}, u32[]{:S(2)}) collective-permute-start(bf16[512,1024]{1,0:T(8,128)(2,1)} %get-tuple-element.129), channel_id=1, source_target_pairs={{0,1},{1,0},{2,3},{3,2},{4,5},{5,4},{6,7},{7,6},{8,9},{9,8},{10,11... | collective-permute-start | bytes 3145736 | tf_op jit(solution)/shard_map/ppermute | solution.py:17
  234.1 4.5 %collective-permute-start.28 = (f32[4,2,256]{2,1,0:T(2,128)S(1)}, f32[4,2,256]{2,1,0:T(2,128)S(1)}, u32[]{:S(2)}, u32[]{:S(2)}) collective-permute-start(f32[4,2,256]{2,1,0:T(2,128)S(1)} %pad_maximum_fusion.24), channel_id=1, source_target_pairs={{1,0},{2,1},{3,2},{4,3},{5,4},{6,5},{7,6},{8,7},{9,8},{10,9},{11,1... | collective-permute-start | bytes 24584 | tf_op jit(solution)/shard_map/ppermute | solution.py:28
  236.5 6.4 %collective-permute-start.26 = (bf16[1024,1024]{0,1:T(8,128)(2,1)S(1)}, bf16[1024,1024]{0,1:T(8,128)(2,1)S(1)}, u32[]{:S(2)}, u32[]{:S(2)}) collective-permute-start(bf16[1024,1024]{0,1:T(8,128)(2,1)S(1)} %pad_maximum_fusion.4), channel_id=1, source_target_pairs={{0,1},{1,0},{2,3},{3,2},{4,5},{5,4},{6,7},{7,6},{8,9},{9,8},{10,11... | collective-permute-start | bytes 6291464 | tf_op jit(solution)/shard_map/ppermute | solution.py:17
  241.4 7.5 %collective-permute-start.29 = (bf16[1024,1024]{0,1:T(8,128)(2,1)S(1)}, bf16[1024,1024]{0,1:T(8,128)(2,1)S(1)}, u32[]{:S(2)}, u32[]{:S(2)}) collective-permute-start(bf16[1024,1024]{0,1:T(8,128)(2,1)S(1)} %convolution_convert_fusion.1), channel_id=1, source_target_pairs={{0,1},{1,0},{2,3},{3,2},{4,5},{5,4},{6,7},{7,6},{8,9},{9,8},{10,11... | collective-permute-start | bytes 6291464 | tf_op jit(solution)/shard_map/ppermute | solution.py:17
  247.7 33.8 %collective-permute-start.27 = (bf16[1024,512]{0,1:T(8,128)(2,1)}, bf16[1024,512]{0,1:T(8,128)(2,1)}, u32[]{:S(2)}, u32[]{:S(2)}) collective-permute-start(bf16[1024,512]{0,1:T(8,128)(2,1)} %pad_maximum_fusion.9), channel_id=1, source_target_pairs={{0,4},{4,0},{8,12},{12,8},{16,20},{20,16},{24,28},{28,24},{1,5},{5... | collective-permute-start | bytes 3145736 | tf_op jit(solution)/shard_map/ppermute | solution.py:17
  251.5 30.7 %collective-permute-start.30 = (bf16[1024,512]{0,1:T(8,128)(2,1)}, bf16[1024,512]{0,1:T(8,128)(2,1)}, u32[]{:S(2)}, u32[]{:S(2)}) collective-permute-start(bf16[1024,512]{0,1:T(8,128)(2,1)} %slice.1027), channel_id=1, source_target_pairs={{0,2},{1,3},{2,0},{3,1},{4,6},{5,7},{6,4},{7,5},{8,10},{9,11},{10,... | collective-permute-start | bytes 3145736 | tf_op jit(solution)/shard_map/ppermute | solution.py:17
  263.4 1.3 collective-permute-start.33
  263.5 52.2 %collective-permute-start.22 = (bf16[512,1024]{1,0:T(8,128)(2,1)}, bf16[512,1024]{1,0:T(8,128)(2,1)}, u32[]{:S(2)}, u32[]{:S(2)}) collective-permute-start(bf16[512,1024]{1,0:T(8,128)(2,1)} %copy-done.5), channel_id=1, source_target_pairs={{0,1},{1,0},{2,3},{3,2},{4,5},{5,4},{6,7},{7,6},{8,9},{9,8},{10,11... | collective-permute-start | bytes 3145736 | tf_op jit(solution)/shard_map/ppermute | solution.py:17
  264.7 7.4 %collective-permute-start.34 = (f32[5,1024]{1,0:T(8,128)S(1)}, f32[5,1024]{1,0:T(8,128)S(1)}, u32[]{:S(2)}, u32[]{:S(2)}) collective-permute-start(f32[5,1024]{1,0:T(8,128)S(1)} %fusion.169), channel_id=1, source_target_pairs={{0,16},{4,20},{8,24},{12,28},{16,0},{20,4},{24,8},{28,12},{1,17},{... | collective-permute-start | bytes 61448 | tf_op jit(solution)/shard_map/ppermute | solution.py:22
  272.1 6.6 %collective-permute-start.35 = (f32[5,1024]{1,0:T(8,128)S(1)}, f32[5,1024]{1,0:T(8,128)S(1)}, u32[]{:S(2)}, u32[]{:S(2)}) collective-permute-start(f32[5,1024]{1,0:T(8,128)S(1)} %add.307), channel_id=1, source_target_pairs={{0,8},{4,12},{8,16},{12,20},{16,24},{20,28},{24,0},{28,4},{1,9},{5... | collective-permute-start | bytes 61448 | tf_op jit(solution)/shard_map/ppermute | solution.py:22
  278.7 6.1 %collective-permute-start.38 = (f32[5,1024]{1,0:T(8,128)S(1)}, f32[5,1024]{1,0:T(8,128)S(1)}, u32[]{:S(2)}, u32[]{:S(2)}) collective-permute-start(f32[5,1024]{1,0:T(8,128)S(1)} %add.308), channel_id=1, source_target_pairs={{0,6},{1,7},{2,4},{3,5},{4,2},{5,3},{6,0},{7,1},{8,14},{9,15},{10,... | collective-permute-start | bytes 61448 | tf_op jit(solution)/shard_map/ppermute | solution.py:34
  279.1 5.7 %collective-permute-start.37 = (f32[5,1024]{1,0:T(8,128)S(1)}, f32[5,1024]{1,0:T(8,128)S(1)}, u32[]{:S(2)}, u32[]{:S(2)}) collective-permute-start(f32[5,1024]{1,0:T(8,128)S(1)} %add.308), channel_id=1, source_target_pairs={{0,2},{1,3},{2,0},{3,1},{4,6},{5,7},{6,4},{7,5},{8,10},{9,11},{10,... | collective-permute-start | bytes 61448 | tf_op jit(solution)/shard_map/ppermute | solution.py:17
  281.5 3.9 %collective-permute-start.36 = (f32[5,1024]{1,0:T(8,128)S(1)}, f32[5,1024]{1,0:T(8,128)S(1)}, u32[]{:S(2)}, u32[]{:S(2)}) collective-permute-start(f32[5,1024]{1,0:T(8,128)S(1)} %add.308), channel_id=1, source_target_pairs={{0,4},{4,0},{8,12},{12,8},{16,20},{20,16},{24,28},{28,24},{1,5},{5... | collective-permute-start | bytes 61448 | tf_op jit(solution)/shard_map/ppermute | solution.py:17
  283.5 12.7 %collective-permute-start.31 = (bf16[512,512]{0,1:T(8,128)(2,1)S(1)}, bf16[512,512]{0,1:T(8,128)(2,1)S(1)}, u32[]{:S(2)}, u32[]{:S(2)}) collective-permute-start(bf16[512,512]{0,1:T(8,128)(2,1)S(1)} %fusion.51), channel_id=1, source_target_pairs={{0,2},{1,3},{2,0},{3,1},{4,6},{5,7},{6,4},{7,5},{8,10},{9,11},{10,... | collective-permute-start | bytes 1572872 | tf_op jit(solution)/shard_map/ppermute | solution.py:17
  287.4 18.4 %collective-permute-start.39 = (bf16[512,512]{0,1:T(8,128)(2,1)S(1)}, bf16[512,512]{0,1:T(8,128)(2,1)S(1)}, u32[]{:S(2)}, u32[]{:S(2)}) collective-permute-start(bf16[512,512]{0,1:T(8,128)(2,1)S(1)} %slice.1028), channel_id=1, source_target_pairs={{0,4},{4,0},{8,12},{12,8},{16,20},{20,16},{24,28},{28,24},{1,5},{5... | collective-permute-start | bytes 1572872 | tf_op jit(solution)/shard_map/ppermute | solution.py:17
  297.4 23.7 %collective-permute-start.32 = (bf16[512,1024]{1,0:T(8,128)(2,1)}, bf16[512,1024]{1,0:T(8,128)(2,1)}, u32[]{:S(2)}, u32[]{:S(2)}) collective-permute-start(bf16[512,1024]{1,0:T(8,128)(2,1)} %add_convert_fusion.2), channel_id=1, source_target_pairs={{0,2},{1,3},{2,0},{3,1},{4,6},{5,7},{6,4},{7,5},{8,10},{9,11},{10,... | collective-permute-start | bytes 3145736 | tf_op jit(solution)/shard_map/ppermute | solution.py:17
  307.1 19.5 %collective-permute-start.40 = (bf16[128,1024]{0,1:T(8,128)(2,1)}, bf16[128,1024]{0,1:T(8,128)(2,1)}, u32[]{:S(2)}, u32[]{:S(2)}) collective-permute-start(bf16[128,1024]{0,1:T(8,128)(2,1)} %get-tuple-element.220), channel_id=1, source_target_pairs={{0,24},{4,28},{8,0},{12,4},{16,8},{20,12},{24,16},{28,20},{1,25},{... | collective-permute-start | bytes 786440 | tf_op jit(solution)/shard_map/ppermute | solution.py:22
  310.0 37.3 %collective-permute-start.41 = (bf16[128,1024]{0,1:T(8,128)(2,1)}, bf16[128,1024]{0,1:T(8,128)(2,1)}, u32[]{:S(2)}, u32[]{:S(2)}) collective-permute-start(bf16[128,1024]{0,1:T(8,128)(2,1)} %get-tuple-element.219), channel_id=1, source_target_pairs={{0,16},{4,20},{8,24},{12,28},{16,0},{20,4},{24,8},{28,12},{1,17},{... | collective-permute-start | bytes 786440 | tf_op jit(solution)/shard_map/ppermute | solution.py:22
  310.3 37.0 %collective-permute-start.42 = (bf16[128,1024]{0,1:T(8,128)(2,1)}, bf16[128,1024]{0,1:T(8,128)(2,1)}, u32[]{:S(2)}, u32[]{:S(2)}) collective-permute-start(bf16[128,1024]{0,1:T(8,128)(2,1)} %get-tuple-element.218), channel_id=1, source_target_pairs={{0,8},{4,12},{8,16},{12,20},{16,24},{20,28},{24,0},{28,4},{1,9},{5... | collective-permute-start | bytes 786440 | tf_op jit(solution)/shard_map/ppermute | solution.py:22
  (92 other events, 518.8 us)
Sparse Core Ops, SparseCore 0:
  10.8 75.8 all-gather.2
  88.9 70.6 all-gather.4
  163.6 72.5 reduce-scatter.6
  239.8 108.8 reduce-scatter.4
